TPU v7x, 32 devices: a whole 2x2x4 slice. The times are simulated.
32 devices in a mesh: member: 2 (over x), passage: 16 (over z, y, core).
Axes of the slice: x: 2, y: 2, z: 4, core: 2. Of those that a mesh axis runs over, the one named last changes fastest.
Arguments:
- states: bfloat16 [64, 5, 16, 2048], P('member', None, None, 'passage'), parts along dimension 0, may hold values from -6 to 6
- basis: bfloat16 [32, 5, 16, 2048], P(None, None, None, 'passage'), may hold values from -0.015625 to 0.015625
- snapshot_times: int32 [64], P('member'), parts along dimension 0, may hold values from 0 to 4095
- pert_ids: int32 [32], P(('member', 'passage')), parts along dimension 0, may hold values from 0 to 7
- pert_table: float32 [8, 16, 128], replicated, may hold values from 0 to 0.6
- cycle_ids: int32 [16, 2048], P(None, 'passage'), may hold values from 0 to 5
- groove_kernel: float32 [16], replicated, may hold values from -4 to 4
- groove_gain: float32 [5], replicated, may hold values from 0.5 to 1.5
- speed: float32 [16, 2048], P(None, 'passage'), may hold values from 0.2 to 1
- force_amp: float32 [16, 2048], P(None, 'passage'), may hold values from -6 to 6
- viscosity: float32 [5], replicated, may hold values from 0.02 to 0.2
- coupling: float32 [5, 5], replicated, may hold values from -2.5 to 2.5
Outputs:
- derivative: bfloat16 [64, 5, 16, 2048], P('member', None, None, 'passage'), parts along dimension 0
- reduced: float32 [64, 64], P(('member', 'passage')), parts along dimension 0
- operator: float32 [1120, 32], P('member'), parts along dimension 0
- fitted: float32 [64, 32], P(('member', 'passage')), parts along dimension 0
There are 2 independent parts, one for each index of `member`. A program takes and returns all parts, laid end to end along the dimension named above; an argument that names none is the same for every part. Nothing has to cross between parts.
Inputs may be any that keep to these rules, and one draw needn't show every extreme that they name: `cycle_ids`: the value 5 marks a cell outside every groove cycle.
All inputs are finite; a program needn't handle non-finite values.
Results may differ from a plain program's by a relative error of at most 0.0031.
Values may be sent and summed in bfloat16 or wider, within the bound.
No kernel may reach another device: no remote copies, remote signals or barrier semaphores. Data moves between devices by JAX's collectives and lax.ppermute only.
A program may use at most 128 MiB of HBM per device.

v0:
```python
import math

import jax
import jax.numpy as jnp
import numpy as np
from jax import lax
from jax.sharding import PartitionSpec as P

NRING = 5


highest = lax.Precision.HIGHEST
time_step = 0.2
forcing_period = 37.0
ridge_factor = 1.0


def with_halo(block, sides, width):
    for axis, dim in sides:
        count = lax.axis_size(axis)
        forward = [(i, i + 1) for i in range(count - 1)]
        forward.append((count - 1, 0))
        backward = [(target, source) for source, target in forward]
        low = lax.ppermute(
            lax.slice_in_dim(block, block.shape[dim] - width, None, axis=dim), axis, forward
        )
        high = lax.ppermute(lax.slice_in_dim(block, 0, width, axis=dim), axis, backward)
        block = jnp.concatenate([low, block, high], axis=dim)
    return block


def flux_rate(padded, groove, damping, speed, viscosity, coupling, groove_gain, forcing):
    cell_values = padded[..., 1:-1]
    east_side = padded[..., 2:]
    west_side = padded[..., :-2]
    padded_x = jnp.pad(cell_values, ((0, 0), (0, 0), (1, 1), (0, 0)))
    north_side = padded_x[:, :, 2:, :]
    south_side = padded_x[:, :, :-2, :]
    advection = -0.5 * speed * (east_side - west_side)
    diffusion = viscosity[None, :, None, None] * (
        east_side + west_side + north_side + south_side - 4.0 * cell_values
    )
    mixing = jnp.einsum("vw,kwxt->kvxt", coupling, cell_values, precision=highest)
    source = groove_gain[None, :, None, None] * groove[:, None] + forcing[:, None]
    return advection + diffusion + mixing - damping * cell_values + source


def body(
    states,
    basis,
    snapshot_times,
    pert_ids,
    pert_table,
    cycle_ids,
    groove_kernel,
    groove_gain,
    speed,
    force_amp,
    viscosity,
    coupling,
):
    snapshots, variables, cross_cells, theta_cells = states.shape
    mode_count = basis.shape[0]
    passages = lax.axis_size("passage")
    position = lax.axis_index("passage")
    cycle_count = NRING
    cycle_levels = jnp.arange(cycle_count, dtype=jnp.int32)
    cycle_hits = cycle_ids[None] == cycle_levels[:, None, None]
    cycle_mask = cycle_hits.astype(jnp.float32).reshape(cycle_count, -1)
    cycle_mask_half = cycle_hits.astype(jnp.bfloat16).reshape(cycle_count, -1)
    peer_ids = jnp.arange(passages, dtype=jnp.int32)
    kernel_row = groove_kernel[(position - peer_ids) % passages]
    damping = pert_table[pert_ids[0]]
    cosine = jnp.cos(2.0 * math.pi * snapshot_times.astype(jnp.float32) / forcing_period)
    forcing = force_amp[None] * cosine[:, None, None]
    cycle_scale = 1.0 / math.sqrt(cross_cells * theta_cells)
    contract_dims = (((1,), (1,)), ((), ()))

    def groove_from(gathered):
        plenum = jnp.einsum("q,qkg->kg", kernel_row, gathered, precision=highest)
        return jnp.dot(plenum, cycle_mask, precision=highest).reshape(
            snapshots, cross_cells, theta_cells
        )

    start_pressure = states[:, variables - 1].reshape(snapshots, -1)
    start_cycles = (
        lax.dot_general(
            start_pressure, cycle_mask_half, contract_dims, preferred_element_type=jnp.float32
        )
        * cycle_scale
    )
    start_gathered = lax.all_gather(start_cycles[None], "passage", axis=0, tiled=True)
    start_padded = with_halo(states, (("passage", 3),), 1)
    first_rate = flux_rate(
        start_padded.astype(jnp.float32),
        groove_from(start_gathered),
        damping,
        speed,
        viscosity,
        coupling,
        groove_gain,
        forcing,
    )
    middle = states.astype(jnp.float32) + time_step * first_rate
    middle_padded = None
    middle_cycles = (
        jnp.dot(middle[:, variables - 1].reshape(snapshots, -1), cycle_mask.T, precision=highest)
        * cycle_scale
    )
    middle_gathered = lax.all_gather(middle_cycles[None], "passage", axis=0, tiled=True)
    middle_padded = with_halo(middle, (("passage", 3),), 1)
    second_rate = flux_rate(
        middle_padded,
        groove_from(middle_gathered),
        damping,
        speed,
        viscosity,
        coupling,
        groove_gain,
        forcing,
    )
    derivative = (0.5 * (first_rate + second_rate)).astype(jnp.bfloat16)
    flat_state = states.reshape(snapshots, -1)
    flat_rate = derivative.reshape(snapshots, -1)
    flat_basis = basis.reshape(mode_count, -1)
    upper_first, upper_second = np.triu_indices(mode_count)
    ridge_weight = ridge_factor * snapshots
    state_part = lax.dot_general(
        flat_state, flat_basis, contract_dims, preferred_element_type=jnp.float32
    )
    rate_part = lax.dot_general(
        flat_rate, flat_basis, contract_dims, preferred_element_type=jnp.float32
    )
    reduced = lax.psum_scatter(
        jnp.concatenate([state_part, rate_part], axis=1), "passage", scatter_dimension=0, tiled=True
    )
    coordinates = reduced[:, :mode_count]
    rate_coords = reduced[:, mode_count:]
    products = coordinates[:, upper_first] * coordinates[:, upper_second]
    design = jnp.concatenate([coordinates, products, rate_coords], axis=1)
    columns = design.shape[1]
    features = columns - mode_count
    identity = jnp.eye(columns, dtype=jnp.float32)
    own_gram = jnp.dot(design.T, design, precision=highest)
    total_gram = lax.psum(own_gram, "passage")
    factor_low = jnp.linalg.cholesky(total_gram + ridge_weight * identity)
    operator = lax.linalg.triangular_solve(
        factor_low[:features, :features],
        factor_low[features:, :features].T,
        left_side=True,
        lower=True,
        transpose_a=True,
    )
    fitted = jnp.dot(design[:, :features], operator, precision=highest)
    return (derivative, reduced, operator, fitted)


def solution(mesh):
    in_specs = (
        P("member", None, None, "passage"),
        P(None, None, None, "passage"),
        P("member"),
        P(("member", "passage")),
        P(),
        P(None, "passage"),
        P(),
        P(),
        P(None, "passage"),
        P(None, "passage"),
        P(),
        P(),
    )
    out_specs = (
        P("member", None, None, "passage"),
        P(("member", "passage"), None),
        P("member", None),
        P(("member", "passage"), None),
    )
    return jax.shard_map(body, mesh=mesh, in_specs=in_specs, out_specs=out_specs, check_vma=False)
```

profile of v0, /device:TPU:0, one launch (start us, length us, event | category | flops | bytes accessed | tf_op | source)
XLA Modules:
  0.0 442.9 jit_solution(7715456121497278818)
XLA Ops:
  10.8 5.1 %collective-permute-start.1 = (bf16[32,5,16,1]{0,2,3,1:T(8,128)(2,1)S(1)}, bf16[32,5,16,1]{0,2,3,1:T(8,128)(2,1)}, u32[]{:S(2)}, u32[]{:S(2)}) collective-permute-start(bf16[32,5,16,1]{0,2,3,1:T(8,128)(2,1)S(1)} %copy.88), channel_id=1, source_target_pairs={{1,0},{2,1},{3,2},{4,3},{5,4},{6,5},{7,6},{8,7},{9,8},{10,9},{11,1... | collective-permute-start | bytes 15368 | tf_op jit(solution)/shard_map/ppermute | solution.py:27
  16.6 19.5 %all-gather.2 = f32[16,32,5]{1,2,0:T(8,128)S(1)} all-gather(f32[1,32,5]{1,2,0:T(8,128)S(1)} %fusion.21), channel_id=2, replica_groups=mesh['member'=2,'passage'=16] {'passage'}, dimensions={0}, use_global_device_ids=true | all-gather | bytes 10880 | tf_op jit(solution)/shard_map/all_gather | solution.py:92
  51.7 4.3 multiply_add_fusion
  56.7 2.8 fusion.105
  59.7 18.1 %all-gather.3 = f32[16,32,5]{1,2,0:T(8,128)S(1)} all-gather(f32[1,32,5]{1,2,0:T(8,128)S(1)} %fusion.20), channel_id=3, replica_groups=mesh['member'=2,'passage'=16] {'passage'}, dimensions={0}, use_global_device_ids=true | all-gather | bytes 10880 | tf_op jit(solution)/shard_map/all_gather | solution.py:110
  85.1 2.9 copy.65
  87.9 2.6 collective-permute-done.3
  90.6 2.9 copy.67
  93.5 5.7 %fusion.18 = bf16[32,5,16,128]{3,1,2,0:T(8,128)(2,1)S(1)} fusion(f32[32,5,16,128]{3,1,2,0:T(8,128)} %get-tuple-element.54, f32[32,5,16,128]{3,1,2,0:T(8,128)S(1)} %get-tuple-element.53, f32[32,5,16,1]{3,1,2,0:T(8,128)} %copy.65, f32[32,5,16,1]{3,1,2,0:T(8,128)} %copy.67, f32[32,16,128]{2,1,0:T(8,128)S(1)} %copy.68, f32[32,16,128]{2,1,0:T(8,128)S(1)} %copy-done.8, ...), kind=kOutput, calls=%fused_computation.27 | convolution fusion | flops 26214400 | bytes 6726656 | tf_op jit(solution)/shard_map/vw,kwxt->kvxt/dot_general | solution.py:43
  101.2 59.3 %all-reduce.5 = f32[32,64]{1,0:T(8,128)S(1)} all-reduce(f32[32,64]{1,0:T(8,128)S(1)} %pad_maximum_fusion.3), channel_id=4, replica_groups=mesh['member'=2,'passage'=16] {'passage'}, use_global_device_ids=true, to_apply=%region_0.1.clone | all-reduce | flops 2048 | bytes 16384
  164.2 2.9 fusion.81
  168.2 91.1 %all-reduce.8.cloned.1.call-done = f32[592,592]{1,0:T(8,128)} async-done(((f32[592,592]{1,0:T(8,128)}), f32[592,592]{1,0:T(8,128)}) %all-reduce.8.cloned.1.call-update) | async-done | bytes 1401872 | tf_op jit(solution)/shard_map/psum | solution.py:145
  262.0 3.1 copy.76
  267.8 11.7 %cholesky.133 = f32[128,128]{1,0:T(8,128)S(1)} custom-call(f32[128,128]{1,0:T(8,128)S(1)} %cholesky.343), custom_call_target="Cholesky" | custom-call | tf_op jit(solution)/shard_map/jit(cholesky)/cholesky | solution.py:146
  279.6 9.8 %custom-call.38 = f32[1,128,128]{1,2,0:T(8,128)S(1)} custom-call(f32[1,128,128]{2,1,0:T(8,128)S(1)} %get-tuple-element.48), custom_call_target="InvertDiagBlocksLowerTriangular" | custom-call | tf_op jit(solution)/shard_map/jit(cholesky)/cholesky | solution.py:146
  292.1 11.9 %cholesky.272 = f32[128,128]{1,0:T(8,128)S(1)} custom-call(f32[128,128]{1,0:T(8,128)S(1)} %cholesky.347), custom_call_target="Cholesky" | custom-call | tf_op jit(solution)/shard_map/jit(cholesky)/cholesky | solution.py:146
  305.3 9.8 %custom-call.39 = f32[1,128,128]{1,2,0:T(8,128)S(1)} custom-call(f32[1,128,128]{2,1,0:T(8,128)S(1)} %get-tuple-element.45), custom_call_target="InvertDiagBlocksLowerTriangular" | custom-call | tf_op jit(solution)/shard_map/jit(cholesky)/cholesky | solution.py:146
  316.8 11.7 %cholesky.293 = f32[128,128]{1,0:T(8,128)S(1)} custom-call(f32[128,128]{1,0:T(8,128)S(1)} %cholesky.352), custom_call_target="Cholesky" | custom-call | tf_op jit(solution)/shard_map/jit(cholesky)/cholesky | solution.py:146
  329.1 9.8 %custom-call.40 = f32[1,128,128]{1,2,0:T(8,128)S(1)} custom-call(f32[1,128,128]{2,1,0:T(8,128)S(1)} %get-tuple-element.42), custom_call_target="InvertDiagBlocksLowerTriangular" | custom-call | tf_op jit(solution)/shard_map/jit(cholesky)/cholesky | solution.py:146
  340.5 12.0 %cholesky.312 = f32[128,128]{1,0:T(8,128)S(1)} custom-call(f32[128,128]{1,0:T(8,128)S(1)} %cholesky.357), custom_call_target="Cholesky" | custom-call | tf_op jit(solution)/shard_map/jit(cholesky)/cholesky | solution.py:146
  353.2 9.8 %custom-call.41 = f32[1,128,128]{1,2,0:T(8,128)S(1)} custom-call(f32[1,128,128]{2,1,0:T(8,128)S(1)} %get-tuple-element.39), custom_call_target="InvertDiagBlocksLowerTriangular" | custom-call | tf_op jit(solution)/shard_map/jit(cholesky)/cholesky | solution.py:146
  364.3 7.3 %cholesky.332 = f32[80,80]{1,0:T(8,128)S(1)} custom-call(f32[80,80]{1,0:T(8,128)S(1)} %convolution_subtract_fusion.3), custom_call_target="Cholesky" | custom-call | tf_op jit(solution)/shard_map/jit(cholesky)/cholesky | solution.py:146
  375.6 8.0 %while.1 = (s32[]{:T(128)}, f32[560,560]{1,0:T(8,128)S(1)}, s32[4,2]{0,1:T(2,128)S(1)}, f32[4,128,128]{2,1,0:T(8,128)S(1)}, s32[]{:T(128)}) while((s32[]{:T(128)}, f32[560,560]{1,0:T(8,128)S(1)}, s32[4,2]{0,1:T(2,128)S(1)}, f32[4,128,128]{2,1,0:T(8,128)S(1)}, s32[]{:T(128)}) %tuple.40), condition=%wide.while_cond, body=%wide.while_body.sunk | while | flops 2 | bytes 131181 | solution.py:147
  383.7 49.1 %custom-call.42 = f32[5,128,128]{1,2,0:T(8,128)S(1)} custom-call(f32[5,128,128]{2,1,0:T(8,128)S(1)} %pad_maximum_fusion.2), custom_call_target="InvertDiagBlocksLowerTriangular" | custom-call | tf_op jit(solution)/shard_map/triangular_solve | solution.py:147
  (173 shorter events, 59.9 us)
Async XLA Ops:
  7.2 30.6 %copy-start = (bf16[32,5,16,128]{3,2,1,0:T(8,128)(2,1)S(1)}, bf16[32,5,16,128]{3,2,1,0:T(8,128)(2,1)}, u32[]{:S(2)}) copy-start(bf16[32,5,16,128]{3,2,1,0:T(8,128)(2,1)} %param.17) | copy-start | bytes 1966084
  7.2 9.3 %slice-start = ((bf16[32,5,16,128]{3,2,1,0:T(8,128)(2,1)}), bf16[32,1,16,128]{3,2,1,0:T(8,128)(2,1)S(1)}, s32[]{:S(2)}) async-start(bf16[32,5,16,128]{3,2,1,0:T(8,128)(2,1)} %param.16), calls=%async_computation.1 | async-start | bytes 262144 | tf_op jit(solution)/shard_map/slice | solution.py:85
  7.2 9.3 %copy-start.11 = (s32[16,128]{1,0:T(8,128)S(1)}, s32[16,128]{1,0:T(8,128)}, u32[]{:S(2)}) copy-start(s32[16,128]{1,0:T(8,128)} %param.21) | copy-start | bytes 24580
  7.2 29.0 %copy-start.1 = (f32[16]{0:T(128)S(1)}, f32[16]{0:T(128)}, u32[]{:S(2)}) copy-start(f32[16]{0:T(128)} %param.22) | copy-start | bytes 196
  7.2 30.5 %copy-start.24 = (s32[32]{0:T(128)S(1)}, s32[32]{0:T(128)}, u32[]{:S(2)}) copy-start(s32[32]{0:T(128)} %param.18) | copy-start | bytes 388
  7.2 30.5 %copy-start.15 = (f32[16,128]{1,0:T(8,128)S(1)}, f32[16,128]{1,0:T(8,128)}, u32[]{:S(2)}) copy-start(f32[16,128]{1,0:T(8,128)} %param.24) | copy-start | bytes 24580
  7.2 252.1 %all-reduce.8.cloned.1.call-start = ((), (), s32[]{:S(2)}) async-start(), calls=%async_computation | async-start | bytes 3031040 | tf_op jit(solution)/shard_map/psum | solution.py:145
  8.9 28.8 %copy-start.2 = (bf16[32,5,16,128]{3,2,1,0:T(8,128)(2,1)S(1)}, bf16[32,5,16,128]{3,2,1,0:T(8,128)(2,1)}, u32[]{:S(2)}) copy-start(bf16[32,5,16,128]{3,2,1,0:T(8,128)(2,1)} %param.16) | copy-start | bytes 1966084
  9.6 29.8 %copy-start.14 = (f32[16,128]{1,0:T(8,128)S(1)}, f32[16,128]{1,0:T(8,128)}, u32[]{:S(2)}) copy-start(f32[16,128]{1,0:T(8,128)} %param.25) | copy-start | bytes 24580
  9.6 34.0 %collective-permute-start = (bf16[32,5,16,1]{0,2,3,1:T(8,128)(2,1)S(1)}, bf16[32,5,16,1]{0,2,3,1:T(8,128)(2,1)S(1)}, u32[]{:S(2)}, u32[]{:S(2)}) collective-permute-start(bf16[32,5,16,1]{0,2,3,1:T(8,128)(2,1)S(1)} %copy.87), channel_id=1, source_target_pairs={{0,1},{1,2},{2,3},{3,4},{4,5},{5,6},{6,7},{7,8},{8,9},{9,10},{10,1... | collective-permute-start | bytes 15368 | tf_op jit(solution)/shard_map/ppermute | solution.py:24
  10.1 30.1 %copy-start.20 = (s32[528]{0:T(1024)S(1)}, s32[528]{0:T(1024)}, u32[]{:S(2)}) copy-start(s32[528]{0:T(1024)} %constant.260) | copy-start | bytes 6340
  10.1 30.1 %copy-start.21 = (s32[528]{0:T(1024)S(1)}, s32[528]{0:T(1024)}, u32[]{:S(2)}) copy-start(s32[528]{0:T(1024)} %constant.261) | copy-start | bytes 6340
  10.8 34.8 %collective-permute-start.1 = (bf16[32,5,16,1]{0,2,3,1:T(8,128)(2,1)S(1)}, bf16[32,5,16,1]{0,2,3,1:T(8,128)(2,1)}, u32[]{:S(2)}, u32[]{:S(2)}) collective-permute-start(bf16[32,5,16,1]{0,2,3,1:T(8,128)(2,1)S(1)} %copy.88), channel_id=1, source_target_pairs={{1,0},{2,1},{3,2},{4,3},{5,4},{6,5},{7,6},{8,7},{9,8},{10,9},{11,1... | collective-permute-start | bytes 15368 | tf_op jit(solution)/shard_map/ppermute | solution.py:27
  37.8 13.5 %copy-start.16 = (f32[16,128]{1,0:T(8,128)}, f32[16,128]{1,0:T(8,128)S(1)}, u32[]{:S(2)}) copy-start(f32[16,128]{1,0:T(8,128)S(1)} %broadcast_multiply_fusion.1) | copy-start | bytes 24580
  39.4 11.9 %copy-start.18 = (f32[16,128]{1,0:T(8,128)}, f32[16,128]{1,0:T(8,128)S(1)}, u32[]{:S(2)}) copy-start(f32[16,128]{1,0:T(8,128)S(1)} %dynamic-slice_bitcast_fusion) | copy-start | bytes 24580
  80.5 4.5 %collective-permute-start.2 = (f32[32,5,16,1]{0,2,3,1:T(8,128)S(1)}, f32[32,5,16,1]{0,2,3,1:T(8,128)S(1)}, u32[]{:S(2)}, u32[]{:S(2)}) collective-permute-start(f32[32,5,16,1]{0,2,3,1:T(8,128)S(1)} %copy.64), channel_id=1, source_target_pairs={{1,0},{2,1},{3,2},{4,3},{5,4},{6,5},{7,6},{8,7},{9,8},{10,9},{11,1... | collective-permute-start | bytes 30728 | tf_op jit(solution)/shard_map/ppermute | solution.py:27
  84.4 6.2 %collective-permute-start.3 = (f32[32,5,16,1]{0,2,3,1:T(8,128)S(1)}, f32[32,5,16,1]{0,2,3,1:T(8,128)S(1)}, u32[]{:S(2)}, u32[]{:S(2)}) collective-permute-start(f32[32,5,16,1]{0,2,3,1:T(8,128)S(1)} %copy.66), channel_id=1, source_target_pairs={{0,1},{1,2},{2,3},{3,4},{4,5},{5,6},{6,7},{7,8},{8,9},{9,10},{10,1... | collective-permute-start | bytes 30728 | tf_op jit(solution)/shard_map/ppermute | solution.py:24
  85.0 8.5 %copy-start.8 = (f32[32,16,128]{2,1,0:T(8,128)S(1)}, f32[32,16,128]{2,1,0:T(8,128)}, u32[]{:S(2)}) copy-start(f32[32,16,128]{2,1,0:T(8,128)} %broadcast_multiply_fusion) | copy-start | bytes 786436
  85.0 8.5 %copy-start.17 = (f32[16,128]{1,0:T(8,128)S(1)}, f32[16,128]{1,0:T(8,128)}, u32[]{:S(2)}) copy-start(f32[16,128]{1,0:T(8,128)} %copy-done.16) | copy-start | bytes 24580
  85.0 8.5 %copy-start.19 = (f32[16,128]{1,0:T(8,128)S(1)}, f32[16,128]{1,0:T(8,128)}, u32[]{:S(2)}) copy-start(f32[16,128]{1,0:T(8,128)} %copy-done.18) | copy-start | bytes 24580
  85.0 8.5 %copy-start.23 = (f32[5,5]{1,0:T(8,128)S(1)}, f32[5,5]{1,0:T(8,128)}, u32[]{:S(2)}) copy-start(f32[5,5]{1,0:T(8,128)} %param.27) | copy-start | bytes 304
  85.0 8.5 %copy-start.26 = (f32[5]{0:T(128)S(1)}, f32[5]{0:T(128)}, u32[]{:S(2)}) copy-start(f32[5]{0:T(128)} %param.23) | copy-start | bytes 64
  85.0 8.5 %copy-start.28 = (f32[5]{0:T(128)S(1)}, f32[5]{0:T(128)}, u32[]{:S(2)}) copy-start(f32[5]{0:T(128)} %param.26) | copy-start | bytes 64
  93.5 7.6 %copy-start.12 = (f32[32,32]{1,0:T(8,128)S(1)}, f32[32,32]{1,0:T(8,128)}, u32[]{:S(2)}) copy-start(f32[32,32]{1,0:T(8,128)} %convolution_bitcast_fusion.1) | copy-start | bytes 12292
  (12 other events, 25.5 us)
Sparse Core Ops, SparseCore 0:
  167.3 91.9 all-reduce.7
where the time goes:
time: 451 us; the launch traced here: 443 us
  other arithmetic  154 us (34%)
  blocking collectives  96.9 us (21%)
  waiting for transfers between devices  93.8 us (21%)
  local copies, waits for them, and re-layouts  44.7 us (10%)
  matrix products  26.2 us (6%)
  between operations  19.6 us (4%)
  starting transfers between devices  7.28 us (2%)
    another operation x19, other arithmetic, body(): factor_low = jnp.linalg.cholesky(total_gram + ridge_weight * identity)  97.2 us
    psum x1, waiting for transfers between devices, body(): total_gram = lax.psum(own_gram, 'passage')  91.1 us
    unnamed x1, blocking collectives  59.3 us
    another operation x7, other arithmetic, body(): lax.linalg.triangular_solve(factor_low[:features, :features], factor_low[...  49.4 us
    all_gather x1, blocking collectives, body(): lax.all_gather(start_cycles[None], 'passage', axis=0, tiled=True)  19.5 us
    all_gather x1, blocking collectives, body(): lax.all_gather(middle_cycles[None], 'passage', axis=0, tiled=True)  18.1 us
    dot_general x2, matrix products, flux_rate(): jnp.einsum('vw,kwxt->kvxt', coupling, cell_values, precision=highest)  10 us
  transfers between devices with their start and end apart: 5, of which 2 were waited for; matrix products, arithmetic and copies ran while one was open for 4% of the time, Pallas kernels for 0%

commit v1 on v0

v1 whole, which is shorter than its diff:
```python
import functools
import math

import jax
import jax.numpy as jnp
import numpy as np
from jax import lax
from jax.experimental import pallas as pl
from jax.experimental.pallas import tpu as pltpu
from jax.sharding import PartitionSpec as P

F32 = jnp.float32
BF16 = jnp.bfloat16
NRING = 5
NV = 5
NX = 16
LANES = 128
PERIOD = 37
TIME_STEP = 0.2
RIDGE_FACTOR = 1.0
CHUNK = 32
BLOB = 16
EDGE = 48
ROWS = BLOB + 2 * EDGE

HIGH = lax.Precision.HIGHEST
NT = (((1,), (1,)), ((), ()))
VMEM = pl.BlockSpec(memory_space=pltpu.VMEM)
SMEM = pl.BlockSpec(memory_space=pltpu.SMEM)


def iota(shape, axis):
    return lax.broadcasted_iota(jnp.int32, shape, axis)


def roll(value, shift, axis):
    size = value.shape[axis]
    return pltpu.roll(value, shift % size if isinstance(shift, int) else shift, axis)


def split(value):
    high = value.astype(BF16).astype(F32)
    return high, (value - high).astype(BF16).astype(F32)


def north_south(u):
    row = iota(u.shape, 0)
    north = jnp.where(row == NX - 1, 0.0, roll(u, -1, 0))
    south = jnp.where(row == 0, 0.0, roll(u, 1, 0))
    return north + south


def cycle_masks(ids):
    return jnp.concatenate([jnp.where(ids == g, 1.0, 0.0) for g in range(NRING)], axis=0)


def lane_part():
    return iota((8, LANES), 1) % 4


def before_kernel(
    times, pert_ids, visc, coup, table, states, pert, ids_ref, speed_ref, force_ref, out, fields
):
    chunks = out.shape[0]
    speed = speed_ref[...]
    force = force_ref[...]
    damping = pert[pert_ids[0]]
    ids = ids_ref[...]
    visc_p = visc[NV - 1]
    lane = iota((NX, LANES), 1)
    half_speed = 0.5 * speed
    coef_east = jnp.where(lane == LANES - 1, 0.0, visc_p - half_speed)
    coef_west = jnp.where(lane == 0, 0.0, visc_p + half_speed)
    coef_own = coup[NV - 1, NV - 1] - 4.0 * visc_p - damping
    masks = cycle_masks(ids)
    masks_half = masks.astype(BF16)
    c8 = lane_part()
    row8 = iota((8, LANES), 0)
    quad = iota((NX, LANES), 1) // 4
    scale = 1.0 / math.sqrt(NX * LANES)

    def pieces(column):
        out16 = jnp.zeros((NX, LANES), F32)
        spot = 0
        for field in (speed, force, damping, ids.astype(F32)):
            for piece in split(field):
                moved = roll(piece, spot - column, 1)
                out16 = jnp.where(lane == spot, moved, out16)
                spot += 1
        return jnp.where(iota((8, LANES), 1) < 64, out16[:8], roll(out16[8:], 64, 1))

    params_right = pieces(LANES - 1)
    params_left = pieces(0)

    east_hi, east_lo = split(jnp.where(lane == LANES - 1, visc_p - half_speed, 0.0))
    west_hi, west_lo = split(jnp.where(lane == 0, visc_p + half_speed, 0.0))
    ids_f = ids.astype(F32)
    id_east = jnp.where(lane == LANES - 1, ids_f, 0.0)
    id_west = jnp.where(lane == 0, ids_f, 0.0)
    ones = jnp.ones((NX, LANES), BF16)
    filler = jnp.zeros((LANES - 32, LANES), F32)

    def as_rows(east, west):
        stacked = jnp.concatenate([east, west, filler], axis=0).astype(BF16)
        return lax.dot_general(ones, stacked, NT, preferred_element_type=F32)[:8]

    row_hi = as_rows(east_hi, west_hi)
    row_lo = as_rows(east_lo, west_lo)
    row_id = as_rows(id_east, id_west)
    counts = lax.dot_general(ones, masks_half, NT, preferred_element_type=F32)[:8]
    spread = jnp.where(
        iota((NRING * NX, LANES), 1) == 32 + iota((NRING * NX, LANES), 0) // NX, 1.0, 0.0
    )
    counts = jnp.dot(counts, spread, precision=HIGH, preferred_element_type=F32)
    count_hi, count_lo = split(counts)
    row_hi = row_hi + count_hi
    row_lo = row_lo + count_lo

    size = CHUNK * NX
    same_x = iota((NRING * NX, 3 * size), 0) % NX == iota((NRING * NX, 3 * size), 1) % NX
    snap_of_row = iota((size, LANES), 0) // NX == iota((size, LANES), 1) // 4
    part_of_lane = iota((size, LANES), 1) % 4
    to_start = jnp.where(snap_of_row & (part_of_lane < 2), scale, 0.0)
    to_rate = jnp.where(snap_of_row & (part_of_lane >= 2), scale, 0.0)

    def chunk_step(chunk, carry):
        first = chunk * CHUNK

        def snap(k, edges):
            u = [states[first + k, v].astype(F32) for v in range(NV)]
            p = u[NV - 1]
            cosine = table[lax.rem(times[first + k], PERIOD)]
            rate = coef_east * roll(p, -1, 1) + coef_west * roll(p, 1, 1)
            rate = rate + visc_p * north_south(p) + coef_own * p + cosine * force
            for v in range(NV - 1):
                rate = rate + coup[NV - 1, v] * u[v]
            high, low = split(rate)
            at = pl.multiple_of(k * NX, NX)
            fields[pl.ds(at, NX), :] = p.astype(BF16)
            fields[pl.ds(pl.multiple_of(size + at, NX), NX), :] = high.astype(BF16)
            fields[pl.ds(pl.multiple_of(2 * size + at, NX), NX), :] = low.astype(BF16)
            return tuple(
                jnp.where(quad == k, roll(u[v], 4 * k + 2, 1), edges[v]) for v in range(NV)
            )

        edges = tuple(jnp.zeros((NX, LANES), F32) for _ in range(NV))
        if chunks == 1:
            for k in range(CHUNK):
                edges = snap(k, edges)
        else:
            edges = lax.fori_loop(0, CHUNK, snap, edges)
        sums = lax.dot_general(masks_half, fields[...], NT, preferred_element_type=F32)
        sums = jnp.where(same_x, sums, 0.0)
        by_cycle = jnp.sum(sums.reshape(NRING, NX, 3 * size), axis=1)
        by_cycle = jnp.concatenate([by_cycle, jnp.zeros((3, 3 * size), F32)], axis=0)
        start = by_cycle[:, :size]
        rate = by_cycle[:, size : 2 * size] + by_cycle[:, 2 * size :]
        packed = jnp.dot(start, to_start, precision=HIGH, preferred_element_type=F32)
        packed += jnp.dot(rate, to_rate, precision=HIGH, preferred_element_type=F32)
        high, low = split(packed)
        packed = jnp.where(c8 % 2 == 0, high, low)
        packed = jnp.where(row8 < NRING, packed, 0.0)
        for at, row in ((5, row_hi), (6, row_lo), (7, row_id)):
            packed = jnp.where(row8 == at, row, packed)
        p_low, p_high = edges[NV - 1][:8], edges[NV - 1][8:]
        p_edges = jnp.where(
            (c8 == 1) | (c8 == 2), p_low, jnp.where(c8 == 3, roll(p_high, 1, 1), roll(p_high, -1, 1))
        )
        right = [jnp.where(c8 < 2, t[:8], roll(t[8:], 2, 1)) for t in edges]
        left = [jnp.where(c8 >= 2, t[:8], roll(t[8:], -2, 1)) for t in edges]
        rows = [packed, p_edges] + right + [params_right] + left + [params_left]
        out[chunk] = jnp.concatenate(rows, axis=0).astype(BF16)
        return carry

    if chunks == 1:
        chunk_step(0, 0)
    else:
        lax.fori_loop(0, chunks, chunk_step, 0)


def after_kernel(
    carries,
    times,
    pert_ids,
    place,
    kern,
    gain,
    visc,
    coup,
    table,
    states,
    basis,
    pert,
    ids_ref,
    speed_ref,
    force_ref,
    own_ref,
    near_ref,
    *rest,
):
    carry_refs = rest[:carries]
    low_ref, high_ref, deriv, partial, mixed, raw, cyc0, cyc1, grooves, halo0, halo1 = rest[carries:]
    chunks = own_ref.shape[0]
    passages = kern.shape[0]
    half = passages // 2
    me = place[0]
    odd = me % 2 == 1
    speed = speed_ref[...]
    force = force_ref[...]
    damping = pert[pert_ids[0]]
    ids = ids_ref[...]
    half_speed = 0.5 * speed
    lane = iota((NX, LANES), 1)
    c16 = lane % 4
    masks = cycle_masks(ids).astype(BF16)
    masks_twice = jnp.concatenate([masks, masks], axis=0)
    scale = 1.0 / math.sqrt(NX * LANES)
    size = CHUNK * NX

    src = iota((LANES, LANES), 0)
    dst = iota((LANES, LANES), 1) // 4 * 4
    mixers = [(src == dst) | (src == dst + 1), (src == dst + 2) | (src == dst + 3)]
    mixers += [src == dst + 2, src == dst + 1, src == dst + 3, src == dst]
    mix = jnp.concatenate([jnp.where(m, 1.0, 0.0).astype(BF16) for m in mixers], axis=1)
    pick_snap = jnp.where(iota((size, LANES), 1) == iota((size, LANES), 0) // NX * 4, 1.0, 0.0)
    pick_snap = pick_snap.astype(BF16)
    wide = 4 * NRING * NX
    same_x = iota((size, wide), 0) % NX == iota((size, wide), 1) % NX

    def unpack_right(t):
        return jnp.concatenate([t, roll(t, -2, 1)], axis=0)

    def unpack_left(t):
        return jnp.concatenate([t, roll(t, 2, 1)], axis=0)

    def chunk_step(chunk, carry):
        first = chunk * CHUNK
        raw[: half * BLOB, :] = low_ref[chunk, : half * BLOB, :].astype(F32)
        raw[half * BLOB :, :] = high_ref[chunk, : half * BLOB, :].astype(F32)
        mixed[...] = jnp.dot(raw[...].astype(BF16), mix, preferred_element_type=F32)

        def slot(offset):
            other = lax.rem(me + offset + passages, passages)
            return pl.multiple_of(jnp.bitwise_xor(me, other) * BLOB, BLOB)

        def load(offset, carry):
            cyc0[pl.ds(pl.multiple_of(offset * 8, 8), 8), :] = mixed[pl.ds(slot(offset), 8), :LANES]
            return carry

        lax.fori_loop(0, passages, load, 0, unroll=passages <= 16)

        def plenum0(offset):
            total = jnp.zeros((8, LANES), F32)
            if passages <= 16 and isinstance(offset, int):
                for other in range(passages):
                    total += kern[(offset - other) % passages] * cyc0[other * 8 : other * 8 + 8, :]
                return total

            def add(other, total):
                weight = kern[lax.rem(offset - other + 2 * passages, passages)]
                return total + weight * cyc0[pl.ds(pl.multiple_of(other * 8, 8), 8), :]

            return lax.fori_loop(0, passages, add, total)

        row8 = iota((8, LANES), 0)
        lane8 = iota((8, LANES), 1)

        def second(offset, total):
            own = slot(offset)
            east, west = slot(offset + 1), slot(offset - 1)
            coefs = raw[pl.ds(own, 8), :]
            id_row = coefs[7:8, :].astype(jnp.int32)
            hit = (id_row == row8) & (lane8 < 32)
            left = jnp.concatenate(
                [jnp.where(hit, coefs[5:6, :], 0.0), jnp.where(hit, coefs[6:7, :], 0.0)], axis=0
            )
            right = jnp.concatenate(
                [
                    mixed[pl.ds(pl.multiple_of(east + 8, 8), 8), 2 * LANES : 3 * LANES],
                    mixed[pl.ds(pl.multiple_of(east + 8, 8), 8), 4 * LANES : 5 * LANES],
                    mixed[pl.ds(pl.multiple_of(west + 8, 8), 8), 3 * LANES : 4 * LANES],
                    mixed[pl.ds(pl.multiple_of(west + 8, 8), 8), 5 * LANES :],
                    jnp.zeros((LANES - 32, LANES), F32),
                ],
                axis=0,
            )
            edge = jnp.dot(left.astype(BF16), right.astype(BF16), preferred_element_type=F32)
            edge = (edge[:8] + edge[8:]) * scale
            count = jnp.where(lane8 == 32 + row8, coefs[5:6, :] + coefs[6:7, :], 0.0)
            count = jnp.sum(count, axis=1, keepdims=True) * (scale * gain[NV - 1])
            rate = mixed[pl.ds(own, 8), LANES : 2 * LANES] + edge + count * plenum0(offset)
            if isinstance(offset, int):
                start = cyc0[offset * 8 : offset * 8 + 8, :]
                weight = kern[-offset % passages]
            else:
                start = cyc0[pl.ds(pl.multiple_of(offset * 8, 8), 8), :]
                weight = kern[lax.rem(passages - offset, passages)]
            return total + weight * (start + TIME_STEP * rate)

        total = jnp.zeros((8, LANES), F32)
        if passages <= 16:
            for offset in range(passages):
                total = second(offset, total)
        else:
            total = lax.fori_loop(0, passages, second, total)
        own0, own1 = plenum0(0), total
        west0, east0 = plenum0(passages - 1), plenum0(1)

        stack = []
        for tile in (own0, own1):
            for piece in split(tile):
                stack += [jnp.broadcast_to(piece[g : g + 1], (NX, LANES)) for g in range(NRING)]
        stack = jnp.concatenate(stack, axis=0).astype(BF16)
        picked = lax.dot_general(pick_snap, stack, NT, preferred_element_type=F32)
        picked = jnp.where(same_x, picked, 0.0).astype(BF16)
        for stage in range(2):
            grooves[stage] = jnp.dot(
                picked[:, stage * wide // 2 : (stage + 1) * wide // 2],
                masks_twice,
                preferred_element_type=F32,
            )

        far = carry_refs[-1][chunk, -EDGE:, :].astype(F32)
        for index in range(carries - 2, -1, -1):
            bit = jnp.bitwise_and(jnp.right_shift(me, index + 1), 1)
            arrived = (bit == 1) != odd
            far = jnp.where(arrived, carry_refs[index][chunk, -EDGE:, :].astype(F32), far)
        near = near_ref[chunk].astype(F32)
        own = own_ref[chunk].astype(F32)
        west = jnp.where(odd, near[BLOB : BLOB + EDGE], far)
        east = jnp.where(odd, far, near[BLOB + EDGE :])

        def param(side, index):
            t = side[40:48]
            low = t[:, index : index + 1] + t[:, index + 1 : index + 2]
            high = t[:, 64 + index : 65 + index] + t[:, 65 + index : 66 + index]
            return jnp.broadcast_to(jnp.concatenate([low, high], axis=0), (NX, LANES))

        speed_h, force_h, damp_h, ids_h = (
            jnp.where(c16 < 2, param(west, 2 * i), param(east, 2 * i)) for i in range(4)
        )
        groove_h = jnp.zeros((NX, LANES), F32)
        for g in range(NRING):
            value = jnp.where(c16 < 2, west0[g : g + 1], east0[g : g + 1])
            groove_h = jnp.where(ids_h == g, value, groove_h)
        cos_h = jnp.zeros((NX, LANES), F32)
        for k in range(CHUNK):
            cos_h = jnp.where(lane // 4 == k, table[lax.rem(times[first + k], PERIOD)], cos_h)
        halo = []
        ours = []
        for v in range(NV):
            at = slice(8 * v, 8 * v + 8)
            halo.append(jnp.where(c16 < 2, unpack_right(west[at]), unpack_left(east[at])))
            mine = slice(BLOB + 8 * v, BLOB + 8 * v + 8)
            mine_left = slice(BLOB + EDGE + 8 * v, BLOB + EDGE + 8 * v + 8)
            ours.append(jnp.where(c16 < 2, unpack_right(own[mine]), unpack_left(own[mine_left])))
        for v in range(NV):
            h = halo[v]
            e = roll(jnp.where(c16 == 3, h, ours[v]), -1, 1)
            w = roll(jnp.where(c16 == 0, h, ours[v]), 1, 1)
            rate = visc[v] * (e + w + north_south(h) - 4.0 * h) - 0.5 * speed_h * (e - w)
            rate = rate - damp_h * h + gain[v] * groove_h + force_h * cos_h
            for other in range(NV):
                rate = rate + coup[v, other] * halo[other]
            halo0[v] = h
            halo1[v] = h + TIME_STEP * rate

        def flux(u, halos, source, spread):
            result = []
            for v in range(NV):
                h = roll(halos[v], spread, 1)
                e = roll(jnp.where(lane == 0, h, u[v]), -1, 1)
                w = roll(jnp.where(lane == LANES - 1, h, u[v]), 1, 1)
                rate = visc[v] * (e + w + north_south(u[v])) - half_speed * (e - w)
                rate = rate + (coup[v, v] - 4.0 * visc[v] - damping) * u[v]
                for other in range(NV):
                    if other != v:
                        rate = rate + coup[v, other] * u[other]
                result.append(rate + gain[v] * source[0] + source[1])
            return result

        def snap(k, carry):
            u = [states[first + k, v].astype(F32) for v in range(NV)]
            drive = table[lax.rem(times[first + k], PERIOD)] * force
            at = pl.multiple_of(k * NX, NX)
            spread = -(4 * k + 2) if isinstance(k, int) else 2 * LANES - 4 * k - 2
            rate0 = flux(u, halo0, (grooves[0, pl.ds(at, NX), :], drive), spread)
            middle = [u[v] + TIME_STEP * rate0[v] for v in range(NV)]
            rate1 = flux(middle, halo1, (grooves[1, pl.ds(at, NX), :], drive), spread)
            for v in range(NV):
                deriv[first + k, v] = (0.5 * (rate0[v] + rate1[v])).astype(BF16)
            return carry

        if chunks == 1:
            for k in range(CHUNK):
                snap(k, 0)
        else:
            lax.fori_loop(0, CHUNK, snap, 0)

        modes = basis.shape[0]
        flat_basis = jnp.concatenate(
            [basis[:, v].reshape(modes * NX, LANES) for v in range(NV)], axis=1
        )
        diagonal = (
            iota((size, modes * NX), 0) % NX == iota((size, modes * NX), 1) % NX
        )
        mode_of = iota((modes * NX, 2 * modes), 0) // NX
        column = iota((modes * NX, 2 * modes), 1)
        total = jnp.zeros((CHUNK, 2 * modes), F32)
        for part, source in ((0, states), (1, deriv)):
            rows = jnp.concatenate(
                [source[pl.ds(first, CHUNK), v].reshape(size, LANES) for v in range(NV)], axis=1
            )
            pairs = lax.dot_general(rows, flat_basis, NT, preferred_element_type=F32)
            pairs = jnp.where(diagonal, pairs, 0.0)
            pairs = jnp.sum(pairs.reshape(CHUNK, NX, modes * NX), axis=1)
            gather = jnp.where(mode_of + part * modes == column, 1.0, 0.0)
            total += jnp.dot(pairs, gather, precision=HIGH, preferred_element_type=F32)
        partial[pl.ds(pl.multiple_of(first, CHUNK), CHUNK), :] = total
        return carry

    if chunks == 1:
        chunk_step(0, 0)
    else:
        lax.fori_loop(0, chunks, chunk_step, 0)


def fit_kernel(ridge, place, red_ref, first_ref, second_ref, lin_ref, reduced, operator, fitted, full):
    snaps, modes = red_ref.shape[0], red_ref.shape[1] // 2
    red = red_ref[...]
    coords = red[:, :modes]
    rates = red[:, modes:]
    dot = functools.partial(
        lax.dot_general, precision=HIGH, preferred_element_type=F32
    )
    gram = dot(coords, coords, NT)
    squares = coords * coords
    kernel = gram + 0.5 * (gram * gram + dot(squares, squares, NT))
    eye = jnp.where(iota((snaps, snaps), 0) == iota((snaps, snaps), 1), ridge, 0.0)
    system = jnp.concatenate([kernel + eye, rates], axis=1)
    width = snaps + modes
    row = iota((snaps, width), 0)
    for j in range(snaps):
        pivot = system[j : j + 1, :] / system[j : j + 1, j : j + 1]
        factor = jnp.where(row == j, 0.0, jnp.broadcast_to(system[:, j : j + 1], (snaps, width)))
        system = jnp.where(row == j, pivot, system - factor * pivot)
    solved = system[:, snaps:]
    one = (((1,), (0,)), ((), ()))
    design = dot(coords, first_ref[...], one) * (dot(coords, second_ref[...], one) + lin_ref[...])
    operator[...] = dot(design, solved, (((0,), (0,)), ((), ())))
    full[...] = dot(kernel, solved, one)
    each = fitted.shape[0]
    for i in range(each):
        fitted[i : i + 1, :] = full[pl.ds(place[0] * each + i, 1), :]
        reduced[i : i + 1, :] = red_ref[pl.ds(place[0] * each + i, 1), :]


def body(
    states,
    basis,
    snapshot_times,
    pert_ids,
    pert_table,
    cycle_ids,
    groove_kernel,
    groove_gain,
    speed,
    force_amp,
    viscosity,
    coupling,
):
    snaps = states.shape[0]
    modes = basis.shape[0]
    chunks = snaps // CHUNK
    passages = lax.axis_size("passage")
    rounds = passages.bit_length() - 1
    position = lax.axis_index("passage")
    place = position.reshape(1).astype(jnp.int32)
    angles = 2.0 * math.pi * np.arange(PERIOD) / PERIOD
    table = jnp.asarray(np.cos(angles).astype(np.float32))

    def swap(value, mask):
        pairs = [(i, i ^ mask) for i in range(passages)]
        return lax.ppermute(value, "passage", pairs)

    first = pl.pallas_call(
        before_kernel,
        out_shape=jax.ShapeDtypeStruct((chunks, ROWS, LANES), BF16),
        in_specs=[SMEM] * 5 + [VMEM] * 5,
        out_specs=VMEM,
        scratch_shapes=[pltpu.VMEM((3 * CHUNK * NX, LANES), BF16)],
        compiler_params=pltpu.CompilerParams(vmem_limit_bytes=40 * 2**20),
        name="before",
    )(
        snapshot_times,
        pert_ids,
        viscosity,
        coupling,
        table,
        states,
        pert_table,
        cycle_ids,
        speed,
        force_amp,
    )
    near = swap(first, 1)
    group = jnp.concatenate([first[:, :BLOB], near[:, :BLOB]], axis=1)
    odd = position % 2
    carry = lax.dynamic_slice_in_dim(near, BLOB + EDGE * odd, EDGE, axis=1)
    carries = []
    for r in range(1, rounds):
        message = jnp.concatenate([group, carry], axis=1)
        if r > 1:
            carries.append(message)
        got = swap(message, 1 << r)
        carry = got[:, -EDGE:]
        if r < rounds - 1:
            group = jnp.concatenate([group, got[:, :-EDGE]], axis=1)
    carries.append(got)

    derivative, partial = pl.pallas_call(
        functools.partial(after_kernel, len(carries)),
        out_shape=(
            jax.ShapeDtypeStruct(states.shape, BF16),
            jax.ShapeDtypeStruct((snaps, 2 * modes), F32),
        ),
        in_specs=[SMEM] * 8 + [VMEM] * (10 + len(carries)),
        out_specs=(VMEM, VMEM),
        scratch_shapes=[
            pltpu.VMEM((passages * BLOB, 6 * LANES), F32),
            pltpu.VMEM((passages * BLOB, LANES), F32),
            pltpu.VMEM((passages * 8, LANES), F32),
            pltpu.VMEM((passages * 8, LANES), F32),
            pltpu.VMEM((2, CHUNK * NX, LANES), F32),
            pltpu.VMEM((NV, NX, LANES), F32),
            pltpu.VMEM((NV, NX, LANES), F32),
        ],
        compiler_params=pltpu.CompilerParams(vmem_limit_bytes=48 * 2**20),
        name="after",
    )(
        snapshot_times,
        pert_ids,
        place,
        groove_kernel,
        groove_gain,
        viscosity,
        coupling,
        table,
        states,
        basis,
        pert_table,
        cycle_ids,
        speed,
        force_amp,
        first,
        near,
        *carries,
        message,
        got,
    )
    total = partial
    for r in range(rounds):
        total = total + swap(total, 1 << r)

    upper_first, upper_second = np.triu_indices(modes)
    features = modes + len(upper_first)
    pick_first = np.zeros((modes, features), np.float32)
    pick_second = np.zeros((modes, features), np.float32)
    linear = np.zeros((1, features), np.float32)
    pick_first[np.arange(modes), np.arange(modes)] = 1.0
    linear[0, :modes] = 1.0
    pick_first[upper_first, modes + np.arange(len(upper_first))] = 1.0
    pick_second[upper_second, modes + np.arange(len(upper_first))] = 1.0
    each = snaps // passages
    reduced, operator, fitted = pl.pallas_call(
        functools.partial(fit_kernel, RIDGE_FACTOR * snaps),
        out_shape=(
            jax.ShapeDtypeStruct((each, 2 * modes), F32),
            jax.ShapeDtypeStruct((features, modes), F32),
            jax.ShapeDtypeStruct((each, modes), F32),
        ),
        in_specs=[SMEM] + [VMEM] * 4,
        out_specs=(VMEM, VMEM, VMEM),
        scratch_shapes=[pltpu.VMEM((snaps, modes), F32)],
        compiler_params=pltpu.CompilerParams(vmem_limit_bytes=16 * 2**20),
        name="fit",
    )(place, total, jnp.asarray(pick_first), jnp.asarray(pick_second), jnp.asarray(linear))
    return derivative, reduced, operator, fitted


def solution(mesh):
    in_specs = (
        P("member", None, None, "passage"),
        P(None, None, None, "passage"),
        P("member"),
        P(("member", "passage")),
        P(),
        P(None, "passage"),
        P(),
        P(),
        P(None, "passage"),
        P(None, "passage"),
        P(),
        P(),
    )
    out_specs = (
        P("member", None, None, "passage"),
        P(("member", "passage"), None),
        P("member", None),
        P(("member", "passage"), None),
    )
    return jax.shard_map(body, mesh=mesh, in_specs=in_specs, out_specs=out_specs, check_vma=False)
```

time: 451 us -> 53.1 us (0.12); the launches traced: 443 us -> 52.7 us
  other arithmetic: 154 us -> 0.03 us
  blocking collectives: 96.9 us -> 0 us
  waiting for transfers between devices: 93.8 us -> 13.1 us
  local copies, waits for them, and re-layouts: 44.7 us -> 6.62 us
  matrix products: 26.2 us -> 0 us
  between operations: 19.6 us -> 1.48 us
  Pallas kernels: 0 us -> 16.1 us
  starting transfers between devices: 7.28 us -> 15.4 us
    another operation x26 -> x0, other arithmetic: 147 us -> none  [the longest x19 97.2 us: body(): factor_low = jnp.linalg.cholesky(total_gram + ridge_weight * identity)]
    psum x1 -> x0, waiting for transfers between devices: 91.1 us -> none  [body(): total_gram = lax.psum(own_gram, 'passage')]
    unnamed x1 -> x0, blocking collectives: 59.3 us -> none
    all_gather x2 -> x0, blocking collectives: 37.6 us -> none  [the longest x1 19.5 us: body(): lax.all_gather(start_cycles[None], 'passage', axis=0, tiled=True)]
    dot_general x12 -> x0, matrix products: 17.3 us -> none  [the longest x2 10 us: flux_rate(): jnp.einsum('vw,kwxt->kvxt', coupling, cell_values, precision=highest)]
    pallas_call x0 -> x3, Pallas kernels: none -> 16.1 us  [the longest x1 10.5 us: body(): pl.pallas_call(functools.partial(after_kernel, len(carries)), out_shape=(...]
    ppermute x4 -> x8, waiting for transfers between devices: 2.65 us -> 13.1 us  [swap(): return lax.ppermute(value, 'passage', pairs)]
    slice x9 -> x3, local copies, waits for them, and re-layouts: 10.4 us -> 0.01 us  [the longest x2 0.01 us: body(): group = jnp.concatenate([first[:, :BLOB], near[:, :BLOB]], axis=1)]
  transfers between devices with their start and end apart: 5 -> 8, of which waited for: 2 -> 8; matrix products, arithmetic and copies ran while one was open for 4% -> 0% of each run, Pallas kernels for 0% -> 0%
where the time goes in v1:
time: 53.1 us; the launch traced here: 52.7 us
  Pallas kernels  16.1 us (30%)
  starting transfers between devices  15.4 us (29%)
  waiting for transfers between devices  13.1 us (25%)
  local copies, waits for them, and re-layouts  6.62 us (12%)
  between operations  1.48 us (3%)
    ppermute x8, starting transfers between devices, swap(): return lax.ppermute(value, 'passage', pairs)  15.4 us
    ppermute x8, waiting for transfers between devices, swap(): return lax.ppermute(value, 'passage', pairs)  13.1 us
    pallas_call x1, Pallas kernels, body(): pl.pallas_call(functools.partial(after_kernel, len(carries)), out_shape=(...  10.5 us
    unnamed x43, local copies, waits for them, and re-layouts  6.61 us
    pallas_call x1, Pallas kernels, body(): pl.pallas_call(functools.partial(fit_kernel, RIDGE_FACTOR * snaps), out_s...  3.88 us
    pallas_call x1, Pallas kernels, body(): pl.pallas_call(before_kernel, out_shape=jax.ShapeDtypeStruct((chunks, ROW...  1.66 us
  transfers between devices with their start and end apart: 8, of which 8 were waited for; matrix products, arithmetic and copies ran while one was open for 0% of the time, Pallas kernels for 0%

profile of v1, /device:TPU:0, one launch (start us, length us, event | category | flops | bytes accessed | tf_op | source)
XLA Modules:
  0.0 52.7 jit_solution(13743762004005027111)
XLA Ops:
  1.4 1.1 %copy-done = bf16[32,5,16,128]{3,2,1,0:T(8,128)(2,1)S(1)} copy-done((bf16[32,5,16,128]{3,2,1,0:T(8,128)(2,1)S(1)}, bf16[32,5,16,128]{3,2,1,0:T(8,128)(2,1)}, u32[]{:S(2)}) %copy-start) | copy-done | bytes 655384
  2.5 0.8 %copy-done.3 = f32[8,16,128]{2,1,0:T(8,128)S(1)} copy-done((f32[8,16,128]{2,1,0:T(8,128)S(1)}, f32[8,16,128]{2,1,0:T(8,128)}, u32[]{:S(2)}) %copy-start.3) | copy-done | bytes 65560
  3.3 0.7 %copy-done.7 = s32[16,128]{1,0:T(8,128)S(1)} copy-done((s32[16,128]{1,0:T(8,128)S(1)}, s32[16,128]{1,0:T(8,128)}, u32[]{:S(2)}) %copy-start.7) | copy-done | bytes 8216
  4.0 0.7 %copy-done.9 = f32[16,128]{1,0:T(8,128)S(1)} copy-done((f32[16,128]{1,0:T(8,128)S(1)}, f32[16,128]{1,0:T(8,128)}, u32[]{:S(2)}) %copy-start.9) | copy-done | bytes 8216
  4.7 0.7 %copy-done.11 = f32[16,128]{1,0:T(8,128)S(1)} copy-done((f32[16,128]{1,0:T(8,128)S(1)}, f32[16,128]{1,0:T(8,128)}, u32[]{:S(2)}) %copy-start.11) | copy-done | bytes 8216
  6.1 1.7 %before.1.own_ref = bf16[1,112,128]{2,1,0:T(8,128)(2,1)S(1)} custom-call(s32[32]{0:T(128)S(1)} %copy-done.16, s32[1]{0:T(128)S(6)} %copy.21.pert_ids, f32[5]{0:T(128)S(1)} %copy-done.17, f32[5,5]{1,0:T(8,128)S(1)} %copy-done.13, f32[37]{0:T(128)S(1)} %copy-done.18, bf16[32,5,16,128]{3,2,1,0:T(8,128)(2,1)S(1)} %copy-done, f32[8,16,128]{2,1,0:T(8,128)S(1)} %copy-done.3, ...), custom_call_target="tpu_custom_call" | custom-call | tf_op jit(solution)/shard_map/before/pallas_call | solution.py:486
  8.3 0.9 %collective-permute-done.near_ref = bf16[1,112,128]{2,1,0:T(8,128)(2,1)S(1)} collective-permute-done((bf16[1,112,128]{2,1,0:T(8,128)(2,1)S(1)}, bf16[1,112,128]{2,1,0:T(8,128)(2,1)S(1)}, u32[]{:S(2)}, u32[]{:S(2)}) %collective-permute-start) | collective-permute-done | bytes 28704 | tf_op jit(solution)/shard_map/ppermute | solution.py:484
  9.1 2.9 %collective-permute-start.1 = (bf16[1,80,128]{2,1,0:T(8,128)(2,1)S(1)}, bf16[1,80,128]{2,1,0:T(8,128)(2,1)S(1)}, u32[]{:S(2)}, u32[]{:S(2)}) collective-permute-start(bf16[1,80,128]{2,1,0:T(8,128)(2,1)S(1)} %pad_maximum_fusion.2), channel_id=1, source_target_pairs={{0,2},{1,3},{2,0},{3,1},{4,6},{5,7},{6,4},{7,5},{8,10},{9,11},{10,... | collective-permute-start | bytes 61448 | tf_op jit(solution)/shard_map/ppermute | solution.py:484
  12.1 1.8 %collective-permute-done.1 = bf16[1,80,128]{2,1,0:T(8,128)(2,1)S(1)} collective-permute-done((bf16[1,80,128]{2,1,0:T(8,128)(2,1)S(1)}, bf16[1,80,128]{2,1,0:T(8,128)(2,1)S(1)}, u32[]{:S(2)}, u32[]{:S(2)}) %collective-permute-start.1) | collective-permute-done | bytes 20512 | tf_op jit(solution)/shard_map/ppermute | solution.py:484
  13.8 2.1 %collective-permute-start.2 = (bf16[1,112,128]{2,1,0:T(8,128)(2,1)S(1)}, bf16[1,112,128]{2,1,0:T(8,128)(2,1)S(1)}, u32[]{:S(2)}, u32[]{:S(2)}) collective-permute-start(bf16[1,112,128]{2,1,0:T(8,128)(2,1)S(1)} %pad_maximum_fusion.1.rest_0_), channel_id=1, source_target_pairs={{0,4},{1,5},{2,6},{3,7},{4,0},{5,1},{6,2},{7,3},{8,12},{9,13},{10,... | collective-permute-start | bytes 86024 | tf_op jit(solution)/shard_map/ppermute | solution.py:484
  15.9 1.8 %collective-permute-done.2 = bf16[1,112,128]{2,1,0:T(8,128)(2,1)S(1)} collective-permute-done((bf16[1,112,128]{2,1,0:T(8,128)(2,1)S(1)}, bf16[1,112,128]{2,1,0:T(8,128)(2,1)S(1)}, u32[]{:S(2)}, u32[]{:S(2)}) %collective-permute-start.2) | collective-permute-done | bytes 28704 | tf_op jit(solution)/shard_map/ppermute | solution.py:484
  17.8 3.1 %collective-permute-start.3 = (bf16[1,176,128]{2,1,0:T(8,128)(2,1)S(1)}, bf16[1,176,128]{2,1,0:T(8,128)(2,1)S(1)}, u32[]{:S(2)}, u32[]{:S(2)}) collective-permute-start(bf16[1,176,128]{2,1,0:T(8,128)(2,1)S(1)} %pad_maximum_fusion.rest_1_.rest_3_), channel_id=1, source_target_pairs={{0,8},{1,9},{2,10},{3,11},{4,12},{5,13},{6,14},{7,15},{8,0},{9,1},... | collective-permute-start | bytes 135176 | tf_op jit(solution)/shard_map/ppermute | solution.py:484
  20.9 2.0 %collective-permute-done.3.rest_2_.rest_4_ = bf16[1,176,128]{2,1,0:T(8,128)(2,1)S(1)} collective-permute-done((bf16[1,176,128]{2,1,0:T(8,128)(2,1)S(1)}, bf16[1,176,128]{2,1,0:T(8,128)(2,1)S(1)}, u32[]{:S(2)}, u32[]{:S(2)}) %collective-permute-start.3) | collective-permute-done | bytes 45088 | tf_op jit(solution)/shard_map/ppermute | solution.py:484
  23.0 1.1 %copy-done.2 = bf16[32,5,16,128]{3,2,1,0:T(8,128)(2,1)S(1)} copy-done((bf16[32,5,16,128]{3,2,1,0:T(8,128)(2,1)S(1)}, bf16[32,5,16,128]{3,2,1,0:T(8,128)(2,1)}, u32[]{:S(2)}) %copy-start.2) | copy-done | bytes 655384
  24.1 10.5 %after.1 = (bf16[32,5,16,128]{3,2,1,0:T(8,128)(2,1)}, f32[32,64]{1,0:T(8,128)S(1)}) custom-call(s32[32]{0:T(128)S(1)} %copy-done.16, s32[1]{0:T(128)S(6)} %copy.21.pert_ids, s32[1]{0:T(128)} %bitcast.place, f32[16]{0:T(128)S(1)} %copy-done.19, f32[5]{0:T(128)S(1)} %copy-done.20, f32[5]{0:T(128)S(1)} %copy-done.17, f32[5,5]{1,0:T(8,128)S(1)} %copy-done.14, ...), custom_call_target="tpu_custom_call" | custom-call | tf_op jit(solution)/shard_map/after/pallas_call | solution.py:521
  34.6 1.2 %collective-permute-done.4 = f32[32,64]{1,0:T(8,128)S(1)} collective-permute-done((f32[32,64]{1,0:T(8,128)S(1)}, f32[32,64]{1,0:T(8,128)S(1)}, u32[]{:S(2)}, u32[]{:S(2)}) %collective-permute-start.4) | collective-permute-done | bytes 8224 | tf_op jit(solution)/shard_map/ppermute | solution.py:484
  35.8 1.9 %collective-permute-start.5 = (f32[32,64]{1,0:T(8,128)S(1)}, f32[32,64]{1,0:T(8,128)S(1)}, u32[]{:S(2)}, u32[]{:S(2)}) collective-permute-start(f32[32,64]{1,0:T(8,128)S(1)} %add.23), channel_id=1, source_target_pairs={{0,2},{1,3},{2,0},{3,1},{4,6},{5,7},{6,4},{7,5},{8,10},{9,11},{10,... | collective-permute-start | bytes 24584 | tf_op jit(solution)/shard_map/ppermute | solution.py:484
  37.7 1.9 %collective-permute-done.5 = f32[32,64]{1,0:T(8,128)S(1)} collective-permute-done((f32[32,64]{1,0:T(8,128)S(1)}, f32[32,64]{1,0:T(8,128)S(1)}, u32[]{:S(2)}, u32[]{:S(2)}) %collective-permute-start.5) | collective-permute-done | bytes 8224 | tf_op jit(solution)/shard_map/ppermute | solution.py:484
  39.6 1.9 %collective-permute-start.6 = (f32[32,64]{1,0:T(8,128)S(1)}, f32[32,64]{1,0:T(8,128)S(1)}, u32[]{:S(2)}, u32[]{:S(2)}) collective-permute-start(f32[32,64]{1,0:T(8,128)S(1)} %add.24), channel_id=1, source_target_pairs={{0,4},{1,5},{2,6},{3,7},{4,0},{5,1},{6,2},{7,3},{8,12},{9,13},{10,... | collective-permute-start | bytes 24584 | tf_op jit(solution)/shard_map/ppermute | solution.py:484
  41.5 1.8 %collective-permute-done.6 = f32[32,64]{1,0:T(8,128)S(1)} collective-permute-done((f32[32,64]{1,0:T(8,128)S(1)}, f32[32,64]{1,0:T(8,128)S(1)}, u32[]{:S(2)}, u32[]{:S(2)}) %collective-permute-start.6) | collective-permute-done | bytes 8224 | tf_op jit(solution)/shard_map/ppermute | solution.py:484
  43.3 3.0 %collective-permute-start.7 = (f32[32,64]{1,0:T(8,128)S(1)}, f32[32,64]{1,0:T(8,128)S(1)}, u32[]{:S(2)}, u32[]{:S(2)}) collective-permute-start(f32[32,64]{1,0:T(8,128)S(1)} %add.25), channel_id=1, source_target_pairs={{0,8},{1,9},{2,10},{3,11},{4,12},{5,13},{6,14},{7,15},{8,0},{9,1},... | collective-permute-start | bytes 24584 | tf_op jit(solution)/shard_map/ppermute | solution.py:484
  46.3 1.7 %collective-permute-done.7 = f32[32,64]{1,0:T(8,128)S(1)} collective-permute-done((f32[32,64]{1,0:T(8,128)S(1)}, f32[32,64]{1,0:T(8,128)S(1)}, u32[]{:S(2)}, u32[]{:S(2)}) %collective-permute-start.7) | collective-permute-done | bytes 8224 | tf_op jit(solution)/shard_map/ppermute | solution.py:484
  48.0 3.9 %fit.1 = (f32[2,64]{1,0:T(2,128)}, f32[560,32]{1,0:T(8,128)S(1)}, f32[2,32]{1,0:T(2,128)}) custom-call(s32[1]{0:T(128)} %bitcast.place, f32[32,64]{1,0:T(8,128)S(1)} %add.26.red_ref, f32[32,560]{1,0:T(8,128)S(1)} %copy-done.6, f32[32,560]{1,0:T(8,128)S(1)} %copy-done.5, f32[1,560]{1,0:T(1,128)S(1)} %copy-done.15), custom_call_target="tpu_custom_call" | custom-call | tf_op jit(solution)/shard_map/fit/pallas_call | solution.py:575
  51.9 0.8 %copy.20 = f32[560,32]{0,1:T(8,128)} copy(f32[560,32]{1,0:T(8,128)S(1)} %get-tuple-element.16) | data formatting | bytes 143360
  (49 shorter events, 1.3 us)
Async XLA Ops:
  0.6 0.7 %copy-start.18 = (f32[37]{0:T(128)S(1)}, f32[37]{0:T(128)}, u32[]{:S(2)}) copy-start(f32[37]{0:T(128)} %constant.33.clone.table) | copy-start | bytes 448
  0.6 0.7 %copy-start.17 = (f32[5]{0:T(128)S(1)}, f32[5]{0:T(128)}, u32[]{:S(2)}) copy-start(f32[5]{0:T(128)} %visc.3) | copy-start | bytes 64
  1.4 1.1 %copy-start = (bf16[32,5,16,128]{3,2,1,0:T(8,128)(2,1)S(1)}, bf16[32,5,16,128]{3,2,1,0:T(8,128)(2,1)}, u32[]{:S(2)}) copy-start(bf16[32,5,16,128]{3,2,1,0:T(8,128)(2,1)} %states.3) | copy-start | bytes 1966084
  2.5 0.8 %copy-start.3 = (f32[8,16,128]{2,1,0:T(8,128)S(1)}, f32[8,16,128]{2,1,0:T(8,128)}, u32[]{:S(2)}) copy-start(f32[8,16,128]{2,1,0:T(8,128)} %pert.3) | copy-start | bytes 196612
  6.1 16.8 %copy-start.1 = (bf16[32,5,16,128]{3,2,1,0:T(8,128)(2,1)S(1)}, bf16[32,5,16,128]{3,2,1,0:T(8,128)(2,1)}, u32[]{:S(2)}) copy-start(bf16[32,5,16,128]{3,2,1,0:T(8,128)(2,1)} %states.3) | copy-start | bytes 1966084
  7.7 1.4 %collective-permute-start = (bf16[1,112,128]{2,1,0:T(8,128)(2,1)S(1)}, bf16[1,112,128]{2,1,0:T(8,128)(2,1)S(1)}, u32[]{:S(2)}, u32[]{:S(2)}) collective-permute-start(bf16[1,112,128]{2,1,0:T(8,128)(2,1)S(1)} %before.1.own_ref), channel_id=1, source_target_pairs={{0,1},{1,0},{2,3},{3,2},{4,5},{5,4},{6,7},{7,6},{8,9},{9,8},{10,11... | collective-permute-start | bytes 86024 | tf_op jit(solution)/shard_map/ppermute | solution.py:484
  9.1 4.7 %collective-permute-start.1 = (bf16[1,80,128]{2,1,0:T(8,128)(2,1)S(1)}, bf16[1,80,128]{2,1,0:T(8,128)(2,1)S(1)}, u32[]{:S(2)}, u32[]{:S(2)}) collective-permute-start(bf16[1,80,128]{2,1,0:T(8,128)(2,1)S(1)} %pad_maximum_fusion.2), channel_id=1, source_target_pairs={{0,2},{1,3},{2,0},{3,1},{4,6},{5,7},{6,4},{7,5},{8,10},{9,11},{10,... | collective-permute-start | bytes 61448 | tf_op jit(solution)/shard_map/ppermute | solution.py:484
  13.8 9.1 %copy-start.4 = (f32[8,16,128]{2,1,0:T(8,128)S(1)}, f32[8,16,128]{2,1,0:T(8,128)}, u32[]{:S(2)}) copy-start(f32[8,16,128]{2,1,0:T(8,128)} %pert.3) | copy-start | bytes 196612
  13.8 3.9 %collective-permute-start.2 = (bf16[1,112,128]{2,1,0:T(8,128)(2,1)S(1)}, bf16[1,112,128]{2,1,0:T(8,128)(2,1)S(1)}, u32[]{:S(2)}, u32[]{:S(2)}) collective-permute-start(bf16[1,112,128]{2,1,0:T(8,128)(2,1)S(1)} %pad_maximum_fusion.1.rest_0_), channel_id=1, source_target_pairs={{0,4},{1,5},{2,6},{3,7},{4,0},{5,1},{6,2},{7,3},{8,12},{9,13},{10,... | collective-permute-start | bytes 86024 | tf_op jit(solution)/shard_map/ppermute | solution.py:484
  15.9 7.0 %copy-start.8 = (s32[16,128]{1,0:T(8,128)S(1)}, s32[16,128]{1,0:T(8,128)}, u32[]{:S(2)}) copy-start(s32[16,128]{1,0:T(8,128)} %ids_ref.3) | copy-start | bytes 24580
  15.9 7.0 %copy-start.10 = (f32[16,128]{1,0:T(8,128)S(1)}, f32[16,128]{1,0:T(8,128)}, u32[]{:S(2)}) copy-start(f32[16,128]{1,0:T(8,128)} %speed_ref.3) | copy-start | bytes 24580
  15.9 7.0 %copy-start.12 = (f32[16,128]{1,0:T(8,128)S(1)}, f32[16,128]{1,0:T(8,128)}, u32[]{:S(2)}) copy-start(f32[16,128]{1,0:T(8,128)} %force_ref.3) | copy-start | bytes 24580
  17.7 5.2 %copy-start.14 = (f32[5,5]{1,0:T(8,128)S(1)}, f32[5,5]{1,0:T(8,128)}, u32[]{:S(2)}) copy-start(f32[5,5]{1,0:T(8,128)} %coup.3) | copy-start | bytes 304
  17.8 5.2 %copy-start.19 = (f32[16]{0:T(128)S(1)}, f32[16]{0:T(128)}, u32[]{:S(2)}) copy-start(f32[16]{0:T(128)} %kern.1) | copy-start | bytes 196
  17.8 5.2 %copy-start.20 = (f32[5]{0:T(128)S(1)}, f32[5]{0:T(128)}, u32[]{:S(2)}) copy-start(f32[5]{0:T(128)} %gain.1) | copy-start | bytes 64
  17.8 5.1 %collective-permute-start.3 = (bf16[1,176,128]{2,1,0:T(8,128)(2,1)S(1)}, bf16[1,176,128]{2,1,0:T(8,128)(2,1)S(1)}, u32[]{:S(2)}, u32[]{:S(2)}) collective-permute-start(bf16[1,176,128]{2,1,0:T(8,128)(2,1)S(1)} %pad_maximum_fusion.rest_1_.rest_3_), channel_id=1, source_target_pairs={{0,8},{1,9},{2,10},{3,11},{4,12},{5,13},{6,14},{7,15},{8,0},{9,1},... | collective-permute-start | bytes 135176 | tf_op jit(solution)/shard_map/ppermute | solution.py:484
  23.0 1.1 %copy-start.2 = (bf16[32,5,16,128]{3,2,1,0:T(8,128)(2,1)S(1)}, bf16[32,5,16,128]{3,2,1,0:T(8,128)(2,1)}, u32[]{:S(2)}) copy-start(bf16[32,5,16,128]{3,2,1,0:T(8,128)(2,1)} %basis.1) | copy-start | bytes 1966084
  34.6 1.2 %collective-permute-start.4 = (f32[32,64]{1,0:T(8,128)S(1)}, f32[32,64]{1,0:T(8,128)S(1)}, u32[]{:S(2)}, u32[]{:S(2)}) collective-permute-start(f32[32,64]{1,0:T(8,128)S(1)} %get-tuple-element.10), channel_id=1, source_target_pairs={{0,1},{1,0},{2,3},{3,2},{4,5},{5,4},{6,7},{7,6},{8,9},{9,8},{10,11... | collective-permute-start | bytes 24584 | tf_op jit(solution)/shard_map/ppermute | solution.py:484
  35.8 12.3 %copy-start.6 = (f32[32,560]{1,0:T(8,128)S(1)}, f32[32,560]{1,0:T(8,128)}, u32[]{:S(2)}) copy-start(f32[32,560]{1,0:T(8,128)} %constant.34.clone.first_ref) | copy-start | bytes 215044
  35.8 12.3 %copy-start.5 = (f32[32,560]{1,0:T(8,128)S(1)}, f32[32,560]{1,0:T(8,128)}, u32[]{:S(2)}) copy-start(f32[32,560]{1,0:T(8,128)} %constant.35.clone.second_ref) | copy-start | bytes 215044
  35.8 3.8 %collective-permute-start.5 = (f32[32,64]{1,0:T(8,128)S(1)}, f32[32,64]{1,0:T(8,128)S(1)}, u32[]{:S(2)}, u32[]{:S(2)}) collective-permute-start(f32[32,64]{1,0:T(8,128)S(1)} %add.23), channel_id=1, source_target_pairs={{0,2},{1,3},{2,0},{3,1},{4,6},{5,7},{6,4},{7,5},{8,10},{9,11},{10,... | collective-permute-start | bytes 24584 | tf_op jit(solution)/shard_map/ppermute | solution.py:484
  39.6 3.7 %collective-permute-start.6 = (f32[32,64]{1,0:T(8,128)S(1)}, f32[32,64]{1,0:T(8,128)S(1)}, u32[]{:S(2)}, u32[]{:S(2)}) collective-permute-start(f32[32,64]{1,0:T(8,128)S(1)} %add.24), channel_id=1, source_target_pairs={{0,4},{1,5},{2,6},{3,7},{4,0},{5,1},{6,2},{7,3},{8,12},{9,13},{10,... | collective-permute-start | bytes 24584 | tf_op jit(solution)/shard_map/ppermute | solution.py:484
  43.3 4.7 %copy-start.15 = (f32[1,560]{1,0:T(1,128)S(1)}, f32[1,560]{1,0:T(1,128)}, u32[]{:S(2)}) copy-start(f32[1,560]{1,0:T(1,128)} %constant.36.clone.lin_ref) | copy-start | bytes 6724
  43.3 4.7 %collective-permute-start.7 = (f32[32,64]{1,0:T(8,128)S(1)}, f32[32,64]{1,0:T(8,128)S(1)}, u32[]{:S(2)}, u32[]{:S(2)}) collective-permute-start(f32[32,64]{1,0:T(8,128)S(1)} %add.25), channel_id=1, source_target_pairs={{0,8},{1,9},{2,10},{3,11},{4,12},{5,13},{6,14},{7,15},{8,0},{9,1},... | collective-permute-start | bytes 24584 | tf_op jit(solution)/shard_map/ppermute | solution.py:484
  (5 other events, 3.5 us)

commit v2 on v1

--- a/solution.py
+++ b/solution.py
@@ -18,14 +18,19 @@
 PERIOD = 37
 TIME_STEP = 0.2
 RIDGE_FACTOR = 1.0
+UNROLL = 4
 CHUNK = 32
 BLOB = 16
+COORD = 16
 EDGE = 48
-ROWS = BLOB + 2 * EDGE
+ROWS = BLOB + COORD + 2 * EDGE
+RIGHT = slice(BLOB + COORD, BLOB + COORD + EDGE)
+LEFT = slice(BLOB + COORD + EDGE, ROWS)
 
 HIGH = lax.Precision.HIGHEST
 NT = (((1,), (1,)), ((), ()))
 VMEM = pl.BlockSpec(memory_space=pltpu.VMEM)
+HBM = pl.BlockSpec(memory_space=pltpu.HBM)
 SMEM = pl.BlockSpec(memory_space=pltpu.SMEM)
 
 
@@ -58,9 +63,52 @@
     return iota((8, LANES), 1) % 4
 
 
-def before_kernel(
-    times, pert_ids, visc, coup, table, states, pert, ids_ref, speed_ref, force_ref, out, fields
-):
+def flat(ref, first, count):
+    parts = [ref[pl.ds(first, count), v].reshape(count * NX, LANES) for v in range(NV)]
+    return jnp.concatenate(parts, axis=1)
+
+
+def project(rows, modes_flat):
+    width = modes_flat.shape[0]
+    size = rows.shape[0]
+    pairs = lax.dot_general(rows, modes_flat, NT, preferred_element_type=F32)
+    diagonal = iota((size, width), 0) % NX == iota((size, width), 1) % NX
+    pairs = jnp.where(diagonal, pairs, 0.0)
+    pairs = jnp.sum(pairs.reshape(size // NX, NX, width), axis=1)
+    high, low = split(pairs)
+    modes = width // NX
+    mode_of = iota((width, LANES), 0) // NX
+    column = iota((width, LANES), 1)
+    total = jnp.zeros((8, LANES), F32)
+    for j in range(CHUNK // 8):
+        pick = jnp.where(mode_of + j * modes == column, 1.0, 0.0).astype(BF16)
+        both = jnp.concatenate([high[8 * j : 8 * j + 8], low[8 * j : 8 * j + 8]], axis=0)
+        both = jnp.dot(both.astype(BF16), pick, preferred_element_type=F32)
+        total += both[:8] + both[8:]
+    return total
+
+
+def unpack(ref, modes):
+    rows = []
+    for chunk in range(ref.shape[0]):
+        tile = ref[chunk]
+        rows += [tile[:, j * modes : (j + 1) * modes] for j in range(CHUNK // 8)]
+    return jnp.concatenate(rows, axis=0)
+
+
+def before_kernel(*refs):
+    count = 11
+    sources, out, targets = refs[:count], refs[count], refs[count + 1 : 2 * count + 1]
+    fields, sems = refs[2 * count + 1 :]
+    copies = [
+        pltpu.make_async_copy(source, target, sems.at[i])
+        for i, (source, target) in enumerate(zip(sources, targets))
+    ]
+    for copy in copies:
+        copy.start()
+    times, pert_ids, visc, coup, table, pert, ids_ref, speed_ref, force_ref, states, basis = targets
+    for copy in copies[:-2]:
+        copy.wait()
     chunks = out.shape[0]
     speed = speed_ref[...]
     force = force_ref[...]
@@ -122,6 +170,9 @@
     part_of_lane = iota((size, LANES), 1) % 4
     to_start = jnp.where(snap_of_row & (part_of_lane < 2), scale, 0.0)
     to_rate = jnp.where(snap_of_row & (part_of_lane >= 2), scale, 0.0)
+    copies[-2].wait()
+    copies[-1].wait()
+    flat_basis = flat(basis, 0, basis.shape[0])
 
     def chunk_step(chunk, carry):
         first = chunk * CHUNK
@@ -168,7 +219,8 @@
         )
         right = [jnp.where(c8 < 2, t[:8], roll(t[8:], 2, 1)) for t in edges]
         left = [jnp.where(c8 >= 2, t[:8], roll(t[8:], -2, 1)) for t in edges]
-        rows = [packed, p_edges] + right + [params_right] + left + [params_left]
+        coords = split(project(flat(states, first, CHUNK), flat_basis))
+        rows = [packed, p_edges, *coords, *right, params_right, *left, params_left]
         out[chunk] = jnp.concatenate(rows, axis=0).astype(BF16)
         return carry
 
@@ -179,7 +231,6 @@
 
 
 def after_kernel(
-    carries,
     times,
     pert_ids,
     place,
@@ -189,21 +240,35 @@
     coup,
     table,
     states,
-    basis,
+    basis_hbm,
     pert,
     ids_ref,
     speed_ref,
     force_ref,
     own_ref,
     near_ref,
-    *rest,
+    far_ref,
+    last_ref,
+    deriv,
+    partial,
+    coords,
+    mixed,
+    raw,
+    cyc0,
+    grooves,
+    halo0,
+    halo1,
+    east_coef,
+    west_coef,
+    basis,
+    sem,
 ):
-    carry_refs = rest[:carries]
-    low_ref, high_ref, deriv, partial, mixed, raw, cyc0, cyc1, grooves, halo0, halo1 = rest[carries:]
+    fetch = pltpu.make_async_copy(basis_hbm, basis, sem)
+    fetch.start()
     chunks = own_ref.shape[0]
     passages = kern.shape[0]
-    half = passages // 2
     me = place[0]
+    base = me - lax.rem(me, 2)
     odd = me % 2 == 1
     speed = speed_ref[...]
     force = force_ref[...]
@@ -227,6 +292,30 @@
     wide = 4 * NRING * NX
     same_x = iota((size, wide), 0) % NX == iota((size, wide), 1) % NX
 
+    for v in range(NV):
+        east_coef[v] = visc[v] - half_speed
+        west_coef[v] = visc[v] + half_speed
+    deep = NV * NX
+    col = iota((NX, 3 * deep), 1)
+    col_var, col_x = col % deep // NX, col % NX
+    row_x = iota((NX, 3 * deep), 0)
+    beside = jnp.abs(row_x - col_x) == 1
+    blocks = []
+    for v in range(NV):
+        weight = jnp.zeros((NX, 3 * deep), F32)
+        for other in range(NV):
+            value = coup[v, other] - (4.0 * visc[v] if other == v else 0.0)
+            weight = jnp.where((col_var == other) & (row_x == col_x), value, weight)
+        blocks.append(jnp.where((col_var == v) & beside, visc[v], weight))
+    high, low = split(jnp.concatenate(blocks, axis=0))
+    col = iota((deep, 3 * deep), 1)
+    mixer = jnp.where((col < deep) | (col >= 2 * deep), high, low).astype(BF16)
+
+    def flat_basis():
+        if chunks == 1:
+            fetch.wait()
+        return flat(basis, 0, basis.shape[0])
+
     def unpack_right(t):
         return jnp.concatenate([t, roll(t, -2, 1)], axis=0)
 
@@ -235,13 +324,17 @@
 
     def chunk_step(chunk, carry):
         first = chunk * CHUNK
-        raw[: half * BLOB, :] = low_ref[chunk, : half * BLOB, :].astype(F32)
-        raw[half * BLOB :, :] = high_ref[chunk, : half * BLOB, :].astype(F32)
-        mixed[...] = jnp.dot(raw[...].astype(BF16), mix, preferred_element_type=F32)
+        final = last_ref[chunk].astype(F32)
+        raw[...] = final[: passages * BLOB]
+        mixed[...] = jnp.dot(
+            final[: passages * BLOB].astype(BF16), mix, preferred_element_type=F32
+        )
+        summed = final[passages * BLOB : passages * BLOB + COORD]
+        coords[chunk] = summed[:8] + summed[8:]
 
         def slot(offset):
             other = lax.rem(me + offset + passages, passages)
-            return pl.multiple_of(jnp.bitwise_xor(me, other) * BLOB, BLOB)
+            return pl.multiple_of(jnp.bitwise_xor(base, other) * BLOB, BLOB)
 
         def load(offset, carry):
             cyc0[pl.ds(pl.multiple_of(offset * 8, 8), 8), :] = mixed[pl.ds(slot(offset), 8), :LANES]
@@ -320,15 +413,11 @@
                 preferred_element_type=F32,
             )
 
-        far = carry_refs[-1][chunk, -EDGE:, :].astype(F32)
-        for index in range(carries - 2, -1, -1):
-            bit = jnp.bitwise_and(jnp.right_shift(me, index + 1), 1)
-            arrived = (bit == 1) != odd
-            far = jnp.where(arrived, carry_refs[index][chunk, -EDGE:, :].astype(F32), far)
         near = near_ref[chunk].astype(F32)
         own = own_ref[chunk].astype(F32)
-        west = jnp.where(odd, near[BLOB : BLOB + EDGE], far)
-        east = jnp.where(odd, far, near[BLOB + EDGE :])
+        far = far_ref[chunk].astype(F32)
+        west = jnp.where(odd, near[RIGHT], far)
+        east = jnp.where(odd, far, near[LEFT])
 
         def param(side, index):
             t = side[40:48]
@@ -351,9 +440,9 @@
         for v in range(NV):
             at = slice(8 * v, 8 * v + 8)
             halo.append(jnp.where(c16 < 2, unpack_right(west[at]), unpack_left(east[at])))
-            mine = slice(BLOB + 8 * v, BLOB + 8 * v + 8)
-            mine_left = slice(BLOB + EDGE + 8 * v, BLOB + EDGE + 8 * v + 8)
-            ours.append(jnp.where(c16 < 2, unpack_right(own[mine]), unpack_left(own[mine_left])))
+            ours.append(
+                jnp.where(c16 < 2, unpack_right(own[RIGHT][at]), unpack_left(own[LEFT][at]))
+            )
         for v in range(NV):
             h = halo[v]
             e = roll(jnp.where(c16 == 3, h, ours[v]), -1, 1)
@@ -365,94 +454,110 @@
             halo0[v] = h
             halo1[v] = h + TIME_STEP * rate
 
-        def flux(u, halos, source, spread):
+        def flux(u, mixed_u, halos, source, spread):
             result = []
             for v in range(NV):
                 h = roll(halos[v], spread, 1)
                 e = roll(jnp.where(lane == 0, h, u[v]), -1, 1)
                 w = roll(jnp.where(lane == LANES - 1, h, u[v]), 1, 1)
-                rate = visc[v] * (e + w + north_south(u[v])) - half_speed * (e - w)
-                rate = rate + (coup[v, v] - 4.0 * visc[v] - damping) * u[v]
-                for other in range(NV):
-                    if other != v:
-                        rate = rate + coup[v, other] * u[other]
-                result.append(rate + gain[v] * source[0] + source[1])
+                rate = mixed_u[NX * v : NX * v + NX] + east_coef[v] * e + west_coef[v] * w
+                result.append(rate - damping * u[v] + gain[v] * source[0] + source[1])
             return result
 
-        def snap(k, carry):
+        def snap(k):
+            half = states[first + k].reshape(NV * NX, LANES)
             u = [states[first + k, v].astype(F32) for v in range(NV)]
             drive = table[lax.rem(times[first + k], PERIOD)] * force
             at = pl.multiple_of(k * NX, NX)
-            spread = -(4 * k + 2) if isinstance(k, int) else 2 * LANES - 4 * k - 2
-            rate0 = flux(u, halo0, (grooves[0, pl.ds(at, NX), :], drive), spread)
+            spread = 2 * LANES - 4 * k - 2
+            mixed0 = jnp.dot(
+                mixer[:, : 2 * NV * NX],
+                jnp.concatenate([half, half], axis=0),
+                preferred_element_type=F32,
+            )
+            rate0 = flux(u, mixed0, halo0, (grooves[0, pl.ds(at, NX), :], drive), spread)
             middle = [u[v] + TIME_STEP * rate0[v] for v in range(NV)]
-            rate1 = flux(middle, halo1, (grooves[1, pl.ds(at, NX), :], drive), spread)
+            stack = jnp.concatenate(middle, axis=0)
+            high = stack.astype(BF16)
+            low = (stack - high.astype(F32)).astype(BF16)
+            mixed1 = jnp.dot(
+                mixer, jnp.concatenate([high, high, low], axis=0), preferred_element_type=F32
+            )
+            rate1 = flux(middle, mixed1, halo1, (grooves[1, pl.ds(at, NX), :], drive), spread)
             for v in range(NV):
                 deriv[first + k, v] = (0.5 * (rate0[v] + rate1[v])).astype(BF16)
+
+        def snaps(step, carry):
+            for i in range(UNROLL):
+                snap(step * UNROLL + i)
             return carry
 
-        if chunks == 1:
-            for k in range(CHUNK):
-                snap(k, 0)
-        else:
-            lax.fori_loop(0, CHUNK, snap, 0)
-
-        modes = basis.shape[0]
-        flat_basis = jnp.concatenate(
-            [basis[:, v].reshape(modes * NX, LANES) for v in range(NV)], axis=1
-        )
-        diagonal = (
-            iota((size, modes * NX), 0) % NX == iota((size, modes * NX), 1) % NX
-        )
-        mode_of = iota((modes * NX, 2 * modes), 0) // NX
-        column = iota((modes * NX, 2 * modes), 1)
-        total = jnp.zeros((CHUNK, 2 * modes), F32)
-        for part, source in ((0, states), (1, deriv)):
-            rows = jnp.concatenate(
-                [source[pl.ds(first, CHUNK), v].reshape(size, LANES) for v in range(NV)], axis=1
-            )
-            pairs = lax.dot_general(rows, flat_basis, NT, preferred_element_type=F32)
-            pairs = jnp.where(diagonal, pairs, 0.0)
-            pairs = jnp.sum(pairs.reshape(CHUNK, NX, modes * NX), axis=1)
-            gather = jnp.where(mode_of + part * modes == column, 1.0, 0.0)
-            total += jnp.dot(pairs, gather, precision=HIGH, preferred_element_type=F32)
-        partial[pl.ds(pl.multiple_of(first, CHUNK), CHUNK), :] = total
+        lax.fori_loop(0, CHUNK // UNROLL, snaps, 0)
+        partial[chunk] = project(flat(deriv, first, CHUNK), flat_basis())
         return carry
 
     if chunks == 1:
         chunk_step(0, 0)
     else:
+        fetch.wait()
         lax.fori_loop(0, chunks, chunk_step, 0)
 
 
-def fit_kernel(ridge, place, red_ref, first_ref, second_ref, lin_ref, reduced, operator, fitted, full):
-    snaps, modes = red_ref.shape[0], red_ref.shape[1] // 2
-    red = red_ref[...]
-    coords = red[:, :modes]
-    rates = red[:, modes:]
-    dot = functools.partial(
-        lax.dot_general, precision=HIGH, preferred_element_type=F32
-    )
-    gram = dot(coords, coords, NT)
+def eliminate(system, columns):
+    row = iota(system.shape, 0)
+    for j in columns:
+        pivot = system[j : j + 1, :] / system[j : j + 1, j : j + 1]
+        factor = jnp.where(row == j, 0.0, jnp.broadcast_to(system[:, j : j + 1], system.shape))
+        system = jnp.where(row == j, pivot, system - factor * pivot)
+    return system
+
+
+highest = functools.partial(lax.dot_general, precision=HIGH, preferred_element_type=F32)
+NN = (((1,), (0,)), ((), ()))
+
+
+def system_kernel(ridge, modes, coords_ref, kernel_ref, system_ref):
+    coords = unpack(coords_ref, modes)
+    snaps = coords.shape[0]
+    gram = highest(coords, coords, NT)
     squares = coords * coords
-    kernel = gram + 0.5 * (gram * gram + dot(squares, squares, NT))
-    eye = jnp.where(iota((snaps, snaps), 0) == iota((snaps, snaps), 1), ridge, 0.0)
-    system = jnp.concatenate([kernel + eye, rates], axis=1)
-    width = snaps + modes
-    row = iota((snaps, width), 0)
-    for j in range(snaps):
-        pivot = system[j : j + 1, :] / system[j : j + 1, j : j + 1]
-        factor = jnp.where(row == j, 0.0, jnp.broadcast_to(system[:, j : j + 1], (snaps, width)))
-        system = jnp.where(row == j, pivot, system - factor * pivot)
-    solved = system[:, snaps:]
-    one = (((1,), (0,)), ((), ()))
-    design = dot(coords, first_ref[...], one) * (dot(coords, second_ref[...], one) + lin_ref[...])
-    operator[...] = dot(design, solved, (((0,), (0,)), ((), ())))
-    full[...] = dot(kernel, solved, one)
+    kernel = gram + 0.5 * (gram * gram + highest(squares, squares, NT))
+    kernel_ref[...] = kernel
+    same = iota((snaps, snaps), 0) == iota((snaps, snaps), 1)
+    eye = jnp.where(same, 1.0, 0.0)
+    system = jnp.concatenate([kernel + ridge * eye, eye], axis=1)
+    system_ref[...] = eliminate(system, range(snaps * 3 // 8))
+
+
+def invert_kernel(modes, system_ref, inverse_ref):
+    snaps = system_ref.shape[0]
+    system = eliminate(system_ref[...], range(snaps * 3 // 8, snaps))
+    inverse_ref[...] = system[:, snaps:]
+
+
+def weight_kernel(
+    coords_ref, kernel_ref, inverse_ref, first_ref, second_ref, lin_ref, weights, fit
+):
+    coords = unpack(coords_ref, first_ref.shape[0])
+    design = highest(coords, first_ref[...], NN)
+    design = design * (highest(coords, second_ref[...], NN) + lin_ref[...])
+    weights[...] = highest(inverse_ref[...], design, NN)
+    fit[...] = highest(kernel_ref[...], inverse_ref[...], NN)
+
+
+def fit_kernel(
+    place, rates_ref, coords_ref, weights, fit, reduced, operator, fitted, full, red
+):
+    modes = operator.shape[0]
+    rates = unpack(rates_ref, modes)
+    operator[...] = highest(rates, weights[...], (((0,), (0,)), ((), ())))
+    full[...] = highest(fit[...], rates, NN)
+    red[...] = jnp.concatenate([unpack(coords_ref, modes), rates], axis=1)
     each = fitted.shape[0]
     for i in range(each):
-        fitted[i : i + 1, :] = full[pl.ds(place[0] * each + i, 1), :]
-        reduced[i : i + 1, :] = red_ref[pl.ds(place[0] * each + i, 1), :]
+        at = pl.ds(place[0] * each + i, 1)
+        fitted[i : i + 1, :] = full[at, :]
+        reduced[i : i + 1, :] = red[at, :]
 
 
 def body(
@@ -483,59 +588,83 @@
         pairs = [(i, i ^ mask) for i in range(passages)]
         return lax.ppermute(value, "passage", pairs)
 
-    first = pl.pallas_call(
-        before_kernel,
-        out_shape=jax.ShapeDtypeStruct((chunks, ROWS, LANES), BF16),
-        in_specs=[SMEM] * 5 + [VMEM] * 5,
-        out_specs=VMEM,
-        scratch_shapes=[pltpu.VMEM((3 * CHUNK * NX, LANES), BF16)],
-        compiler_params=pltpu.CompilerParams(vmem_limit_bytes=40 * 2**20),
-        name="before",
-    )(
+    def swap_chip(value, mask):
+        return swap(value, mask + 1)
+
+    def add_pieces(one, two):
+        total = one[:, :8].astype(F32) + one[:, 8:].astype(F32)
+        total += two[:, :8].astype(F32) + two[:, 8:].astype(F32)
+        high = lax.reduce_precision(total, 8, 7)
+        return jnp.concatenate([high, total - high], axis=1).astype(BF16)
+
+    operands = (
         snapshot_times,
         pert_ids,
         viscosity,
         coupling,
         table,
-        states,
         pert_table,
         cycle_ids,
         speed,
         force_amp,
+        states,
+        basis,
     )
+    first = pl.pallas_call(
+        before_kernel,
+        out_shape=jax.ShapeDtypeStruct((chunks, ROWS, LANES), BF16),
+        in_specs=[HBM] * len(operands),
+        out_specs=VMEM,
+        scratch_shapes=[pltpu.SMEM(x.shape, x.dtype) for x in operands[:5]]
+        + [pltpu.VMEM(x.shape, x.dtype) for x in operands[5:]]
+        + [
+            pltpu.VMEM((3 * CHUNK * NX, LANES), BF16),
+            pltpu.SemaphoreType.DMA((len(operands),)),
+        ],
+        compiler_params=pltpu.CompilerParams(vmem_limit_bytes=60 * 2**20),
+        name="before",
+    )(*operands)
     near = swap(first, 1)
-    group = jnp.concatenate([first[:, :BLOB], near[:, :BLOB]], axis=1)
-    odd = position % 2
-    carry = lax.dynamic_slice_in_dim(near, BLOB + EDGE * odd, EDGE, axis=1)
-    carries = []
+    odd = position % 2 == 1
+    low, high = jnp.where(odd, near, first), jnp.where(odd, first, near)
+    group = jnp.concatenate([low[:, :BLOB], high[:, :BLOB]], axis=1)
+    coords = add_pieces(first[:, BLOB : BLOB + COORD], near[:, BLOB : BLOB + COORD])
+    right, left = high[:, RIGHT], low[:, LEFT]
+    far_right, far_left = [], []
     for r in range(1, rounds):
-        message = jnp.concatenate([group, carry], axis=1)
-        if r > 1:
-            carries.append(message)
-        got = swap(message, 1 << r)
-        carry = got[:, -EDGE:]
-        if r < rounds - 1:
-            group = jnp.concatenate([group, got[:, :-EDGE]], axis=1)
-    carries.append(got)
-
-    derivative, partial = pl.pallas_call(
-        functools.partial(after_kernel, len(carries)),
-        out_shape=(
-            jax.ShapeDtypeStruct(states.shape, BF16),
-            jax.ShapeDtypeStruct((snaps, 2 * modes), F32),
-        ),
-        in_specs=[SMEM] * 8 + [VMEM] * (10 + len(carries)),
-        out_specs=(VMEM, VMEM),
+        got = swap_chip(jnp.concatenate([group, coords, right, left], axis=1), 1 << r)
+        rows = group.shape[1]
+        group = jnp.concatenate([group, got[:, :rows]], axis=1)
+        coords = add_pieces(coords, got[:, rows : rows + COORD])
+        right, left = got[:, rows + COORD : rows + COORD + EDGE], got[:, rows + COORD + EDGE :]
+        far_right.append(right)
+        far_left.append(left)
+    for r in range(rounds - 2, 0, -1):
+        bit = (position >> r) & 1
+        right = jnp.where(bit == 1, far_right[r - 1], right)
+        left = jnp.where(bit == 0, far_left[r - 1], left)
+    far = jnp.where(odd, left, right)
+    last = jnp.concatenate([group, coords], axis=1)
+
+    tile = jax.ShapeDtypeStruct((chunks, 8, LANES), F32)
+    derivative, partial, coords = pl.pallas_call(
+        after_kernel,
+        out_shape=(jax.ShapeDtypeStruct(states.shape, BF16), tile, tile),
+        in_specs=[SMEM] * 8 + [VMEM, HBM] + [VMEM] * 8,
+        out_specs=(VMEM, VMEM, VMEM),
         scratch_shapes=[
             pltpu.VMEM((passages * BLOB, 6 * LANES), F32),
             pltpu.VMEM((passages * BLOB, LANES), F32),
             pltpu.VMEM((passages * 8, LANES), F32),
-            pltpu.VMEM((passages * 8, LANES), F32),
             pltpu.VMEM((2, CHUNK * NX, LANES), F32),
             pltpu.VMEM((NV, NX, LANES), F32),
             pltpu.VMEM((NV, NX, LANES), F32),
+            pltpu.VMEM((NV, NX, LANES), F32),
+            pltpu.VMEM((NV, NX, LANES), F32),
+            pltpu.VMEM(basis.shape, BF16),
+            pltpu.SemaphoreType.DMA,
         ],
-        compiler_params=pltpu.CompilerParams(vmem_limit_bytes=48 * 2**20),
+        compiler_params=pltpu.CompilerParams(vmem_limit_bytes=32 * 2**20),
         name="after",
     )(
         snapshot_times,
@@ -554,13 +683,9 @@
         force_amp,
         first,
         near,
-        *carries,
-        message,
-        got,
+        far,
+        last,
     )
-    total = partial
-    for r in range(rounds):
-        total = total + swap(total, 1 << r)
 
     upper_first, upper_second = np.triu_indices(modes)
     features = modes + len(upper_first)
@@ -571,21 +696,62 @@
     linear[0, :modes] = 1.0
     pick_first[upper_first, modes + np.arange(len(upper_first))] = 1.0
     pick_second[upper_second, modes + np.arange(len(upper_first))] = 1.0
+
+    def small(kernel, name, outs, *args):
+        return pl.pallas_call(
+            kernel,
+            out_shape=tuple(jax.ShapeDtypeStruct(shape, F32) for shape in outs),
+            in_specs=[VMEM] * len(args),
+            out_specs=tuple(VMEM for _ in outs),
+            cost_estimate=pl.CostEstimate(flops=10**8, bytes_accessed=2**20, transcendentals=0),
+            compiler_params=pltpu.CompilerParams(vmem_limit_bytes=16 * 2**20),
+            name=name,
+        )(*args)
+
+    total = partial + swap(partial, 1)
+    kernel, system = small(
+        functools.partial(system_kernel, RIDGE_FACTOR * snaps, modes),
+        "system",
+        [(snaps, snaps), (snaps, 2 * snaps)],
+        coords,
+    )
+    for r in range(1, rounds):
+        got = swap_chip(total, 1 << r)
+        if r == 1:
+            total, kernel, system = lax.optimization_barrier((total + got, kernel, system))
+            (inverse,) = small(
+                functools.partial(invert_kernel, modes), "invert", [(snaps, snaps)], system
+            )
+        elif r == 2:
+            total, inverse = lax.optimization_barrier((total + got, inverse))
+            weights, fit = small(
+                weight_kernel,
+                "weights",
+                [(snaps, features), (snaps, snaps)],
+                coords,
+                kernel,
+                inverse,
+                jnp.asarray(pick_first),
+                jnp.asarray(pick_second),
+                jnp.asarray(linear),
+            )
+        else:
+            total = total + got
     each = snaps // passages
     reduced, operator, fitted = pl.pallas_call(
-        functools.partial(fit_kernel, RIDGE_FACTOR * snaps),
+        fit_kernel,
         out_shape=(
             jax.ShapeDtypeStruct((each, 2 * modes), F32),
-            jax.ShapeDtypeStruct((features, modes), F32),
+            jax.ShapeDtypeStruct((modes, features), F32),
             jax.ShapeDtypeStruct((each, modes), F32),
         ),
         in_specs=[SMEM] + [VMEM] * 4,
         out_specs=(VMEM, VMEM, VMEM),
-        scratch_shapes=[pltpu.VMEM((snaps, modes), F32)],
+        scratch_shapes=[pltpu.VMEM((snaps, modes), F32), pltpu.VMEM((snaps, 2 * modes), F32)],
         compiler_params=pltpu.CompilerParams(vmem_limit_bytes=16 * 2**20),
         name="fit",
-    )(place, total, jnp.asarray(pick_first), jnp.asarray(pick_second), jnp.asarray(linear))
-    return derivative, reduced, operator, fitted
+    )(place, total, coords, weights, fit)
+    return derivative, reduced, operator.T, fitted
 
 
 def solution(mesh):

time: 53.1 us -> 45.3 us (0.85)
  local copies, waits for them, and re-layouts: 6.62 us -> 0.75 us
  waiting for transfers between devices: 13.1 us -> 8.4 us
  other arithmetic: 0.03 us -> 2.3 us
  starting transfers between devices: 15.4 us -> 16 us
    unnamed x43 -> x38, local copies, waits for them, and re-layouts: 6.61 us -> 0.73 us
    ppermute x8, waiting for transfers between devices: 13.1 us -> 8.4 us  [swap(): return lax.ppermute(value, 'passage', pairs)]
    pallas_call x2 -> x5, Pallas kernels: 14.4 us -> 12.2 us  [the longest x1 7.76 us: body(): pl.pallas_call(after_kernel, out_shape=(jax.ShapeDtypeStruct(states.shape...]
    pallas_call x1, Pallas kernels: 1.66 us -> 3.82 us  [body(): pl.pallas_call(before_kernel, out_shape=jax.ShapeDtypeStruct((chunks, ROW...]
    unnamed x0 -> x7, other arithmetic: none -> 1.5 us
    select_n x0 -> x2, other arithmetic: none -> 0.78 us  [the longest x1 0.77 us: body(): low, high = (jnp.where(odd, near, first), jnp.where(odd, first, near))]
    ppermute x8, starting transfers between devices: 15.4 us -> 16 us  [swap(): return lax.ppermute(value, 'passage', pairs)]
  transfers between devices with their start and end apart: 8 -> 8, of which waited for: 8 -> 8; matrix products, arithmetic and copies ran while one was open for 0% -> 0% of each run, Pallas kernels for 0% -> 8%
where the time goes in v2:
time: 45.3 us; the launch traced here: 45 us
  Pallas kernels  16 us (35%)
  starting transfers between devices  16 us (35%)
  waiting for transfers between devices  8.4 us (19%)
  other arithmetic  2.3 us (5%)
  between operations  1.51 us (3%)
  local copies, waits for them, and re-layouts  0.75 us (2%)
    ppermute x8, starting transfers between devices, swap(): return lax.ppermute(value, 'passage', pairs)  16 us
    ppermute x8, waiting for transfers between devices, swap(): return lax.ppermute(value, 'passage', pairs)  8.4 us
    pallas_call x1, Pallas kernels, body(): pl.pallas_call(after_kernel, out_shape=(jax.ShapeDtypeStruct(states.shape...  7.76 us
    pallas_call x1, Pallas kernels, body(): pl.pallas_call(before_kernel, out_shape=jax.ShapeDtypeStruct((chunks, ROW...  3.82 us
    pallas_call x3, Pallas kernels, small(): pl.pallas_call(kernel, out_shape=tuple((jax.ShapeDtypeStruct(shape, F32)...  3.45 us
    unnamed x7, other arithmetic  1.5 us
    pallas_call x1, Pallas kernels, body(): pl.pallas_call(fit_kernel, out_shape=(jax.ShapeDtypeStruct((each, 2 * mod...  1 us
  transfers between devices with their start and end apart: 8, of which 8 were waited for; matrix products, arithmetic and copies ran while one was open for 0% of the time, Pallas kernels for 8%

profile of v2, /device:TPU:0, one launch (start us, length us, event | category | flops | bytes accessed | tf_op | source)
XLA Modules:
  0.0 45.0 jit_solution(11969342887100330223)
XLA Ops:
  1.3 3.8 %before.1.own_ref = bf16[1,128,128]{2,1,0:T(8,128)(2,1)} custom-call(s32[32]{0:T(128)} %times.1, s32[1]{0:T(128)S(6)} %copy.42.refs_1_.pert_ids, f32[5]{0:T(128)} %visc.1, f32[5,5]{1,0:T(8,128)} %coup.1, f32[37]{0:T(128)} %constant.27.clone.refs_4_.table, f32[8,16,128]{2,1,0:T(8,128)} %pert.1, s32[16,128]{1,0:T(8,128)} %ids_ref.1, f32[16,128]{1,0:T(8,128)} %speed_ref.1, ...), custom_call_target="tpu_custom_call" | custom-call | tf_op jit(solution)/shard_map/before/pallas_call | solution.py:613
  5.1 0.5 %collective-permute-start = (bf16[1,128,128]{2,1,0:T(8,128)(2,1)}, bf16[1,128,128]{2,1,0:T(8,128)(2,1)S(1)}, u32[]{:S(2)}, u32[]{:S(2)}) collective-permute-start(bf16[1,128,128]{2,1,0:T(8,128)(2,1)} %before.1.own_ref), channel_id=1, source_target_pairs={{0,1},{1,0},{2,3},{3,2},{4,5},{5,4},{6,7},{7,6},{8,9},{9,8},{10,11... | collective-permute-start | bytes 98312 | tf_op jit(solution)/shard_map/ppermute | solution.py:589
  5.7 1.1 %collective-permute-done.near_ref = bf16[1,128,128]{2,1,0:T(8,128)(2,1)S(1)} collective-permute-done((bf16[1,128,128]{2,1,0:T(8,128)(2,1)}, bf16[1,128,128]{2,1,0:T(8,128)(2,1)S(1)}, u32[]{:S(2)}, u32[]{:S(2)}) %collective-permute-start) | collective-permute-done | bytes 32800 | tf_op jit(solution)/shard_map/ppermute | solution.py:589
  6.7 0.8 %broadcast_select_fusion = (bf16[1,128,128]{2,1,0:T(8,128)(2,1)S(1)}, bf16[1,128,128]{2,1,0:T(8,128)(2,1)S(1)}) fusion(bf16[1,128,128]{2,1,0:T(8,128)(2,1)} %before.1.own_ref, bf16[1,128,128]{2,1,0:T(8,128)(2,1)S(1)} %collective-permute-done.near_ref, pred[]{:T(512)S(6)} %eq.17), kind=kLoop, calls=%fused_computation.26 | loop fusion | flops 32768 | bytes 131073 | tf_op jit(solution)/shard_map/jit(_where)/select_n | solution.py:629
  7.5 0.7 %constant_dynamic-update-slice_fusion.3 = (bf16[1,144,128]{2,1,0:T(8,128)(2,1)S(1)}, bf16[1,8,128]{2,1,0:T(8,128)(2,1)S(1)}) fusion(bf16[1,144,128]{2,1,0:T(8,128)(2,1)S(1)} %get-tuple-element.56, bf16[1,128,128]{2,1,0:T(8,128)(2,1)S(1)} %collective-permute-done.near_ref, bf16[1,128,128]{2,1,0:T(8,128)(2,1)} %before.1.own_ref), kind=kLoop, calls=%fused_computation.3 | loop fusion | flops 9216 | bytes 12288
  8.2 0.7 %constant_dynamic-update-slice_fusion.2 = (bf16[1,144,128]{2,1,0:T(8,128)(2,1)S(1)}, bf16[1,8,128]{2,1,0:T(8,128)(2,1)S(1)}) fusion(bf16[1,144,128]{2,1,0:T(8,128)(2,1)S(1)} %get-tuple-element.44, bf16[1,128,128]{2,1,0:T(8,128)(2,1)S(1)} %collective-permute-done.near_ref, bf16[1,128,128]{2,1,0:T(8,128)(2,1)} %before.1.own_ref), kind=kLoop, calls=%fused_computation.2 | loop fusion | flops 10240 | bytes 12288
  9.0 2.7 %collective-permute-start.1 = (bf16[1,144,128]{2,1,0:T(8,128)(2,1)S(1)}, bf16[1,144,128]{2,1,0:T(8,128)(2,1)S(1)}, u32[]{:S(2)}, u32[]{:S(2)}) collective-permute-start(bf16[1,144,128]{2,1,0:T(8,128)(2,1)S(1)} %constant_dynamic-update-slice_fusion), channel_id=1, source_target_pairs={{0,3},{1,2},{2,1},{3,0},{4,7},{5,6},{6,5},{7,4},{8,11},{9,10},{10,... | collective-permute-start | bytes 110600 | tf_op jit(solution)/shard_map/ppermute | solution.py:589
  11.7 1.6 %collective-permute-done.1 = bf16[1,144,128]{2,1,0:T(8,128)(2,1)S(1)} collective-permute-done((bf16[1,144,128]{2,1,0:T(8,128)(2,1)S(1)}, bf16[1,144,128]{2,1,0:T(8,128)(2,1)S(1)}, u32[]{:S(2)}, u32[]{:S(2)}) %collective-permute-start.1) | collective-permute-done | bytes 36896 | tf_op jit(solution)/shard_map/ppermute | solution.py:589
  13.3 1.9 %collective-permute-start.2 = (bf16[1,176,128]{2,1,0:T(8,128)(2,1)S(1)}, bf16[1,176,128]{2,1,0:T(8,128)(2,1)S(1)}, u32[]{:S(2)}, u32[]{:S(2)}) collective-permute-start(bf16[1,176,128]{2,1,0:T(8,128)(2,1)S(1)} %constant_dynamic-update-slice_fusion.6), channel_id=1, source_target_pairs={{0,5},{1,4},{2,7},{3,6},{4,1},{5,0},{6,3},{7,2},{8,13},{9,12},{10,... | collective-permute-start | bytes 135176 | tf_op jit(solution)/shard_map/ppermute | solution.py:589
  15.3 1.7 %collective-permute-done.2 = bf16[1,176,128]{2,1,0:T(8,128)(2,1)S(1)} collective-permute-done((bf16[1,176,128]{2,1,0:T(8,128)(2,1)S(1)}, bf16[1,176,128]{2,1,0:T(8,128)(2,1)S(1)}, u32[]{:S(2)}, u32[]{:S(2)}) %collective-permute-start.2) | collective-permute-done | bytes 45088 | tf_op jit(solution)/shard_map/ppermute | solution.py:589
  17.0 3.0 %collective-permute-start.3 = (bf16[1,240,128]{2,1,0:T(8,128)(2,1)S(1)}, bf16[1,240,128]{2,1,0:T(8,128)(2,1)S(1)}, u32[]{:S(2)}, u32[]{:S(2)}) collective-permute-start(bf16[1,240,128]{2,1,0:T(8,128)(2,1)S(1)} %constant_dynamic-update-slice_fusion.12), channel_id=1, source_target_pairs={{0,9},{1,8},{2,11},{3,10},{4,13},{5,12},{6,15},{7,14},{8,1},{9,0},... | collective-permute-start | bytes 184328 | tf_op jit(solution)/shard_map/ppermute | solution.py:589
  20.0 2.1 %collective-permute-done.3 = bf16[1,240,128]{2,1,0:T(8,128)(2,1)S(1)} collective-permute-done((bf16[1,240,128]{2,1,0:T(8,128)(2,1)S(1)}, bf16[1,240,128]{2,1,0:T(8,128)(2,1)S(1)}, u32[]{:S(2)}, u32[]{:S(2)}) %collective-permute-start.3) | collective-permute-done | bytes 61472 | tf_op jit(solution)/shard_map/ppermute | solution.py:589
  22.3 0.6 %copy-done.2 = bf16[1,128,128]{2,1,0:T(8,128)(2,1)S(1)} copy-done((bf16[1,128,128]{2,1,0:T(8,128)(2,1)S(1)}, bf16[1,128,128]{2,1,0:T(8,128)(2,1)}, u32[]{:S(2)}) %copy-start.2) | copy-done | bytes 32792
  23.0 7.8 %after.1 = (bf16[32,5,16,128]{3,2,1,0:T(8,128)(2,1)}, f32[1,8,128]{2,1,0:T(8,128)S(1)}, f32[1,8,128]{2,1,0:T(8,128)S(1)}) custom-call(s32[32]{0:T(128)S(1)} %copy-done.8, s32[1]{0:T(128)S(6)} %copy.42.refs_1_.pert_ids, s32[1]{0:T(128)} %bitcast.place, f32[16]{0:T(128)S(1)} %copy-done.11, f32[5]{0:T(128)S(1)} %copy-done.12, f32[5]{0:T(128)S(1)} %copy-done.9, ...), custom_call_target="tpu_custom_call" | custom-call | tf_op jit(solution)/shard_map/after/pallas_call | solution.py:650
  30.7 0.3 collective-permute-start.4
  31.1 0.9 %collective-permute-done.4 = f32[1,8,128]{2,1,0:T(8,128)S(1)} collective-permute-done((f32[1,8,128]{2,1,0:T(8,128)S(1)}, f32[1,8,128]{2,1,0:T(8,128)S(1)}, u32[]{:S(2)}, u32[]{:S(2)}) %collective-permute-start.4) | collective-permute-done | bytes 4128 | tf_op jit(solution)/shard_map/ppermute | solution.py:589
  32.0 3.0 %collective-permute-start.5 = (f32[1,8,128]{2,1,0:T(8,128)S(1)}, f32[1,8,128]{2,1,0:T(8,128)S(1)}, u32[]{:S(2)}, u32[]{:S(2)}) collective-permute-start(f32[1,8,128]{2,1,0:T(8,128)S(1)} %add.65), channel_id=1, source_target_pairs={{0,3},{1,2},{2,1},{3,0},{4,7},{5,6},{6,5},{7,4},{8,11},{9,10},{10,... | collective-permute-start | bytes 12296 | tf_op jit(solution)/shard_map/ppermute | solution.py:589
  35.0 1.2 %system.1 = (f32[32,32]{1,0:T(8,128)S(1)}, f32[32,64]{1,0:T(8,128)S(1)}) custom-call(f32[1,8,128]{2,1,0:T(8,128)S(1)} %get-tuple-element.21.coords_ref), custom_call_target="tpu_custom_call" | custom-call | flops 100000000 | bytes 1048576 | tf_op jit(solution)/shard_map/system/pallas_call | solution.py:701
  36.3 1.3 %collective-permute-start.6 = (f32[1,8,128]{2,1,0:T(8,128)S(1)}, f32[1,8,128]{2,1,0:T(8,128)S(1)}, u32[]{:S(2)}, u32[]{:S(2)}) collective-permute-start(f32[1,8,128]{2,1,0:T(8,128)S(1)} %add.66), channel_id=1, source_target_pairs={{0,5},{1,4},{2,7},{3,6},{4,1},{5,0},{6,3},{7,2},{8,13},{9,12},{10,... | collective-permute-start | bytes 12296 | tf_op jit(solution)/shard_map/ppermute | solution.py:589
  37.6 1.7 %invert.1.inverse_ref = f32[32,32]{1,0:T(8,128)S(1)} custom-call(f32[32,64]{1,0:T(8,128)S(1)} %get-tuple-element.25.system_ref), custom_call_target="tpu_custom_call" | custom-call | flops 100000000 | bytes 1048576 | tf_op jit(solution)/shard_map/invert/pallas_call | solution.py:701
  39.4 3.3 %collective-permute-start.7 = (f32[1,8,128]{2,1,0:T(8,128)S(1)}, f32[1,8,128]{2,1,0:T(8,128)S(1)}, u32[]{:S(2)}, u32[]{:S(2)}) collective-permute-start(f32[1,8,128]{2,1,0:T(8,128)S(1)} %add.67), channel_id=1, source_target_pairs={{0,9},{1,8},{2,11},{3,10},{4,13},{5,12},{6,15},{7,14},{8,1},{9,0},... | collective-permute-start | bytes 12296 | tf_op jit(solution)/shard_map/ppermute | solution.py:589
  42.7 0.6 %weights.1 = (f32[32,560]{1,0:T(8,128)S(1)}, f32[32,32]{1,0:T(8,128)S(1)}) custom-call(f32[1,8,128]{2,1,0:T(8,128)S(1)} %get-tuple-element.21.coords_ref, f32[32,32]{1,0:T(8,128)S(1)} %get-tuple-element.27.kernel_ref, f32[32,32]{1,0:T(8,128)S(1)} %invert.1.inverse_ref, f32[32,560]{1,0:T(8,128)S(1)} %copy-done.14, f32[32,560]{1,0:T(8,128)S(1)} %copy-done.13, ...), custom_call_target="tpu_custom_call" | custom-call | flops 100000000 | bytes 1048576 | tf_op jit(solution)/shard_map/weights/pallas_call | solution.py:701
  43.2 0.7 %collective-permute-done.7 = f32[1,8,128]{2,1,0:T(8,128)S(1)} collective-permute-done((f32[1,8,128]{2,1,0:T(8,128)S(1)}, f32[1,8,128]{2,1,0:T(8,128)S(1)}, u32[]{:S(2)}, u32[]{:S(2)}) %collective-permute-start.7) | collective-permute-done | bytes 4128 | tf_op jit(solution)/shard_map/ppermute | solution.py:589
  44.0 1.0 %fit.1 = (f32[2,64]{1,0:T(2,128)}, f32[32,560]{1,0:T(8,128)}, f32[2,32]{1,0:T(2,128)}) custom-call(s32[1]{0:T(128)} %bitcast.place, f32[1,8,128]{2,1,0:T(8,128)S(1)} %add.68.rates_ref, f32[1,8,128]{2,1,0:T(8,128)S(1)} %get-tuple-element.21.coords_ref, f32[32,560]{1,0:T(8,128)S(1)} %get-tuple-element.29.weights, f32[32,32]{1,0:T(8,128)S(1)} %get-tuple-element.30.fit), custom_call_target="tpu_custom_call" | custom-call | tf_op jit(solution)/shard_map/fit/pallas_call | solution.py:741
  (53 shorter events, 0.5 us)
Async XLA Ops:
  1.3 21.0 %copy-start.1 = (bf16[32,5,16,128]{3,2,1,0:T(8,128)(2,1)S(1)}, bf16[32,5,16,128]{3,2,1,0:T(8,128)(2,1)}, u32[]{:S(2)}) copy-start(bf16[32,5,16,128]{3,2,1,0:T(8,128)(2,1)} %basis_hbm.1) | copy-start | bytes 1966084
  1.3 21.0 %copy-start.3 = (f32[8,16,128]{2,1,0:T(8,128)S(1)}, f32[8,16,128]{2,1,0:T(8,128)}, u32[]{:S(2)}) copy-start(f32[8,16,128]{2,1,0:T(8,128)} %pert.1) | copy-start | bytes 196612
  5.1 17.2 %copy-start = (bf16[32,5,16,128]{3,2,1,0:T(8,128)(2,1)S(1)}, bf16[32,5,16,128]{3,2,1,0:T(8,128)(2,1)}, u32[]{:S(2)}) copy-start(bf16[32,5,16,128]{3,2,1,0:T(8,128)(2,1)} %states.1) | copy-start | bytes 1966084
  5.1 1.6 %collective-permute-start = (bf16[1,128,128]{2,1,0:T(8,128)(2,1)}, bf16[1,128,128]{2,1,0:T(8,128)(2,1)S(1)}, u32[]{:S(2)}, u32[]{:S(2)}) collective-permute-start(bf16[1,128,128]{2,1,0:T(8,128)(2,1)} %before.1.own_ref), channel_id=1, source_target_pairs={{0,1},{1,0},{2,3},{3,2},{4,5},{5,4},{6,7},{7,6},{8,9},{9,8},{10,11... | collective-permute-start | bytes 98312 | tf_op jit(solution)/shard_map/ppermute | solution.py:589
  9.0 4.3 %collective-permute-start.1 = (bf16[1,144,128]{2,1,0:T(8,128)(2,1)S(1)}, bf16[1,144,128]{2,1,0:T(8,128)(2,1)S(1)}, u32[]{:S(2)}, u32[]{:S(2)}) collective-permute-start(bf16[1,144,128]{2,1,0:T(8,128)(2,1)S(1)} %constant_dynamic-update-slice_fusion), channel_id=1, source_target_pairs={{0,3},{1,2},{2,1},{3,0},{4,7},{5,6},{6,5},{7,4},{8,11},{9,10},{10,... | collective-permute-start | bytes 110600 | tf_op jit(solution)/shard_map/ppermute | solution.py:589
  13.3 3.6 %collective-permute-start.2 = (bf16[1,176,128]{2,1,0:T(8,128)(2,1)S(1)}, bf16[1,176,128]{2,1,0:T(8,128)(2,1)S(1)}, u32[]{:S(2)}, u32[]{:S(2)}) collective-permute-start(bf16[1,176,128]{2,1,0:T(8,128)(2,1)S(1)} %constant_dynamic-update-slice_fusion.6), channel_id=1, source_target_pairs={{0,5},{1,4},{2,7},{3,6},{4,1},{5,0},{6,3},{7,2},{8,13},{9,12},{10,... | collective-permute-start | bytes 135176 | tf_op jit(solution)/shard_map/ppermute | solution.py:589
  17.0 5.1 %collective-permute-start.3 = (bf16[1,240,128]{2,1,0:T(8,128)(2,1)S(1)}, bf16[1,240,128]{2,1,0:T(8,128)(2,1)S(1)}, u32[]{:S(2)}, u32[]{:S(2)}) collective-permute-start(bf16[1,240,128]{2,1,0:T(8,128)(2,1)S(1)} %constant_dynamic-update-slice_fusion.12), channel_id=1, source_target_pairs={{0,9},{1,8},{2,11},{3,10},{4,13},{5,12},{6,15},{7,14},{8,1},{9,0},... | collective-permute-start | bytes 184328 | tf_op jit(solution)/shard_map/ppermute | solution.py:589
  22.2 0.8 %copy-start.2 = (bf16[1,128,128]{2,1,0:T(8,128)(2,1)S(1)}, bf16[1,128,128]{2,1,0:T(8,128)(2,1)}, u32[]{:S(2)}) copy-start(bf16[1,128,128]{2,1,0:T(8,128)(2,1)} %before.1.own_ref) | copy-start | bytes 98308
  22.2 0.8 %copy-start.4 = (s32[16,128]{1,0:T(8,128)S(1)}, s32[16,128]{1,0:T(8,128)}, u32[]{:S(2)}) copy-start(s32[16,128]{1,0:T(8,128)} %ids_ref.1) | copy-start | bytes 24580
  22.2 0.7 %copy-start.5 = (f32[16,128]{1,0:T(8,128)S(1)}, f32[16,128]{1,0:T(8,128)}, u32[]{:S(2)}) copy-start(f32[16,128]{1,0:T(8,128)} %speed_ref.1) | copy-start | bytes 24580
  22.2 0.7 %copy-start.6 = (f32[16,128]{1,0:T(8,128)S(1)}, f32[16,128]{1,0:T(8,128)}, u32[]{:S(2)}) copy-start(f32[16,128]{1,0:T(8,128)} %force_ref.1) | copy-start | bytes 24580
  22.2 0.7 %copy-start.7 = (f32[5,5]{1,0:T(8,128)S(1)}, f32[5,5]{1,0:T(8,128)}, u32[]{:S(2)}) copy-start(f32[5,5]{1,0:T(8,128)} %coup.1) | copy-start | bytes 304
  22.2 0.7 %copy-start.11 = (f32[16]{0:T(128)S(1)}, f32[16]{0:T(128)}, u32[]{:S(2)}) copy-start(f32[16]{0:T(128)} %kern.1) | copy-start | bytes 196
  22.2 0.7 %copy-start.12 = (f32[5]{0:T(128)S(1)}, f32[5]{0:T(128)}, u32[]{:S(2)}) copy-start(f32[5]{0:T(128)} %gain.1) | copy-start | bytes 64
  22.3 0.7 %copy-start.8 = (s32[32]{0:T(128)S(1)}, s32[32]{0:T(128)}, u32[]{:S(2)}) copy-start(s32[32]{0:T(128)} %times.1) | copy-start | bytes 388
  22.3 0.7 %copy-start.9 = (f32[5]{0:T(128)S(1)}, f32[5]{0:T(128)}, u32[]{:S(2)}) copy-start(f32[5]{0:T(128)} %visc.1) | copy-start | bytes 64
  22.3 0.7 %copy-start.10 = (f32[37]{0:T(128)S(1)}, f32[37]{0:T(128)}, u32[]{:S(2)}) copy-start(f32[37]{0:T(128)} %constant.27.clone.refs_4_.table) | copy-start | bytes 448
  30.7 1.2 %collective-permute-start.4 = (f32[1,8,128]{2,1,0:T(8,128)S(1)}, f32[1,8,128]{2,1,0:T(8,128)S(1)}, u32[]{:S(2)}, u32[]{:S(2)}) collective-permute-start(f32[1,8,128]{2,1,0:T(8,128)S(1)} %get-tuple-element.20), channel_id=1, source_target_pairs={{0,1},{1,0},{2,3},{3,2},{4,5},{5,4},{6,7},{7,6},{8,9},{9,8},{10,11... | collective-permute-start | bytes 12296 | tf_op jit(solution)/shard_map/ppermute | solution.py:589
  32.0 4.3 %collective-permute-start.5 = (f32[1,8,128]{2,1,0:T(8,128)S(1)}, f32[1,8,128]{2,1,0:T(8,128)S(1)}, u32[]{:S(2)}, u32[]{:S(2)}) collective-permute-start(f32[1,8,128]{2,1,0:T(8,128)S(1)} %add.65), channel_id=1, source_target_pairs={{0,3},{1,2},{2,1},{3,0},{4,7},{5,6},{6,5},{7,4},{8,11},{9,10},{10,... | collective-permute-start | bytes 12296 | tf_op jit(solution)/shard_map/ppermute | solution.py:589
  36.3 6.3 %copy-start.13 = (f32[32,560]{1,0:T(8,128)S(1)}, f32[32,560]{1,0:T(8,128)}, u32[]{:S(2)}) copy-start(f32[32,560]{1,0:T(8,128)} %constant.29.clone.second_ref) | copy-start | bytes 215044
  36.3 6.3 %copy-start.14 = (f32[32,560]{1,0:T(8,128)S(1)}, f32[32,560]{1,0:T(8,128)}, u32[]{:S(2)}) copy-start(f32[32,560]{1,0:T(8,128)} %constant.28.clone.first_ref) | copy-start | bytes 215044
  36.3 3.1 %collective-permute-start.6 = (f32[1,8,128]{2,1,0:T(8,128)S(1)}, f32[1,8,128]{2,1,0:T(8,128)S(1)}, u32[]{:S(2)}, u32[]{:S(2)}) collective-permute-start(f32[1,8,128]{2,1,0:T(8,128)S(1)} %add.66), channel_id=1, source_target_pairs={{0,5},{1,4},{2,7},{3,6},{4,1},{5,0},{6,3},{7,2},{8,13},{9,12},{10,... | collective-permute-start | bytes 12296 | tf_op jit(solution)/shard_map/ppermute | solution.py:589
  39.3 3.4 %copy-start.15 = (f32[1,560]{1,0:T(1,128)S(1)}, f32[1,560]{1,0:T(1,128)}, u32[]{:S(2)}) copy-start(f32[1,560]{1,0:T(1,128)} %constant.30.clone.lin_ref) | copy-start | bytes 6724
  39.4 4.6 %collective-permute-start.7 = (f32[1,8,128]{2,1,0:T(8,128)S(1)}, f32[1,8,128]{2,1,0:T(8,128)S(1)}, u32[]{:S(2)}, u32[]{:S(2)}) collective-permute-start(f32[1,8,128]{2,1,0:T(8,128)S(1)} %add.67), channel_id=1, source_target_pairs={{0,9},{1,8},{2,11},{3,10},{4,13},{5,12},{6,15},{7,14},{8,1},{9,0},... | collective-permute-start | bytes 12296 | tf_op jit(solution)/shard_map/ppermute | solution.py:589

commit v3 on v2

--- a/solution.py
+++ b/solution.py
@@ -171,8 +171,8 @@
     to_start = jnp.where(snap_of_row & (part_of_lane < 2), scale, 0.0)
     to_rate = jnp.where(snap_of_row & (part_of_lane >= 2), scale, 0.0)
     copies[-2].wait()
-    copies[-1].wait()
-    flat_basis = flat(basis, 0, basis.shape[0])
+    if chunks > 1:
+        copies[-1].wait()
 
     def chunk_step(chunk, carry):
         first = chunk * CHUNK
@@ -219,6 +219,9 @@
         )
         right = [jnp.where(c8 < 2, t[:8], roll(t[8:], 2, 1)) for t in edges]
         left = [jnp.where(c8 >= 2, t[:8], roll(t[8:], -2, 1)) for t in edges]
+        if chunks == 1:
+            copies[-1].wait()
+        flat_basis = flat(basis, 0, basis.shape[0])
         coords = split(project(flat(states, first, CHUNK), flat_basis))
         rows = [packed, p_edges, *coords, *right, params_right, *left, params_left]
         out[chunk] = jnp.concatenate(rows, axis=0).astype(BF16)
@@ -228,6 +231,45 @@
         chunk_step(0, 0)
     else:
         lax.fori_loop(0, chunks, chunk_step, 0)
+
+
+def start_kernel(top, place, first, near, out, edges):
+    odd = place[0] % 2 == 1
+    for chunk in range(out.shape[0]):
+        mine, other = first[chunk].astype(F32), near[chunk].astype(F32)
+        low, high = jnp.where(odd, other, mine), jnp.where(odd, mine, other)
+        total = mine[BLOB : BLOB + COORD] + other[BLOB : BLOB + COORD]
+        right, left = high[RIGHT], low[LEFT]
+        edges[chunk] = jnp.concatenate([right, left], axis=0).astype(BF16)
+        payload = jnp.where(goes_right(place[0], top), right, left)
+        rows = [payload, *split(total[:8] + total[8:]), low[:BLOB], high[:BLOB]]
+        out[chunk] = jnp.concatenate(rows, axis=0).astype(BF16)
+
+
+def goes_right(me, bit):
+    if bit == 0:
+        return me % 2 == 1
+    lower = jnp.bitwise_and(jnp.right_shift(me, 1), (1 << bit) - 1)
+    return lower == (1 << bit) - 1
+
+
+def goes_left(me, bit):
+    lower = jnp.bitwise_and(jnp.right_shift(me, 1), (1 << bit) - 1)
+    return lower == 0
+
+
+def next_kernel(bit, place, sent, got, edges, out, new_edges):
+    me = place[0]
+    for chunk in range(out.shape[0]):
+        mine, other = sent[chunk].astype(F32), got[chunk].astype(F32)
+        both = edges[chunk].astype(F32)
+        right = jnp.where(goes_right(me, bit + 1), other[:EDGE], both[:EDGE])
+        left = jnp.where(goes_left(me, bit + 1), other[:EDGE], both[EDGE:])
+        new_edges[chunk] = jnp.concatenate([right, left], axis=0).astype(BF16)
+        payload = jnp.where(goes_right(me, bit), right, left)
+        total = mine[EDGE : EDGE + COORD] + other[EDGE : EDGE + COORD]
+        rows = [payload, *split(total[:8] + total[8:]), mine[EDGE + COORD :], other[EDGE + COORD :]]
+        out[chunk] = jnp.concatenate(rows, axis=0).astype(BF16)
 
 
 def after_kernel(
@@ -239,7 +281,7 @@
     visc,
     coup,
     table,
-    states,
+    states_hbm,
     basis_hbm,
     pert,
     ids_ref,
@@ -247,7 +289,7 @@
     force_ref,
     own_ref,
     near_ref,
-    far_ref,
+    sent_ref,
     last_ref,
     deriv,
     partial,
@@ -261,14 +303,18 @@
     east_coef,
     west_coef,
     basis,
-    sem,
+    states,
+    sems,
 ):
-    fetch = pltpu.make_async_copy(basis_hbm, basis, sem)
+    fetch_states = pltpu.make_async_copy(states_hbm, states, sems.at[0])
+    fetch = pltpu.make_async_copy(basis_hbm, basis, sems.at[1])
+    fetch_states.start()
     fetch.start()
     chunks = own_ref.shape[0]
     passages = kern.shape[0]
     me = place[0]
     base = me - lax.rem(me, 2)
+    bits = passages.bit_length() - 2
     odd = me % 2 == 1
     speed = speed_ref[...]
     force = force_ref[...]
@@ -324,17 +370,23 @@
 
     def chunk_step(chunk, carry):
         first = chunk * CHUNK
-        final = last_ref[chunk].astype(F32)
-        raw[...] = final[: passages * BLOB]
-        mixed[...] = jnp.dot(
-            final[: passages * BLOB].astype(BF16), mix, preferred_element_type=F32
-        )
-        summed = final[passages * BLOB : passages * BLOB + COORD]
+        head = EDGE + COORD
+        half = passages // 2 * BLOB
+        raw[:half, :] = sent_ref[chunk, head:, :].astype(F32)
+        raw[half:, :] = last_ref[chunk, head:, :].astype(F32)
+        summed = sent_ref[chunk, EDGE:head, :].astype(F32)
+        summed += last_ref[chunk, EDGE:head, :].astype(F32)
         coords[chunk] = summed[:8] + summed[8:]
+        mixed[...] = jnp.dot(raw[...].astype(BF16), mix, preferred_element_type=F32)
 
         def slot(offset):
             other = lax.rem(me + offset + passages, passages)
-            return pl.multiple_of(jnp.bitwise_xor(base, other) * BLOB, BLOB)
+            flips = jnp.bitwise_xor(base, other)
+            index = jnp.bitwise_and(flips, 1)
+            for bit in range(bits):
+                moved = jnp.bitwise_and(jnp.right_shift(flips, bit + 1), 1)
+                index = index + jnp.left_shift(moved, bits - bit)
+            return pl.multiple_of(index * BLOB, BLOB)
 
         def load(offset, carry):
             cyc0[pl.ds(pl.multiple_of(offset * 8, 8), 8), :] = mixed[pl.ds(slot(offset), 8), :LANES]
@@ -415,7 +467,7 @@
 
         near = near_ref[chunk].astype(F32)
         own = own_ref[chunk].astype(F32)
-        far = far_ref[chunk].astype(F32)
+        far = last_ref[chunk, :EDGE, :].astype(F32)
         west = jnp.where(odd, near[RIGHT], far)
         east = jnp.where(odd, far, near[LEFT])
 
@@ -492,6 +544,8 @@
                 snap(step * UNROLL + i)
             return carry
 
+        if chunks == 1:
+            fetch_states.wait()
         lax.fori_loop(0, CHUNK // UNROLL, snaps, 0)
         partial[chunk] = project(flat(deriv, first, CHUNK), flat_basis())
         return carry
@@ -499,6 +553,7 @@
     if chunks == 1:
         chunk_step(0, 0)
     else:
+        fetch_states.wait()
         fetch.wait()
         lax.fori_loop(0, chunks, chunk_step, 0)
 
@@ -590,12 +645,6 @@
 
     def swap_chip(value, mask):
         return swap(value, mask + 1)
-
-    def add_pieces(one, two):
-        total = one[:, :8].astype(F32) + one[:, 8:].astype(F32)
-        total += two[:, :8].astype(F32) + two[:, 8:].astype(F32)
-        high = lax.reduce_precision(total, 8, 7)
-        return jnp.concatenate([high, total - high], axis=1).astype(BF16)
 
     operands = (
         snapshot_times,
@@ -621,36 +670,38 @@
             pltpu.VMEM((3 * CHUNK * NX, LANES), BF16),
             pltpu.SemaphoreType.DMA((len(operands),)),
         ],
-        compiler_params=pltpu.CompilerParams(vmem_limit_bytes=60 * 2**20),
+        compiler_params=pltpu.CompilerParams(vmem_limit_bytes=24 * 2**20),
         name="before",
-    )(*operands)
+    )(*(x if x is pert_ids else pltpu.with_memory_space_constraint(x, pltpu.HBM) for x in operands))
     near = swap(first, 1)
-    odd = position % 2 == 1
-    low, high = jnp.where(odd, near, first), jnp.where(odd, first, near)
-    group = jnp.concatenate([low[:, :BLOB], high[:, :BLOB]], axis=1)
-    coords = add_pieces(first[:, BLOB : BLOB + COORD], near[:, BLOB : BLOB + COORD])
-    right, left = high[:, RIGHT], low[:, LEFT]
-    far_right, far_left = [], []
-    for r in range(1, rounds):
-        got = swap_chip(jnp.concatenate([group, coords, right, left], axis=1), 1 << r)
-        rows = group.shape[1]
-        group = jnp.concatenate([group, got[:, :rows]], axis=1)
-        coords = add_pieces(coords, got[:, rows : rows + COORD])
-        right, left = got[:, rows + COORD : rows + COORD + EDGE], got[:, rows + COORD + EDGE :]
-        far_right.append(right)
-        far_left.append(left)
-    for r in range(rounds - 2, 0, -1):
-        bit = (position >> r) & 1
-        right = jnp.where(bit == 1, far_right[r - 1], right)
-        left = jnp.where(bit == 0, far_left[r - 1], left)
-    far = jnp.where(odd, left, right)
-    last = jnp.concatenate([group, coords], axis=1)
+    bits = rounds - 1
+    edges_shape = jax.ShapeDtypeStruct((chunks, 2 * EDGE, LANES), BF16)
+    head = EDGE + COORD
+
+    def glue(kernel, name, rows, *args):
+        return pl.pallas_call(
+            kernel,
+            out_shape=(jax.ShapeDtypeStruct((chunks, rows, LANES), BF16), edges_shape),
+            in_specs=[SMEM] + [VMEM] * len(args),
+            out_specs=(VMEM, VMEM),
+            compiler_params=pltpu.CompilerParams(vmem_limit_bytes=16 * 2**20),
+            name=name,
+        )(place, *args)
+
+    start = functools.partial(start_kernel, bits - 1)
+    message, edges = glue(start, "start", head + 2 * BLOB, first, near)
+    for bit in range(bits - 1, -1, -1):
+        got = swap_chip(message, 2 << bit)
+        if bit:
+            rows = 2 * message.shape[1] - head
+            step = functools.partial(next_kernel, bit - 1)
+            message, edges = glue(step, "next", rows, message, got, edges)
 
     tile = jax.ShapeDtypeStruct((chunks, 8, LANES), F32)
     derivative, partial, coords = pl.pallas_call(
         after_kernel,
         out_shape=(jax.ShapeDtypeStruct(states.shape, BF16), tile, tile),
-        in_specs=[SMEM] * 8 + [VMEM, HBM] + [VMEM] * 8,
+        in_specs=[SMEM] * 8 + [HBM, HBM] + [VMEM] * 8,
         out_specs=(VMEM, VMEM, VMEM),
         scratch_shapes=[
             pltpu.VMEM((passages * BLOB, 6 * LANES), F32),
@@ -662,7 +713,8 @@
             pltpu.VMEM((NV, NX, LANES), F32),
             pltpu.VMEM((NV, NX, LANES), F32),
             pltpu.VMEM(basis.shape, BF16),
-            pltpu.SemaphoreType.DMA,
+            pltpu.VMEM(states.shape, BF16),
+            pltpu.SemaphoreType.DMA((2,)),
         ],
         compiler_params=pltpu.CompilerParams(vmem_limit_bytes=32 * 2**20),
         name="after",
@@ -675,16 +727,16 @@
         viscosity,
         coupling,
         table,
-        states,
-        basis,
+        pltpu.with_memory_space_constraint(states, pltpu.HBM),
+        pltpu.with_memory_space_constraint(basis, pltpu.HBM),
         pert_table,
         cycle_ids,
         speed,
         force_amp,
         first,
         near,
-        far,
-        last,
+        message,
+        got,
     )
 
     upper_first, upper_second = np.triu_indices(modes)

time: 45.3 us -> 41.1 us (0.907)
  other arithmetic: 2.3 us -> 0.04 us
  starting transfers between devices: 16 us -> 14.6 us
  Pallas kernels: 16 us -> 16.9 us
  local copies, waits for them, and re-layouts: 0.75 us -> 0.05 us
  waiting for transfers between devices: 8.4 us -> 7.89 us
    unnamed x7 -> x0, other arithmetic: 1.5 us -> none
    ppermute x8, starting transfers between devices: 16 us -> 14.6 us  [swap(): return lax.ppermute(value, 'passage', pairs)]
    pallas_call x1, Pallas kernels: 7.76 us -> 8.6 us  [body(): pl.pallas_call(after_kernel, out_shape=(jax.ShapeDtypeStruct(states.shape...]
    select_n x2 -> x0, other arithmetic: 0.78 us -> none  [the longest x1 0.77 us: body(): low, high = (jnp.where(odd, near, first), jnp.where(odd, first, near))]
    unnamed x38 -> x26, local copies, waits for them, and re-layouts: 0.73 us -> 0.05 us
    pallas_call x1, Pallas kernels: 3.82 us -> 3.16 us  [body(): pl.pallas_call(before_kernel, out_shape=jax.ShapeDtypeStruct((chunks, ROW...]
    pallas_call x0 -> x3, Pallas kernels: none -> 0.65 us  [glue(): pl.pallas_call(kernel, out_shape=(jax.ShapeDtypeStruct((chunks, rows, LAN...]
    ppermute x8, waiting for transfers between devices: 8.4 us -> 7.89 us  [swap(): return lax.ppermute(value, 'passage', pairs)]
  transfers between devices with their start and end apart: 8 -> 8, of which waited for: 8 -> 7; matrix products, arithmetic and copies ran while one was open for 0% -> 0% of each run, Pallas kernels for 8% -> 8%
where the time goes in v3:
time: 41.1 us; the launch traced here: 40.9 us
  Pallas kernels  16.9 us (41%)
  starting transfers between devices  14.6 us (36%)
  waiting for transfers between devices  7.89 us (19%)
  between operations  1.4 us (3%)
    ppermute x8, starting transfers between devices, swap(): return lax.ppermute(value, 'passage', pairs)  14.6 us
    pallas_call x1, Pallas kernels, body(): pl.pallas_call(after_kernel, out_shape=(jax.ShapeDtypeStruct(states.shape...  8.6 us
    ppermute x8, waiting for transfers between devices, swap(): return lax.ppermute(value, 'passage', pairs)  7.89 us
    pallas_call x3, Pallas kernels, small(): pl.pallas_call(kernel, out_shape=tuple((jax.ShapeDtypeStruct(shape, F32)...  3.45 us
    pallas_call x1, Pallas kernels, body(): pl.pallas_call(before_kernel, out_shape=jax.ShapeDtypeStruct((chunks, ROW...  3.16 us
    pallas_call x1, Pallas kernels, body(): pl.pallas_call(fit_kernel, out_shape=(jax.ShapeDtypeStruct((each, 2 * mod...  1 us
  transfers between devices with their start and end apart: 8, of which 7 were waited for; matrix products, arithmetic and copies ran while one was open for 0% of the time, Pallas kernels for 8%

profile of v3, /device:TPU:0, one launch (start us, length us, event | category | flops | bytes accessed | tf_op | source)
XLA Modules:
  0.0 40.9 jit_solution(5328627245526583512)
XLA Ops:
  1.3 3.2 %before.1.first.own_ref = bf16[1,128,128]{2,1,0:T(8,128)(2,1)S(1)} custom-call(s32[32]{0:T(128)} %times.1, s32[1]{0:T(128)S(6)} %copy.20.refs_1_.pert_ids, f32[5]{0:T(128)} %visc.1, f32[5,5]{1,0:T(8,128)} %coup.1, f32[37]{0:T(128)} %constant.12.clone.refs_4_.table, f32[8,16,128]{2,1,0:T(8,128)} %pert.1, s32[16,128]{1,0:T(8,128)} %ids_ref.1, ...), custom_call_target="tpu_custom_call" | custom-call | tf_op jit(solution)/shard_map/before/pallas_call | solution.py:662
  4.4 0.5 %collective-permute-start = (bf16[1,128,128]{2,1,0:T(8,128)(2,1)S(1)}, bf16[1,128,128]{2,1,0:T(8,128)(2,1)S(1)}, u32[]{:S(2)}, u32[]{:S(2)}) collective-permute-start(bf16[1,128,128]{2,1,0:T(8,128)(2,1)S(1)} %before.1.first.own_ref), channel_id=1, source_target_pairs={{0,1},{1,0},{2,3},{3,2},{4,5},{5,4},{6,7},{7,6},{8,9},{9,8},{10,11... | collective-permute-start | bytes 98312 | tf_op jit(solution)/shard_map/ppermute | solution.py:644
  5.0 0.9 %collective-permute-done.near.near_ref = bf16[1,128,128]{2,1,0:T(8,128)(2,1)S(1)} collective-permute-done((bf16[1,128,128]{2,1,0:T(8,128)(2,1)S(1)}, bf16[1,128,128]{2,1,0:T(8,128)(2,1)S(1)}, u32[]{:S(2)}, u32[]{:S(2)}) %collective-permute-start) | collective-permute-done | bytes 32800 | tf_op jit(solution)/shard_map/ppermute | solution.py:644
  5.8 3.8 %collective-permute-start.1 = (bf16[1,96,128]{2,1,0:T(8,128)(2,1)S(1)}, bf16[1,96,128]{2,1,0:T(8,128)(2,1)S(1)}, u32[]{:S(2)}, u32[]{:S(2)}) collective-permute-start(bf16[1,96,128]{2,1,0:T(8,128)(2,1)S(1)} %get-tuple-element.24.sent), channel_id=1, source_target_pairs={{0,9},{1,8},{2,11},{3,10},{4,13},{5,12},{6,15},{7,14},{8,1},{9,0},... | collective-permute-start | bytes 73736 | tf_op jit(solution)/shard_map/ppermute | solution.py:644
  9.6 1.5 %collective-permute-done.1.got = bf16[1,96,128]{2,1,0:T(8,128)(2,1)S(1)} collective-permute-done((bf16[1,96,128]{2,1,0:T(8,128)(2,1)S(1)}, bf16[1,96,128]{2,1,0:T(8,128)(2,1)S(1)}, u32[]{:S(2)}, u32[]{:S(2)}) %collective-permute-start.1) | collective-permute-done | bytes 24608 | tf_op jit(solution)/shard_map/ppermute | solution.py:644
  11.1 0.0 copy-start
  11.2 1.7 %collective-permute-start.2 = (bf16[1,128,128]{2,1,0:T(8,128)(2,1)S(1)}, bf16[1,128,128]{2,1,0:T(8,128)(2,1)S(1)}, u32[]{:S(2)}, u32[]{:S(2)}) collective-permute-start(bf16[1,128,128]{2,1,0:T(8,128)(2,1)S(1)} %get-tuple-element.26.sent), channel_id=1, source_target_pairs={{0,5},{1,4},{2,7},{3,6},{4,1},{5,0},{6,3},{7,2},{8,13},{9,12},{10,... | collective-permute-start | bytes 98312 | tf_op jit(solution)/shard_map/ppermute | solution.py:644
  12.8 1.7 %collective-permute-done.2.got = bf16[1,128,128]{2,1,0:T(8,128)(2,1)S(1)} collective-permute-done((bf16[1,128,128]{2,1,0:T(8,128)(2,1)S(1)}, bf16[1,128,128]{2,1,0:T(8,128)(2,1)S(1)}, u32[]{:S(2)}, u32[]{:S(2)}) %collective-permute-start.2) | collective-permute-done | bytes 32800 | tf_op jit(solution)/shard_map/ppermute | solution.py:644
  14.6 0.0 copy-start.8
  14.6 0.6 %next.3 = (bf16[1,192,128]{2,1,0:T(8,128)(2,1)S(1)}, bf16[1,96,128]{2,1,0:T(8,128)(2,1)}) custom-call(s32[1]{0:T(128)} %bitcast.place, bf16[1,128,128]{2,1,0:T(8,128)(2,1)S(1)} %get-tuple-element.26.sent, bf16[1,128,128]{2,1,0:T(8,128)(2,1)S(1)} %collective-permute-done.2.got, bf16[1,96,128]{2,1,0:T(8,128)(2,1)S(1)} %get-tuple-element.27.edges), custom_call_target="tpu_custom_call" | custom-call | tf_op jit(solution)/shard_map/next/pallas_call | solution.py:682
  15.2 1.6 %collective-permute-start.3 = (bf16[1,192,128]{2,1,0:T(8,128)(2,1)S(1)}, bf16[1,192,128]{2,1,0:T(8,128)(2,1)S(1)}, u32[]{:S(2)}, u32[]{:S(2)}) collective-permute-start(bf16[1,192,128]{2,1,0:T(8,128)(2,1)S(1)} %get-tuple-element.28.sent_ref), channel_id=1, source_target_pairs={{0,3},{1,2},{2,1},{3,0},{4,7},{5,6},{6,5},{7,4},{8,11},{9,10},{10,... | collective-permute-start | bytes 147464 | tf_op jit(solution)/shard_map/ppermute | solution.py:644
  16.8 2.0 %collective-permute-done.3.last_ref = bf16[1,192,128]{2,1,0:T(8,128)(2,1)S(1)} collective-permute-done((bf16[1,192,128]{2,1,0:T(8,128)(2,1)S(1)}, bf16[1,192,128]{2,1,0:T(8,128)(2,1)S(1)}, u32[]{:S(2)}, u32[]{:S(2)}) %collective-permute-start.3) | collective-permute-done | bytes 49184 | tf_op jit(solution)/shard_map/ppermute | solution.py:644
  18.9 8.6 %after.1 = (bf16[32,5,16,128]{3,2,1,0:T(8,128)(2,1)}, f32[1,8,128]{2,1,0:T(8,128)S(1)}, f32[1,8,128]{2,1,0:T(8,128)S(1)}) custom-call(s32[32]{0:T(128)S(1)} %copy-done.5, s32[1]{0:T(128)S(6)} %copy.20.refs_1_.pert_ids, s32[1]{0:T(128)} %bitcast.place, f32[16]{0:T(128)S(1)} %copy-done.8, f32[5]{0:T(128)S(1)} %copy-done.9, f32[5]{0:T(128)S(1)} %copy-done.6, ...), custom_call_target="tpu_custom_call" | custom-call | tf_op jit(solution)/shard_map/after/pallas_call | solution.py:701
  27.5 0.3 collective-permute-start.4
  27.8 0.9 %collective-permute-done.4 = f32[1,8,128]{2,1,0:T(8,128)S(1)} collective-permute-done((f32[1,8,128]{2,1,0:T(8,128)S(1)}, f32[1,8,128]{2,1,0:T(8,128)S(1)}, u32[]{:S(2)}, u32[]{:S(2)}) %collective-permute-start.4) | collective-permute-done | bytes 4128 | tf_op jit(solution)/shard_map/ppermute | solution.py:644
  28.7 1.8 %collective-permute-start.5 = (f32[1,8,128]{2,1,0:T(8,128)S(1)}, f32[1,8,128]{2,1,0:T(8,128)S(1)}, u32[]{:S(2)}, u32[]{:S(2)}) collective-permute-start(f32[1,8,128]{2,1,0:T(8,128)S(1)} %add.12), channel_id=1, source_target_pairs={{0,3},{1,2},{2,1},{3,0},{4,7},{5,6},{6,5},{7,4},{8,11},{9,10},{10,... | collective-permute-start | bytes 12296 | tf_op jit(solution)/shard_map/ppermute | solution.py:644
  30.5 1.2 %system.1 = (f32[32,32]{1,0:T(8,128)S(1)}, f32[32,64]{1,0:T(8,128)S(1)}) custom-call(f32[1,8,128]{2,1,0:T(8,128)S(1)} %get-tuple-element.31.coords_ref), custom_call_target="tpu_custom_call" | custom-call | flops 100000000 | bytes 1048576 | tf_op jit(solution)/shard_map/system/pallas_call | solution.py:753
  31.7 0.1 collective-permute-done.5
  31.8 1.8 %collective-permute-start.6 = (f32[1,8,128]{2,1,0:T(8,128)S(1)}, f32[1,8,128]{2,1,0:T(8,128)S(1)}, u32[]{:S(2)}, u32[]{:S(2)}) collective-permute-start(f32[1,8,128]{2,1,0:T(8,128)S(1)} %add.13), channel_id=1, source_target_pairs={{0,5},{1,4},{2,7},{3,6},{4,1},{5,0},{6,3},{7,2},{8,13},{9,12},{10,... | collective-permute-start | bytes 12296 | tf_op jit(solution)/shard_map/ppermute | solution.py:644
  33.7 1.7 %invert.1.inverse_ref = f32[32,32]{1,0:T(8,128)S(1)} custom-call(f32[32,64]{1,0:T(8,128)S(1)} %get-tuple-element.35.system_ref), custom_call_target="tpu_custom_call" | custom-call | flops 100000000 | bytes 1048576 | tf_op jit(solution)/shard_map/invert/pallas_call | solution.py:753
  35.4 3.2 %collective-permute-start.7 = (f32[1,8,128]{2,1,0:T(8,128)S(1)}, f32[1,8,128]{2,1,0:T(8,128)S(1)}, u32[]{:S(2)}, u32[]{:S(2)}) collective-permute-start(f32[1,8,128]{2,1,0:T(8,128)S(1)} %add.14), channel_id=1, source_target_pairs={{0,9},{1,8},{2,11},{3,10},{4,13},{5,12},{6,15},{7,14},{8,1},{9,0},... | collective-permute-start | bytes 12296 | tf_op jit(solution)/shard_map/ppermute | solution.py:644
  38.6 0.6 %weights.1 = (f32[32,560]{1,0:T(8,128)S(1)}, f32[32,32]{1,0:T(8,128)S(1)}) custom-call(f32[1,8,128]{2,1,0:T(8,128)S(1)} %get-tuple-element.31.coords_ref, f32[32,32]{1,0:T(8,128)S(1)} %get-tuple-element.37.kernel_ref, f32[32,32]{1,0:T(8,128)S(1)} %invert.1.inverse_ref, f32[32,560]{1,0:T(8,128)S(1)} %copy-done.11, f32[32,560]{1,0:T(8,128)S(1)} %copy-done.10, ...), custom_call_target="tpu_custom_call" | custom-call | flops 100000000 | bytes 1048576 | tf_op jit(solution)/shard_map/weights/pallas_call | solution.py:753
  39.1 0.8 %collective-permute-done.7 = f32[1,8,128]{2,1,0:T(8,128)S(1)} collective-permute-done((f32[1,8,128]{2,1,0:T(8,128)S(1)}, f32[1,8,128]{2,1,0:T(8,128)S(1)}, u32[]{:S(2)}, u32[]{:S(2)}) %collective-permute-start.7) | collective-permute-done | bytes 4128 | tf_op jit(solution)/shard_map/ppermute | solution.py:644
  39.9 1.0 %fit.1 = (f32[2,64]{1,0:T(2,128)}, f32[32,560]{1,0:T(8,128)}, f32[2,32]{1,0:T(2,128)}) custom-call(s32[1]{0:T(128)} %bitcast.place, f32[1,8,128]{2,1,0:T(8,128)S(1)} %add.15.rates_ref, f32[1,8,128]{2,1,0:T(8,128)S(1)} %get-tuple-element.31.coords_ref, f32[32,560]{1,0:T(8,128)S(1)} %get-tuple-element.39.weights, f32[32,32]{1,0:T(8,128)S(1)} %get-tuple-element.40.fit), custom_call_target="tpu_custom_call" | custom-call | tf_op jit(solution)/shard_map/fit/pallas_call | solution.py:793
  (31 shorter events, 0.1 us)
Async XLA Ops:
  4.4 1.4 %collective-permute-start = (bf16[1,128,128]{2,1,0:T(8,128)(2,1)S(1)}, bf16[1,128,128]{2,1,0:T(8,128)(2,1)S(1)}, u32[]{:S(2)}, u32[]{:S(2)}) collective-permute-start(bf16[1,128,128]{2,1,0:T(8,128)(2,1)S(1)} %before.1.first.own_ref), channel_id=1, source_target_pairs={{0,1},{1,0},{2,3},{3,2},{4,5},{5,4},{6,7},{7,6},{8,9},{9,8},{10,11... | collective-permute-start | bytes 98312 | tf_op jit(solution)/shard_map/ppermute | solution.py:644
  5.8 5.3 %collective-permute-start.1 = (bf16[1,96,128]{2,1,0:T(8,128)(2,1)S(1)}, bf16[1,96,128]{2,1,0:T(8,128)(2,1)S(1)}, u32[]{:S(2)}, u32[]{:S(2)}) collective-permute-start(bf16[1,96,128]{2,1,0:T(8,128)(2,1)S(1)} %get-tuple-element.24.sent), channel_id=1, source_target_pairs={{0,9},{1,8},{2,11},{3,10},{4,13},{5,12},{6,15},{7,14},{8,1},{9,0},... | collective-permute-start | bytes 73736 | tf_op jit(solution)/shard_map/ppermute | solution.py:644
  11.1 7.7 %copy-start.9 = (f32[5]{0:T(128)S(1)}, f32[5]{0:T(128)}, u32[]{:S(2)}) copy-start(f32[5]{0:T(128)} %gain.1) | copy-start | bytes 64
  11.1 7.7 %copy-start = (f32[8,16,128]{2,1,0:T(8,128)S(1)}, f32[8,16,128]{2,1,0:T(8,128)}, u32[]{:S(2)}) copy-start(f32[8,16,128]{2,1,0:T(8,128)} %pert.1) | copy-start | bytes 196612
  11.2 3.4 %collective-permute-start.2 = (bf16[1,128,128]{2,1,0:T(8,128)(2,1)S(1)}, bf16[1,128,128]{2,1,0:T(8,128)(2,1)S(1)}, u32[]{:S(2)}, u32[]{:S(2)}) collective-permute-start(bf16[1,128,128]{2,1,0:T(8,128)(2,1)S(1)} %get-tuple-element.26.sent), channel_id=1, source_target_pairs={{0,5},{1,4},{2,7},{3,6},{4,1},{5,0},{6,3},{7,2},{8,13},{9,12},{10,... | collective-permute-start | bytes 98312 | tf_op jit(solution)/shard_map/ppermute | solution.py:644
  14.6 4.3 %copy-start.1 = (s32[16,128]{1,0:T(8,128)S(1)}, s32[16,128]{1,0:T(8,128)}, u32[]{:S(2)}) copy-start(s32[16,128]{1,0:T(8,128)} %ids_ref.1) | copy-start | bytes 24580
  14.6 4.3 %copy-start.2 = (f32[16,128]{1,0:T(8,128)S(1)}, f32[16,128]{1,0:T(8,128)}, u32[]{:S(2)}) copy-start(f32[16,128]{1,0:T(8,128)} %speed_ref.1) | copy-start | bytes 24580
  14.6 4.3 %copy-start.3 = (f32[16,128]{1,0:T(8,128)S(1)}, f32[16,128]{1,0:T(8,128)}, u32[]{:S(2)}) copy-start(f32[16,128]{1,0:T(8,128)} %force_ref.1) | copy-start | bytes 24580
  14.6 4.3 %copy-start.4 = (f32[5,5]{1,0:T(8,128)S(1)}, f32[5,5]{1,0:T(8,128)}, u32[]{:S(2)}) copy-start(f32[5,5]{1,0:T(8,128)} %coup.1) | copy-start | bytes 304
  14.6 4.3 %copy-start.8 = (f32[16]{0:T(128)S(1)}, f32[16]{0:T(128)}, u32[]{:S(2)}) copy-start(f32[16]{0:T(128)} %kern.1) | copy-start | bytes 196
  15.2 3.7 %copy-start.5 = (s32[32]{0:T(128)S(1)}, s32[32]{0:T(128)}, u32[]{:S(2)}) copy-start(s32[32]{0:T(128)} %times.1) | copy-start | bytes 388
  15.2 3.7 %copy-start.6 = (f32[5]{0:T(128)S(1)}, f32[5]{0:T(128)}, u32[]{:S(2)}) copy-start(f32[5]{0:T(128)} %visc.1) | copy-start | bytes 64
  15.2 3.7 %copy-start.7 = (f32[37]{0:T(128)S(1)}, f32[37]{0:T(128)}, u32[]{:S(2)}) copy-start(f32[37]{0:T(128)} %constant.12.clone.refs_4_.table) | copy-start | bytes 448
  15.2 3.6 %collective-permute-start.3 = (bf16[1,192,128]{2,1,0:T(8,128)(2,1)S(1)}, bf16[1,192,128]{2,1,0:T(8,128)(2,1)S(1)}, u32[]{:S(2)}, u32[]{:S(2)}) collective-permute-start(bf16[1,192,128]{2,1,0:T(8,128)(2,1)S(1)} %get-tuple-element.28.sent_ref), channel_id=1, source_target_pairs={{0,3},{1,2},{2,1},{3,0},{4,7},{5,6},{6,5},{7,4},{8,11},{9,10},{10,... | collective-permute-start | bytes 147464 | tf_op jit(solution)/shard_map/ppermute | solution.py:644
  27.5 1.2 %collective-permute-start.4 = (f32[1,8,128]{2,1,0:T(8,128)S(1)}, f32[1,8,128]{2,1,0:T(8,128)S(1)}, u32[]{:S(2)}, u32[]{:S(2)}) collective-permute-start(f32[1,8,128]{2,1,0:T(8,128)S(1)} %get-tuple-element.30), channel_id=1, source_target_pairs={{0,1},{1,0},{2,3},{3,2},{4,5},{5,4},{6,7},{7,6},{8,9},{9,8},{10,11... | collective-permute-start | bytes 12296 | tf_op jit(solution)/shard_map/ppermute | solution.py:644
  28.7 3.1 %collective-permute-start.5 = (f32[1,8,128]{2,1,0:T(8,128)S(1)}, f32[1,8,128]{2,1,0:T(8,128)S(1)}, u32[]{:S(2)}, u32[]{:S(2)}) collective-permute-start(f32[1,8,128]{2,1,0:T(8,128)S(1)} %add.12), channel_id=1, source_target_pairs={{0,3},{1,2},{2,1},{3,0},{4,7},{5,6},{6,5},{7,4},{8,11},{9,10},{10,... | collective-permute-start | bytes 12296 | tf_op jit(solution)/shard_map/ppermute | solution.py:644
  31.8 6.7 %copy-start.10 = (f32[32,560]{1,0:T(8,128)S(1)}, f32[32,560]{1,0:T(8,128)}, u32[]{:S(2)}) copy-start(f32[32,560]{1,0:T(8,128)} %constant.14.clone.second_ref) | copy-start | bytes 215044
  31.8 6.7 %copy-start.11 = (f32[32,560]{1,0:T(8,128)S(1)}, f32[32,560]{1,0:T(8,128)}, u32[]{:S(2)}) copy-start(f32[32,560]{1,0:T(8,128)} %constant.13.clone.first_ref) | copy-start | bytes 215044
  31.8 3.5 %collective-permute-start.6 = (f32[1,8,128]{2,1,0:T(8,128)S(1)}, f32[1,8,128]{2,1,0:T(8,128)S(1)}, u32[]{:S(2)}, u32[]{:S(2)}) collective-permute-start(f32[1,8,128]{2,1,0:T(8,128)S(1)} %add.13), channel_id=1, source_target_pairs={{0,5},{1,4},{2,7},{3,6},{4,1},{5,0},{6,3},{7,2},{8,13},{9,12},{10,... | collective-permute-start | bytes 12296 | tf_op jit(solution)/shard_map/ppermute | solution.py:644
  35.3 3.2 %copy-start.12 = (f32[1,560]{1,0:T(1,128)S(1)}, f32[1,560]{1,0:T(1,128)}, u32[]{:S(2)}) copy-start(f32[1,560]{1,0:T(1,128)} %constant.15.clone.lin_ref) | copy-start | bytes 6724
  35.4 4.5 %collective-permute-start.7 = (f32[1,8,128]{2,1,0:T(8,128)S(1)}, f32[1,8,128]{2,1,0:T(8,128)S(1)}, u32[]{:S(2)}, u32[]{:S(2)}) collective-permute-start(f32[1,8,128]{2,1,0:T(8,128)S(1)} %add.14), channel_id=1, source_target_pairs={{0,9},{1,8},{2,11},{3,10},{4,13},{5,12},{6,15},{7,14},{8,1},{9,0},... | collective-permute-start | bytes 12296 | tf_op jit(solution)/shard_map/ppermute | solution.py:644

commit v4 on v3

--- a/solution.py
+++ b/solution.py
@@ -23,9 +23,9 @@
 BLOB = 16
 COORD = 16
 EDGE = 48
-ROWS = BLOB + COORD + 2 * EDGE
-RIGHT = slice(BLOB + COORD, BLOB + COORD + EDGE)
-LEFT = slice(BLOB + COORD + EDGE, ROWS)
+ROWS = BLOB + 2 * EDGE
+RIGHT = slice(BLOB, BLOB + EDGE)
+LEFT = slice(BLOB + EDGE, ROWS)
 
 HIGH = lax.Precision.HIGHEST
 NT = (((1,), (1,)), ((), ()))
@@ -98,15 +98,17 @@
 
 def before_kernel(*refs):
     count = 11
-    sources, out, targets = refs[:count], refs[count], refs[count + 1 : 2 * count + 1]
-    fields, sems = refs[2 * count + 1 :]
+    sources = refs[:count]
+    out, states, basis, cells, cosines, cos_lanes = refs[count : count + 6]
+    targets = (*refs[count + 6 : 2 * count + 4], states, basis)
+    fields, sems = refs[2 * count + 4 :]
     copies = [
         pltpu.make_async_copy(source, target, sems.at[i])
         for i, (source, target) in enumerate(zip(sources, targets))
     ]
     for copy in copies:
         copy.start()
-    times, pert_ids, visc, coup, table, pert, ids_ref, speed_ref, force_ref, states, basis = targets
+    times, pert_ids, visc, coup, table, pert, ids_ref, speed_ref, force_ref = targets[:-2]
     for copy in copies[:-2]:
         copy.wait()
     chunks = out.shape[0]
@@ -125,6 +127,8 @@
     c8 = lane_part()
     row8 = iota((8, LANES), 0)
     quad = iota((NX, LANES), 1) // 4
+    for index, field in enumerate((speed, force, damping, ids.astype(F32))):
+        cells[index] = field
     scale = 1.0 / math.sqrt(NX * LANES)
 
     def pieces(column):
@@ -171,16 +175,17 @@
     to_start = jnp.where(snap_of_row & (part_of_lane < 2), scale, 0.0)
     to_rate = jnp.where(snap_of_row & (part_of_lane >= 2), scale, 0.0)
     copies[-2].wait()
-    if chunks > 1:
-        copies[-1].wait()
 
     def chunk_step(chunk, carry):
         first = chunk * CHUNK
 
-        def snap(k, edges):
+        def snap(k, carried):
+            edges, cos_row = carried
             u = [states[first + k, v].astype(F32) for v in range(NV)]
             p = u[NV - 1]
             cosine = table[lax.rem(times[first + k], PERIOD)]
+            cosines[pl.ds(first + k, 1), :] = jnp.full((1, LANES), cosine, F32)
+            cos_row = jnp.where(quad[:8] == k, cosine, cos_row)
             rate = coef_east * roll(p, -1, 1) + coef_west * roll(p, 1, 1)
             rate = rate + visc_p * north_south(p) + coef_own * p + cosine * force
             for v in range(NV - 1):
@@ -190,16 +195,18 @@
             fields[pl.ds(at, NX), :] = p.astype(BF16)
             fields[pl.ds(pl.multiple_of(size + at, NX), NX), :] = high.astype(BF16)
             fields[pl.ds(pl.multiple_of(2 * size + at, NX), NX), :] = low.astype(BF16)
-            return tuple(
+            edges = tuple(
                 jnp.where(quad == k, roll(u[v], 4 * k + 2, 1), edges[v]) for v in range(NV)
             )
-
-        edges = tuple(jnp.zeros((NX, LANES), F32) for _ in range(NV))
+            return edges, cos_row
+
+        carried = tuple(jnp.zeros((NX, LANES), F32) for _ in range(NV)), jnp.zeros((8, LANES), F32)
         if chunks == 1:
             for k in range(CHUNK):
-                edges = snap(k, edges)
+                carried = snap(k, carried)
         else:
-            edges = lax.fori_loop(0, CHUNK, snap, edges)
+            carried = lax.fori_loop(0, CHUNK, snap, carried)
+        edges, cos_lanes[chunk] = carried
         sums = lax.dot_general(masks_half, fields[...], NT, preferred_element_type=F32)
         sums = jnp.where(same_x, sums, 0.0)
         by_cycle = jnp.sum(sums.reshape(NRING, NX, 3 * size), axis=1)
@@ -219,11 +226,7 @@
         )
         right = [jnp.where(c8 < 2, t[:8], roll(t[8:], 2, 1)) for t in edges]
         left = [jnp.where(c8 >= 2, t[:8], roll(t[8:], -2, 1)) for t in edges]
-        if chunks == 1:
-            copies[-1].wait()
-        flat_basis = flat(basis, 0, basis.shape[0])
-        coords = split(project(flat(states, first, CHUNK), flat_basis))
-        rows = [packed, p_edges, *coords, *right, params_right, *left, params_left]
+        rows = [packed, p_edges, *right, params_right, *left, params_left]
         out[chunk] = jnp.concatenate(rows, axis=0).astype(BF16)
         return carry
 
@@ -231,18 +234,31 @@
         chunk_step(0, 0)
     else:
         lax.fori_loop(0, chunks, chunk_step, 0)
-
-
-def start_kernel(top, place, first, near, out, edges):
+    copies[-1].wait()
+
+
+def coords_kernel(states, basis, after, out):
+    flat_basis = flat(basis, 0, basis.shape[0])
+    if out.shape[0] == 1:
+        out[0] = project(flat(states, 0, CHUNK), flat_basis)
+        return
+
+    def chunk_step(chunk, carry):
+        out[chunk] = project(flat(states, chunk * CHUNK, CHUNK), flat_basis)
+        return carry
+
+    lax.fori_loop(0, out.shape[0], chunk_step, 0)
+
+
+def start_kernel(top, place, first, near, coords, out, edges):
     odd = place[0] % 2 == 1
     for chunk in range(out.shape[0]):
         mine, other = first[chunk].astype(F32), near[chunk].astype(F32)
         low, high = jnp.where(odd, other, mine), jnp.where(odd, mine, other)
-        total = mine[BLOB : BLOB + COORD] + other[BLOB : BLOB + COORD]
         right, left = high[RIGHT], low[LEFT]
         edges[chunk] = jnp.concatenate([right, left], axis=0).astype(BF16)
         payload = jnp.where(goes_right(place[0], top), right, left)
-        rows = [payload, *split(total[:8] + total[8:]), low[:BLOB], high[:BLOB]]
+        rows = [payload, *split(coords[chunk]), low[:BLOB], high[:BLOB]]
         out[chunk] = jnp.concatenate(rows, axis=0).astype(BF16)
 
 
@@ -258,89 +274,27 @@
     return lower == 0
 
 
-def next_kernel(bit, place, sent, got, edges, out, new_edges):
+def next_kernel(bit, place, sent, got, edges, out, new_edges=None):
     me = place[0]
     for chunk in range(out.shape[0]):
         mine, other = sent[chunk].astype(F32), got[chunk].astype(F32)
         both = edges[chunk].astype(F32)
         right = jnp.where(goes_right(me, bit + 1), other[:EDGE], both[:EDGE])
         left = jnp.where(goes_left(me, bit + 1), other[:EDGE], both[EDGE:])
-        new_edges[chunk] = jnp.concatenate([right, left], axis=0).astype(BF16)
+        if new_edges is not None:
+            new_edges[chunk] = jnp.concatenate([right, left], axis=0).astype(BF16)
         payload = jnp.where(goes_right(me, bit), right, left)
         total = mine[EDGE : EDGE + COORD] + other[EDGE : EDGE + COORD]
         rows = [payload, *split(total[:8] + total[8:]), mine[EDGE + COORD :], other[EDGE + COORD :]]
         out[chunk] = jnp.concatenate(rows, axis=0).astype(BF16)
 
 
-def after_kernel(
-    times,
-    pert_ids,
-    place,
-    kern,
-    gain,
-    visc,
-    coup,
-    table,
-    states_hbm,
-    basis_hbm,
-    pert,
-    ids_ref,
-    speed_ref,
-    force_ref,
-    own_ref,
-    near_ref,
-    sent_ref,
-    last_ref,
-    deriv,
-    partial,
-    coords,
-    mixed,
-    raw,
-    cyc0,
-    grooves,
-    halo0,
-    halo1,
-    east_coef,
-    west_coef,
-    basis,
-    states,
-    sems,
-):
-    fetch_states = pltpu.make_async_copy(states_hbm, states, sems.at[0])
-    fetch = pltpu.make_async_copy(basis_hbm, basis, sems.at[1])
-    fetch_states.start()
-    fetch.start()
-    chunks = own_ref.shape[0]
-    passages = kern.shape[0]
-    me = place[0]
-    base = me - lax.rem(me, 2)
-    bits = passages.bit_length() - 2
-    odd = me % 2 == 1
-    speed = speed_ref[...]
-    force = force_ref[...]
-    damping = pert[pert_ids[0]]
-    ids = ids_ref[...]
-    half_speed = 0.5 * speed
+def prepare_kernel(visc, coup, kern, gain, cells, after, mixer, east_coef, west_coef):
+    half_speed = 0.5 * cells[0]
     lane = iota((NX, LANES), 1)
-    c16 = lane % 4
-    masks = cycle_masks(ids).astype(BF16)
-    masks_twice = jnp.concatenate([masks, masks], axis=0)
-    scale = 1.0 / math.sqrt(NX * LANES)
-    size = CHUNK * NX
-
-    src = iota((LANES, LANES), 0)
-    dst = iota((LANES, LANES), 1) // 4 * 4
-    mixers = [(src == dst) | (src == dst + 1), (src == dst + 2) | (src == dst + 3)]
-    mixers += [src == dst + 2, src == dst + 1, src == dst + 3, src == dst]
-    mix = jnp.concatenate([jnp.where(m, 1.0, 0.0).astype(BF16) for m in mixers], axis=1)
-    pick_snap = jnp.where(iota((size, LANES), 1) == iota((size, LANES), 0) // NX * 4, 1.0, 0.0)
-    pick_snap = pick_snap.astype(BF16)
-    wide = 4 * NRING * NX
-    same_x = iota((size, wide), 0) % NX == iota((size, wide), 1) % NX
-
     for v in range(NV):
-        east_coef[v] = visc[v] - half_speed
-        west_coef[v] = visc[v] + half_speed
+        east_coef[v] = jnp.where(lane == LANES - 1, 0.0, visc[v] - half_speed)
+        west_coef[v] = jnp.where(lane == 0, 0.0, visc[v] + half_speed)
     deep = NV * NX
     col = iota((NX, 3 * deep), 1)
     col_var, col_x = col % deep // NX, col % NX
@@ -355,11 +309,95 @@
         blocks.append(jnp.where((col_var == v) & beside, visc[v], weight))
     high, low = split(jnp.concatenate(blocks, axis=0))
     col = iota((deep, 3 * deep), 1)
-    mixer = jnp.where((col < deep) | (col >= 2 * deep), high, low).astype(BF16)
+    mixer[...] = jnp.where((col < deep) | (col >= 2 * deep), high, low).astype(BF16)
+
+
+def local_kernel(
+    offset,
+    states,
+    cells,
+    cosines,
+    mixer_ref,
+    east_coef,
+    west_coef,
+    after,
+    out,
+):
+    count = out.shape[0]
+    deep = NV * NX
+    force = cells[1]
+    damping = cells[2]
+    mixer = mixer_ref[...]
+
+    def linear(u, mixed):
+        result = []
+        for v in range(NV):
+            rate = mixed[NX * v : NX * v + NX] - damping * u[v]
+            rate = rate + east_coef[v] * roll(u[v], -1, 1) + west_coef[v] * roll(u[v], 1, 1)
+            result.append(rate)
+        return result
+
+    def snap(k):
+        half = states[offset + k].reshape(deep, LANES)
+        u = [states[offset + k, v].astype(F32) for v in range(NV)]
+        drive = cosines[pl.ds(offset + k, 1), :] * force
+        mixed = jnp.dot(
+            mixer[:, : 2 * deep],
+            jnp.concatenate([half, half], axis=0),
+            preferred_element_type=F32,
+        )
+        rate = [r + drive for r in linear(u, mixed)]
+        stack = jnp.concatenate(rate, axis=0)
+        high = stack.astype(BF16)
+        low = (stack - high.astype(F32)).astype(BF16)
+        mixed = jnp.dot(
+            mixer, jnp.concatenate([high, high, low], axis=0), preferred_element_type=F32
+        )
+        again = linear(rate, mixed)
+        for v in range(NV):
+            out[k, v] = rate[v] + 0.5 * TIME_STEP * again[v]
+
+    def snaps(step, carry):
+        for i in range(UNROLL):
+            snap(step * UNROLL + i)
+        return carry
+
+    lax.fori_loop(0, count // UNROLL, snaps, 0)
+
+
+def after_kernel(parts, *refs):
+    place, kern, gain, visc, coup, basis, cells, cos_lanes = refs[:8]
+    own_ref, near_ref, sent_ref, last_ref = refs[8:12]
+    bases = refs[12 : 12 + parts]
+    deriv, partial, mixed, raw, cyc0, grooves, ends = refs[12 + parts :]
+    chunks = own_ref.shape[0]
+    passages = kern.shape[0]
+    me = place[0]
+    base = me - lax.rem(me, 2)
+    bits = passages.bit_length() - 2
+    odd = me % 2 == 1
+    speed = cells[0]
+    damping = cells[2]
+    ids = cells[3]
+    half_speed = 0.5 * speed
+    lane = iota((NX, LANES), 1)
+    c16 = lane % 4
+    masks = cycle_masks(ids).astype(BF16)
+    masks_twice = jnp.concatenate([masks, masks], axis=0)
+    scale = 1.0 / math.sqrt(NX * LANES)
+    size = CHUNK * NX
+
+    src = iota((LANES, LANES), 0)
+    dst = iota((LANES, LANES), 1) // 4 * 4
+    mixers = [(src == dst) | (src == dst + 1), (src == dst + 2) | (src == dst + 3)]
+    mixers += [src == dst + 2, src == dst + 1, src == dst + 3, src == dst]
+    mix = jnp.concatenate([jnp.where(m, 1.0, 0.0).astype(BF16) for m in mixers], axis=1)
+    pick_snap = jnp.where(iota((size, LANES), 1) == iota((size, LANES), 0) // NX * 4, 1.0, 0.0)
+    pick_snap = pick_snap.astype(BF16)
+    wide = 4 * NRING * NX
+    same_x = iota((size, wide), 0) % NX == iota((size, wide), 1) % NX
 
     def flat_basis():
-        if chunks == 1:
-            fetch.wait()
         return flat(basis, 0, basis.shape[0])
 
     def unpack_right(t):
@@ -376,7 +414,7 @@
         raw[half:, :] = last_ref[chunk, head:, :].astype(F32)
         summed = sent_ref[chunk, EDGE:head, :].astype(F32)
         summed += last_ref[chunk, EDGE:head, :].astype(F32)
-        coords[chunk] = summed[:8] + summed[8:]
+        partial[chunk, :8, :] = summed[:8] + summed[8:]
         mixed[...] = jnp.dot(raw[...].astype(BF16), mix, preferred_element_type=F32)
 
         def slot(offset):
@@ -484,11 +522,8 @@
         for g in range(NRING):
             value = jnp.where(c16 < 2, west0[g : g + 1], east0[g : g + 1])
             groove_h = jnp.where(ids_h == g, value, groove_h)
-        cos_h = jnp.zeros((NX, LANES), F32)
-        for k in range(CHUNK):
-            cos_h = jnp.where(lane // 4 == k, table[lax.rem(times[first + k], PERIOD)], cos_h)
-        halo = []
-        ours = []
+        cos_h = jnp.concatenate([cos_lanes[chunk]] * 2, axis=0)
+        halo, ours, rates = [], [], []
         for v in range(NV):
             at = slice(8 * v, 8 * v + 8)
             halo.append(jnp.where(c16 < 2, unpack_right(west[at]), unpack_left(east[at])))
@@ -503,58 +538,81 @@
             rate = rate - damp_h * h + gain[v] * groove_h + force_h * cos_h
             for other in range(NV):
                 rate = rate + coup[v, other] * halo[other]
-            halo0[v] = h
-            halo1[v] = h + TIME_STEP * rate
-
-        def flux(u, mixed_u, halos, source, spread):
-            result = []
+            rates.append(rate)
+
+        def columns(field):
+            tiles = [
+                jnp.broadcast_to(field[:, c : c + 1], (NX, LANES))
+                for c in (LANES - 2, LANES - 1, 0, 1)
+            ]
+            return jnp.where(
+                c16 < 2,
+                jnp.where(c16 == 0, tiles[0], tiles[1]),
+                jnp.where(c16 == 2, tiles[2], tiles[3]),
+            )
+
+        def across(t):
+            return jnp.where(c16 == 2, roll(t, 1, 1), roll(t, -1, 1))
+
+        inner = (c16 == 1) | (c16 == 2)
+        signed_speed = columns(half_speed) * jnp.where(c16 < 2, -1.0, 1.0)
+        damp_e = columns(damping)
+        half_step = 0.5 * TIME_STEP
+        shifts = [
+            jnp.where(inner, (visc[v] + signed_speed) * across(halo[v]), 0.0) for v in range(NV)
+        ]
+        for v in range(NV):
+            change = shifts[v]
+            rate = visc[v] * (north_south(change) - 4.0 * change) - damp_e * change
+            for other in range(NV):
+                rate = rate + coup[v, other] * shifts[other]
+            rate = rate + (visc[v] + signed_speed) * across(rates[v])
+            beside = jnp.where(c16 == 0, roll(change, -1, 1), roll(change, 1, 1))
+            outer = (visc[v] + signed_speed) * beside
+            ends[v] = jnp.where(inner, change + half_step * rate, half_step * outer)
+
+        at_ends = (lane < 2) | (lane >= LANES - 2)
+        damp_step = half_step * damping
+        speed_step = half_step * half_speed
+        diffuse = [half_step * visc[v] * gain[v] for v in range(NV)]
+        couple = []
+        for v in range(NV):
+            total = coup[v, 0] * gain[0]
+            for other in range(1, NV):
+                total = total + coup[v, other] * gain[other]
+            couple.append(half_step * total)
+
+        def snap(k, share, index):
+            at = pl.ds(pl.multiple_of(k * NX, NX), NX)
+            m0, m1 = grooves[0, at, :], grooves[1, at, :]
+            e = jnp.where(lane == LANES - 1, 0.0, roll(m0, -1, 1))
+            w = jnp.where(lane == 0, 0.0, roll(m0, 1, 1))
+            spread = 2 * LANES - 4 * k - 2
+            lap = e + w + north_south(m0) - 4.0 * m0
+            own = 0.5 * (m0 + m1) - speed_step * (e - w) - damp_step * m0
             for v in range(NV):
-                h = roll(halos[v], spread, 1)
-                e = roll(jnp.where(lane == 0, h, u[v]), -1, 1)
-                w = roll(jnp.where(lane == LANES - 1, h, u[v]), 1, 1)
-                rate = mixed_u[NX * v : NX * v + NX] + east_coef[v] * e + west_coef[v] * w
-                result.append(rate - damping * u[v] + gain[v] * source[0] + source[1])
-            return result
-
-        def snap(k):
-            half = states[first + k].reshape(NV * NX, LANES)
-            u = [states[first + k, v].astype(F32) for v in range(NV)]
-            drive = table[lax.rem(times[first + k], PERIOD)] * force
-            at = pl.multiple_of(k * NX, NX)
-            spread = 2 * LANES - 4 * k - 2
-            mixed0 = jnp.dot(
-                mixer[:, : 2 * NV * NX],
-                jnp.concatenate([half, half], axis=0),
-                preferred_element_type=F32,
-            )
-            rate0 = flux(u, mixed0, halo0, (grooves[0, pl.ds(at, NX), :], drive), spread)
-            middle = [u[v] + TIME_STEP * rate0[v] for v in range(NV)]
-            stack = jnp.concatenate(middle, axis=0)
-            high = stack.astype(BF16)
-            low = (stack - high.astype(F32)).astype(BF16)
-            mixed1 = jnp.dot(
-                mixer, jnp.concatenate([high, high, low], axis=0), preferred_element_type=F32
-            )
-            rate1 = flux(middle, mixed1, halo1, (grooves[1, pl.ds(at, NX), :], drive), spread)
-            for v in range(NV):
-                deriv[first + k, v] = (0.5 * (rate0[v] + rate1[v])).astype(BF16)
-
-        def snaps(step, carry):
-            for i in range(UNROLL):
-                snap(step * UNROLL + i)
-            return carry
-
-        if chunks == 1:
-            fetch_states.wait()
-        lax.fori_loop(0, CHUNK // UNROLL, snaps, 0)
-        partial[chunk] = project(flat(deriv, first, CHUNK), flat_basis())
+                total = share[index, v] + gain[v] * own + diffuse[v] * lap + couple[v] * m0
+                total = total + jnp.where(at_ends, roll(ends[v], spread, 1), 0.0)
+                deriv[first + k, v] = total.astype(BF16)
+
+        done = 0
+        for share in bases:
+            count = share.shape[0] if chunks == 1 else CHUNK
+
+            def snaps(step, carry, share=share, done=done):
+                for i in range(UNROLL):
+                    k = step * UNROLL + i
+                    snap(done + k, share, k if chunks == 1 else first + k)
+                return carry
+
+            lax.fori_loop(0, count // UNROLL, snaps, 0)
+            done += count
+        partial[chunk, 8:, :] = project(flat(deriv, first, CHUNK), flat_basis())
         return carry
 
     if chunks == 1:
         chunk_step(0, 0)
     else:
-        fetch_states.wait()
-        fetch.wait()
         lax.fori_loop(0, chunks, chunk_step, 0)
 
 
@@ -571,7 +629,9 @@
 NN = (((1,), (0,)), ((), ()))
 
 
-def system_kernel(ridge, modes, coords_ref, kernel_ref, system_ref):
+def system_kernel(ridge, modes, coords_ref, deriv, kernel_ref, system_ref, deriv_out, sem):
+    write = pltpu.make_async_copy(deriv, deriv_out, sem)
+    write.start()
     coords = unpack(coords_ref, modes)
     snaps = coords.shape[0]
     gram = highest(coords, coords, NT)
@@ -581,23 +641,25 @@
     same = iota((snaps, snaps), 0) == iota((snaps, snaps), 1)
     eye = jnp.where(same, 1.0, 0.0)
     system = jnp.concatenate([kernel + ridge * eye, eye], axis=1)
-    system_ref[...] = eliminate(system, range(snaps * 3 // 8))
-
-
-def invert_kernel(modes, system_ref, inverse_ref):
+    system_ref[...] = eliminate(system, range(snaps // 4))
+    write.wait()
+
+
+def invert_kernel(system_ref, out_ref):
     snaps = system_ref.shape[0]
-    system = eliminate(system_ref[...], range(snaps * 3 // 8, snaps))
-    inverse_ref[...] = system[:, snaps:]
+    out_ref[...] = eliminate(system_ref[...], range(snaps // 4, snaps * 5 // 8))
 
 
 def weight_kernel(
-    coords_ref, kernel_ref, inverse_ref, first_ref, second_ref, lin_ref, weights, fit
+    coords_ref, kernel_ref, system_ref, first_ref, second_ref, lin_ref, weights, fit
 ):
+    snaps = kernel_ref.shape[0]
+    inverse = eliminate(system_ref[...], range(snaps * 5 // 8, snaps))[:, snaps:]
     coords = unpack(coords_ref, first_ref.shape[0])
     design = highest(coords, first_ref[...], NN)
     design = design * (highest(coords, second_ref[...], NN) + lin_ref[...])
-    weights[...] = highest(inverse_ref[...], design, NN)
-    fit[...] = highest(kernel_ref[...], inverse_ref[...], NN)
+    weights[...] = highest(inverse, design, NN)
+    fit[...] = highest(kernel_ref[...], inverse, NN)
 
 
 def fit_kernel(
@@ -659,13 +721,20 @@
         states,
         basis,
     )
-    first = pl.pallas_call(
+    first, held, held_basis, cells, cosines, cos_lanes = pl.pallas_call(
         before_kernel,
-        out_shape=jax.ShapeDtypeStruct((chunks, ROWS, LANES), BF16),
+        out_shape=(
+            jax.ShapeDtypeStruct((chunks, ROWS, LANES), BF16),
+            jax.ShapeDtypeStruct(states.shape, BF16),
+            jax.ShapeDtypeStruct(basis.shape, BF16),
+            jax.ShapeDtypeStruct((4, NX, LANES), F32),
+            jax.ShapeDtypeStruct((snaps, LANES), F32),
+            jax.ShapeDtypeStruct((chunks, 8, LANES), F32),
+        ),
         in_specs=[HBM] * len(operands),
-        out_specs=VMEM,
+        out_specs=(VMEM,) * 6,
         scratch_shapes=[pltpu.SMEM(x.shape, x.dtype) for x in operands[:5]]
-        + [pltpu.VMEM(x.shape, x.dtype) for x in operands[5:]]
+        + [pltpu.VMEM(x.shape, x.dtype) for x in operands[5:9]]
         + [
             pltpu.VMEM((3 * CHUNK * NX, LANES), BF16),
             pltpu.SemaphoreType.DMA((len(operands),)),
@@ -678,65 +747,112 @@
     edges_shape = jax.ShapeDtypeStruct((chunks, 2 * EDGE, LANES), BF16)
     head = EDGE + COORD
 
-    def glue(kernel, name, rows, *args):
+    def glue(kernel, name, rows, *args, more=True):
+        outs = (jax.ShapeDtypeStruct((chunks, rows, LANES), BF16), edges_shape)
         return pl.pallas_call(
             kernel,
-            out_shape=(jax.ShapeDtypeStruct((chunks, rows, LANES), BF16), edges_shape),
+            out_shape=outs if more else outs[:1],
             in_specs=[SMEM] + [VMEM] * len(args),
-            out_specs=(VMEM, VMEM),
+            out_specs=(VMEM, VMEM) if more else (VMEM,),
             compiler_params=pltpu.CompilerParams(vmem_limit_bytes=16 * 2**20),
             name=name,
         )(place, *args)
 
+    hidden = pl.CostEstimate(flops=2 * 10**9, bytes_accessed=2**20, transcendentals=0)
+    anywhere = pl.BlockSpec(memory_space=pl.ANY)
+    tile = jax.ShapeDtypeStruct((chunks, 8, LANES), F32)
+    coords = pl.pallas_call(
+        coords_kernel,
+        out_shape=tile,
+        in_specs=[VMEM, VMEM, anywhere],
+        out_specs=VMEM,
+        cost_estimate=hidden,
+        compiler_params=pltpu.CompilerParams(vmem_limit_bytes=24 * 2**20),
+        name="coords",
+    )(held, held_basis, first)
+    near, coords = lax.optimization_barrier((near, coords))
+
+    def local(offset, count, after):
+        return pl.pallas_call(
+            functools.partial(local_kernel, offset),
+            out_shape=jax.ShapeDtypeStruct((count,) + states.shape[1:], F32),
+            in_specs=[VMEM] * 6 + [anywhere],
+            out_specs=VMEM,
+            cost_estimate=hidden,
+            compiler_params=pltpu.CompilerParams(vmem_limit_bytes=24 * 2**20),
+            name="local",
+        )(
+            held,
+            cells,
+            cosines,
+            mixer,
+            east_coef,
+            west_coef,
+            after,
+        )
+
     start = functools.partial(start_kernel, bits - 1)
-    message, edges = glue(start, "start", head + 2 * BLOB, first, near)
+    message, edges = glue(start, "start", head + 2 * BLOB, first, near, coords)
+    mixer, east_coef, west_coef = pl.pallas_call(
+        prepare_kernel,
+        out_shape=(
+            jax.ShapeDtypeStruct((NV * NX, 3 * NV * NX), BF16),
+            jax.ShapeDtypeStruct((NV, NX, LANES), F32),
+            jax.ShapeDtypeStruct((NV, NX, LANES), F32),
+        ),
+        in_specs=[SMEM] * 4 + [VMEM, anywhere],
+        out_specs=(VMEM, VMEM, VMEM),
+        cost_estimate=hidden,
+        compiler_params=pltpu.CompilerParams(vmem_limit_bytes=16 * 2**20),
+        name="prepare",
+    )(viscosity, coupling, groove_kernel, groove_gain, cells, message)
+    shares = [4, 12, 16] if chunks == 1 and bits == 3 else [snaps]
+    bases, offset = [], 0
     for bit in range(bits - 1, -1, -1):
         got = swap_chip(message, 2 << bit)
+        if shares:
+            count = shares.pop(0)
+            base = local(offset, count, message)
+            got, base = lax.optimization_barrier((got, base))
+            bases.append(base)
+            offset += count
         if bit:
             rows = 2 * message.shape[1] - head
             step = functools.partial(next_kernel, bit - 1)
-            message, edges = glue(step, "next", rows, message, got, edges)
-
-    tile = jax.ShapeDtypeStruct((chunks, 8, LANES), F32)
-    derivative, partial, coords = pl.pallas_call(
-        after_kernel,
-        out_shape=(jax.ShapeDtypeStruct(states.shape, BF16), tile, tile),
-        in_specs=[SMEM] * 8 + [HBM, HBM] + [VMEM] * 8,
-        out_specs=(VMEM, VMEM, VMEM),
+            message, *edges = glue(step, "next", rows, message, got, edges, more=bit > 1)
+            edges = edges[0] if edges else None
+
+    derivative, partial = pl.pallas_call(
+        functools.partial(after_kernel, len(bases)),
+        out_shape=(
+            jax.ShapeDtypeStruct(states.shape, BF16),
+            jax.ShapeDtypeStruct((chunks, 16, LANES), F32),
+        ),
+        in_specs=[SMEM] * 5 + [VMEM] * (7 + len(bases)),
+        out_specs=(VMEM, VMEM),
         scratch_shapes=[
             pltpu.VMEM((passages * BLOB, 6 * LANES), F32),
             pltpu.VMEM((passages * BLOB, LANES), F32),
             pltpu.VMEM((passages * 8, LANES), F32),
             pltpu.VMEM((2, CHUNK * NX, LANES), F32),
             pltpu.VMEM((NV, NX, LANES), F32),
-            pltpu.VMEM((NV, NX, LANES), F32),
-            pltpu.VMEM((NV, NX, LANES), F32),
-            pltpu.VMEM((NV, NX, LANES), F32),
-            pltpu.VMEM(basis.shape, BF16),
-            pltpu.VMEM(states.shape, BF16),
-            pltpu.SemaphoreType.DMA((2,)),
         ],
         compiler_params=pltpu.CompilerParams(vmem_limit_bytes=32 * 2**20),
         name="after",
     )(
-        snapshot_times,
-        pert_ids,
         place,
         groove_kernel,
         groove_gain,
         viscosity,
         coupling,
-        table,
-        pltpu.with_memory_space_constraint(states, pltpu.HBM),
-        pltpu.with_memory_space_constraint(basis, pltpu.HBM),
-        pert_table,
-        cycle_ids,
-        speed,
-        force_amp,
+        held_basis,
+        cells,
+        cos_lanes,
         first,
         near,
         message,
         got,
+        *bases,
     )
 
     upper_first, upper_second = np.triu_indices(modes)
@@ -755,25 +871,33 @@
             out_shape=tuple(jax.ShapeDtypeStruct(shape, F32) for shape in outs),
             in_specs=[VMEM] * len(args),
             out_specs=tuple(VMEM for _ in outs),
-            cost_estimate=pl.CostEstimate(flops=10**8, bytes_accessed=2**20, transcendentals=0),
+            cost_estimate=hidden,
             compiler_params=pltpu.CompilerParams(vmem_limit_bytes=16 * 2**20),
             name=name,
         )(*args)
 
     total = partial + swap(partial, 1)
-    kernel, system = small(
+    coords, total, derivative = lax.optimization_barrier((total[:, :8], total[:, 8:], derivative))
+    kernel, system, derivative = pl.pallas_call(
         functools.partial(system_kernel, RIDGE_FACTOR * snaps, modes),
-        "system",
-        [(snaps, snaps), (snaps, 2 * snaps)],
-        coords,
-    )
+        out_shape=(
+            jax.ShapeDtypeStruct((snaps, snaps), F32),
+            jax.ShapeDtypeStruct((snaps, 2 * snaps), F32),
+            jax.ShapeDtypeStruct(states.shape, BF16),
+        ),
+        in_specs=[VMEM, VMEM],
+        out_specs=(VMEM, VMEM, HBM),
+        scratch_shapes=[pltpu.SemaphoreType.DMA],
+        cost_estimate=hidden,
+        compiler_params=pltpu.CompilerParams(vmem_limit_bytes=16 * 2**20),
+        name="system",
+    )(coords, derivative)
     for r in range(1, rounds):
         got = swap_chip(total, 1 << r)
         if r == 1:
-            total, kernel, system = lax.optimization_barrier((total + got, kernel, system))
-            (inverse,) = small(
-                functools.partial(invert_kernel, modes), "invert", [(snaps, snaps)], system
-            )
+            got, kernel, system = lax.optimization_barrier((got, kernel, system))
+            total = total + got
+            (inverse,) = small(invert_kernel, "invert", [(snaps, 2 * snaps)], system)
         elif r == 2:
             total, inverse = lax.optimization_barrier((total + got, inverse))
             weights, fit = small(

time: 41.1 us -> 34.2 us (0.83)
  waiting for transfers between devices: 7.89 us -> 2.66 us
  starting transfers between devices: 14.6 us -> 13.5 us
  Pallas kernels: 16.9 us -> 16.3 us
    ppermute x8, waiting for transfers between devices: 7.89 us -> 2.66 us  [swap(): return lax.ppermute(value, 'passage', pairs)]
    pallas_call x3 -> x2, Pallas kernels: 3.45 us -> 2.29 us  [small(): pl.pallas_call(kernel, out_shape=tuple((jax.ShapeDtypeStruct(shape, F32)...]
    ppermute x8, starting transfers between devices: 14.6 us -> 13.5 us  [swap(): return lax.ppermute(value, 'passage', pairs)]
    pallas_call x5 -> x11, Pallas kernels: 12.4 us -> 13.1 us  [the longest x3 4.37 us: local(): pl.pallas_call(functools.partial(local_kernel, offset), out_shape=jax.Sha...]
  transfers between devices with their start and end apart: 8 -> 8, of which waited for: 7 -> 5; matrix products, arithmetic and copies ran while one was open for 0% -> 0% of each run, Pallas kernels for 8% -> 27%
where the time goes in v4:
time: 34.2 us; the launch traced here: 34 us
  Pallas kernels  16.3 us (48%)
  starting transfers between devices  13.5 us (39%)
  waiting for transfers between devices  2.66 us (8%)
  between operations  1.41 us (4%)
    ppermute x8, starting transfers between devices, swap(): return lax.ppermute(value, 'passage', pairs)  13.5 us
    pallas_call x3, Pallas kernels, local(): pl.pallas_call(functools.partial(local_kernel, offset), out_shape=jax.Sha...  4.37 us
    pallas_call x1, Pallas kernels, body(): pl.pallas_call(functools.partial(after_kernel, len(bases)), out_shape=(ja...  3.87 us
    ppermute x8, waiting for transfers between devices, swap(): return lax.ppermute(value, 'passage', pairs)  2.66 us
    pallas_call x2, Pallas kernels, small(): pl.pallas_call(kernel, out_shape=tuple((jax.ShapeDtypeStruct(shape, F32)...  2.29 us
    pallas_call x1, Pallas kernels, body(): pl.pallas_call(before_kernel, out_shape=(jax.ShapeDtypeStruct((chunks, RO...  2.23 us
    pallas_call x1, Pallas kernels, body(): pl.pallas_call(fit_kernel, out_shape=(jax.ShapeDtypeStruct((each, 2 * mod...  1 us
    pallas_call x1, Pallas kernels, body(): pl.pallas_call(coords_kernel, out_shape=tile, in_specs=[VMEM, VMEM, anywh...  0.95 us
  transfers between devices with their start and end apart: 8, of which 5 were waited for; matrix products, arithmetic and copies ran while one was open for 0% of the time, Pallas kernels for 27%

profile of v4, /device:TPU:0, one launch (start us, length us, event | category | flops | bytes accessed | tf_op | source)
XLA Modules:
  0.0 34.0 jit_solution(12884162991501897864)
XLA Ops:
  1.3 2.2 %before.1 = (bf16[1,112,128]{2,1,0:T(8,128)(2,1)S(1)}, bf16[32,5,16,128]{3,2,1,0:T(8,128)(2,1)S(1)}, bf16[32,5,16,128]{3,2,1,0:T(8,128)(2,1)S(1)}, f32[4,16,128]...) custom-call(s32[32]{0:T(128)} %refs_0_.1, s32[1]{0:T(128)S(6)} %copy.20.refs_1_, f32[5]{0:T(128)} %refs_3_.3, ...), custom_call_target="tpu_custom_call" | custom-call | tf_op jit(solution)/shard_map/before/pallas_call | solution.py:724
  3.5 0.5 %collective-permute-start = (bf16[1,112,128]{2,1,0:T(8,128)(2,1)S(1)}, bf16[1,112,128]{2,1,0:T(8,128)(2,1)S(1)}, u32[]{:S(2)}, u32[]{:S(2)}) collective-permute-start(bf16[1,112,128]{2,1,0:T(8,128)(2,1)S(1)} %get-tuple-element.46.after.first.refs_8_), channel_id=1, source_target_pairs={{0,1},{1,0},{2,3},{3,2},{4,5},{5,4},{6,7},{7,6},{8,9},{9,8},{10,11... | collective-permute-start | bytes 86024 | tf_op jit(solution)/shard_map/ppermute | solution.py:706
  4.0 0.9 %coords.1 = f32[1,8,128]{2,1,0:T(8,128)S(1)} custom-call(bf16[32,5,16,128]{3,2,1,0:T(8,128)(2,1)S(1)} %get-tuple-element.47.states, bf16[32,5,16,128]{3,2,1,0:T(8,128)(2,1)S(1)} %get-tuple-element.43.basis.refs_5_, bf16[1,112,128]{2,1,0:T(8,128)(2,1)S(1)} %get-tuple-element.46.after.first.refs_8_), custom_call_target="tpu_custom_call" | custom-call | flops 2000000000 | bytes 1048576 | tf_op jit(solution)/shard_map/coords/pallas_call | solution.py:764
  5.1 3.8 %collective-permute-start.1 = (bf16[1,96,128]{2,1,0:T(8,128)(2,1)S(1)}, bf16[1,96,128]{2,1,0:T(8,128)(2,1)S(1)}, u32[]{:S(2)}, u32[]{:S(2)}) collective-permute-start(bf16[1,96,128]{2,1,0:T(8,128)(2,1)S(1)} %get-tuple-element.50.after.sent), channel_id=1, source_target_pairs={{0,9},{1,8},{2,11},{3,10},{4,13},{5,12},{6,15},{7,14},{8,1},{9,0},... | collective-permute-start | bytes 73736 | tf_op jit(solution)/shard_map/ppermute | solution.py:706
  8.8 0.7 %prepare.1 = (bf16[80,240]{1,0:T(8,128)(2,1)S(1)}, f32[5,16,128]{2,1,0:T(8,128)S(1)}, f32[5,16,128]{2,1,0:T(8,128)S(1)}) custom-call(f32[5]{0:T(128)S(1)} %copy-done.1, f32[5,5]{1,0:T(8,128)S(1)} %copy-done, f32[16]{0:T(128)S(1)} %copy-done.2, f32[5]{0:T(128)S(1)} %copy-done.3, f32[4,16,128]{2,1,0:T(8,128)S(1)} %get-tuple-element.44.cells.refs_6_, ...), custom_call_target="tpu_custom_call" | custom-call | flops 2000000000 | bytes 1048576 | tf_op jit(solution)/shard_map/prepare/pallas_call | solution.py:796
  9.5 0.5 %local.3.refs_12_ = f32[4,5,16,128]{3,2,1,0:T(8,128)S(1)} custom-call(bf16[32,5,16,128]{3,2,1,0:T(8,128)(2,1)S(1)} %get-tuple-element.47.states, f32[4,16,128]{2,1,0:T(8,128)S(1)} %get-tuple-element.44.cells.refs_6_, f32[32,128]{1,0:T(8,128)S(1)} %get-tuple-element.51.cosines, bf16[80,240]{1,0:T(8,128)(2,1)S(1)} %get-tuple-element.52.mixer_ref, ...), custom_call_target="tpu_custom_call" | custom-call | flops 2000000000 | bytes 1048576 | tf_op jit(solution)/shard_map/local/pallas_call | solution.py:776
  10.1 0.3 collective-permute-done.1.got
  10.4 1.7 %collective-permute-start.2 = (bf16[1,128,128]{2,1,0:T(8,128)(2,1)S(1)}, bf16[1,128,128]{2,1,0:T(8,128)(2,1)S(1)}, u32[]{:S(2)}, u32[]{:S(2)}) collective-permute-start(bf16[1,128,128]{2,1,0:T(8,128)(2,1)S(1)} %get-tuple-element.57.after.sent), channel_id=1, source_target_pairs={{0,5},{1,4},{2,7},{3,6},{4,1},{5,0},{6,3},{7,2},{8,13},{9,12},{10,... | collective-permute-start | bytes 98312 | tf_op jit(solution)/shard_map/ppermute | solution.py:706
  12.0 1.6 %local.4.refs_13_ = f32[12,5,16,128]{3,2,1,0:T(8,128)S(1)} custom-call(bf16[32,5,16,128]{3,2,1,0:T(8,128)(2,1)S(1)} %get-tuple-element.47.states, f32[4,16,128]{2,1,0:T(8,128)S(1)} %get-tuple-element.44.cells.refs_6_, f32[32,128]{1,0:T(8,128)S(1)} %get-tuple-element.51.cosines, bf16[80,240]{1,0:T(8,128)(2,1)S(1)} %get-tuple-element.52.mixer_ref, ...), custom_call_target="tpu_custom_call" | custom-call | flops 2000000000 | bytes 1048576 | tf_op jit(solution)/shard_map/local/pallas_call | solution.py:776
  13.7 0.1 collective-permute-done.2.got
  13.8 1.6 %collective-permute-start.3 = (bf16[1,192,128]{2,1,0:T(8,128)(2,1)S(1)}, bf16[1,192,128]{2,1,0:T(8,128)(2,1)S(1)}, u32[]{:S(2)}, u32[]{:S(2)}) collective-permute-start(bf16[1,192,128]{2,1,0:T(8,128)(2,1)S(1)} %next.3.after.refs_10_), channel_id=1, source_target_pairs={{0,3},{1,2},{2,1},{3,0},{4,7},{5,6},{6,5},{7,4},{8,11},{9,10},{10,... | collective-permute-start | bytes 147464 | tf_op jit(solution)/shard_map/ppermute | solution.py:706
  15.4 2.2 %local.5.refs_14_ = f32[16,5,16,128]{3,2,1,0:T(8,128)S(1)} custom-call(bf16[32,5,16,128]{3,2,1,0:T(8,128)(2,1)S(1)} %get-tuple-element.47.states, f32[4,16,128]{2,1,0:T(8,128)S(1)} %get-tuple-element.44.cells.refs_6_, f32[32,128]{1,0:T(8,128)S(1)} %get-tuple-element.51.cosines, bf16[80,240]{1,0:T(8,128)(2,1)S(1)} %get-tuple-element.52.mixer_ref, ...), custom_call_target="tpu_custom_call" | custom-call | flops 2000000000 | bytes 1048576 | tf_op jit(solution)/shard_map/local/pallas_call | solution.py:776
  17.6 3.9 %after.1 = (bf16[32,5,16,128]{3,2,1,0:T(8,128)(2,1)S(1)}, f32[1,16,128]{2,1,0:T(8,128)S(1)}) custom-call(s32[1]{0:T(128)} %bitcast.place.refs_0_, f32[16]{0:T(128)S(1)} %copy-done.2, f32[5]{0:T(128)S(1)} %copy-done.3, f32[5]{0:T(128)S(1)} %copy-done.1, f32[5,5]{1,0:T(8,128)S(1)} %copy-done, bf16[32,5,16,128]{3,2,1,0:T(8,128)(2,1)S(1)} %get-tuple-element.43.basis.refs_5_, ...), custom_call_target="tpu_custom_call" | custom-call | tf_op jit(solution)/shard_map/after/pallas_call | solution.py:825
  21.5 0.3 collective-permute-start.4
  21.7 0.9 %collective-permute-done.4 = f32[1,16,128]{2,1,0:T(8,128)S(1)} collective-permute-done((f32[1,16,128]{2,1,0:T(8,128)S(1)}, f32[1,16,128]{2,1,0:T(8,128)S(1)}, u32[]{:S(2)}, u32[]{:S(2)}) %collective-permute-start.4) | collective-permute-done | bytes 8224 | tf_op jit(solution)/shard_map/ppermute | solution.py:706
  22.7 1.4 %collective-permute-start.5 = (f32[1,8,128]{2,1,0:T(8,128)S(1)}, f32[1,8,128]{2,1,0:T(8,128)S(1)}, u32[]{:S(2)}, u32[]{:S(2)}) collective-permute-start(f32[1,8,128]{2,1,0:T(8,128)S(1)} %get-tuple-element.69), channel_id=1, source_target_pairs={{0,3},{1,2},{2,1},{3,0},{4,7},{5,6},{6,5},{7,4},{8,11},{9,10},{10,... | collective-permute-start | bytes 12296 | tf_op jit(solution)/shard_map/ppermute | solution.py:706
  24.1 0.9 %system.1 = (f32[32,32]{1,0:T(8,128)S(1)}, f32[32,64]{1,0:T(8,128)S(1)}, bf16[32,5,16,128]{3,2,1,0:T(8,128)(2,1)}) custom-call(f32[1,8,128]{2,1,0:T(8,128)S(1)} %get-tuple-element.66.coords_ref, bf16[32,5,16,128]{3,2,1,0:T(8,128)(2,1)S(1)} %get-tuple-element.67.deriv), custom_call_target="tpu_custom_call" | custom-call | flops 2000000000 | bytes 1048576 | tf_op jit(solution)/shard_map/system/pallas_call | solution.py:881
  25.0 0.7 %collective-permute-done.5 = f32[1,8,128]{2,1,0:T(8,128)S(1)} collective-permute-done((f32[1,8,128]{2,1,0:T(8,128)S(1)}, f32[1,8,128]{2,1,0:T(8,128)S(1)}, u32[]{:S(2)}, u32[]{:S(2)}) %collective-permute-start.5) | collective-permute-done | bytes 4128 | tf_op jit(solution)/shard_map/ppermute | solution.py:706
  25.7 1.5 %collective-permute-start.6 = (f32[1,8,128]{2,1,0:T(8,128)S(1)}, f32[1,8,128]{2,1,0:T(8,128)S(1)}, u32[]{:S(2)}, u32[]{:S(2)}) collective-permute-start(f32[1,8,128]{2,1,0:T(8,128)S(1)} %add.13), channel_id=1, source_target_pairs={{0,5},{1,4},{2,7},{3,6},{4,1},{5,0},{6,3},{7,2},{8,13},{9,12},{10,... | collective-permute-start | bytes 12296 | tf_op jit(solution)/shard_map/ppermute | solution.py:706
  27.2 1.0 %invert.1.system_ref = f32[32,64]{1,0:T(8,128)S(1)} custom-call(f32[32,64]{1,0:T(8,128)S(1)} %get-tuple-element.73.system_ref), custom_call_target="tpu_custom_call" | custom-call | flops 2000000000 | bytes 1048576 | tf_op jit(solution)/shard_map/invert/pallas_call | solution.py:869
  28.2 0.6 %collective-permute-done.6 = f32[1,8,128]{2,1,0:T(8,128)S(1)} collective-permute-done((f32[1,8,128]{2,1,0:T(8,128)S(1)}, f32[1,8,128]{2,1,0:T(8,128)S(1)}, u32[]{:S(2)}, u32[]{:S(2)}) %collective-permute-start.6) | collective-permute-done | bytes 4128 | tf_op jit(solution)/shard_map/ppermute | solution.py:706
  28.8 2.8 %collective-permute-start.7 = (f32[1,8,128]{2,1,0:T(8,128)S(1)}, f32[1,8,128]{2,1,0:T(8,128)S(1)}, u32[]{:S(2)}, u32[]{:S(2)}) collective-permute-start(f32[1,8,128]{2,1,0:T(8,128)S(1)} %add.14), channel_id=1, source_target_pairs={{0,9},{1,8},{2,11},{3,10},{4,13},{5,12},{6,15},{7,14},{8,1},{9,0},... | collective-permute-start | bytes 12296 | tf_op jit(solution)/shard_map/ppermute | solution.py:706
  31.6 1.3 %weights.1 = (f32[32,560]{1,0:T(8,128)S(1)}, f32[32,32]{1,0:T(8,128)S(1)}) custom-call(f32[1,8,128]{2,1,0:T(8,128)S(1)} %get-tuple-element.66.coords_ref, f32[32,32]{1,0:T(8,128)S(1)} %get-tuple-element.75.kernel_ref, f32[32,64]{1,0:T(8,128)S(1)} %invert.1.system_ref, f32[32,560]{1,0:T(8,128)S(1)} %copy-done.5, f32[32,560]{1,0:T(8,128)S(1)} %copy-done.4, ...), custom_call_target="tpu_custom_call" | custom-call | flops 2000000000 | bytes 1048576 | tf_op jit(solution)/shard_map/weights/pallas_call | solution.py:869
  33.0 1.0 %fit.1 = (f32[2,64]{1,0:T(2,128)}, f32[32,560]{1,0:T(8,128)}, f32[2,32]{1,0:T(2,128)}) custom-call(s32[1]{0:T(128)} %bitcast.place.refs_0_, f32[1,8,128]{2,1,0:T(8,128)S(1)} %add.15.rates_ref, f32[1,8,128]{2,1,0:T(8,128)S(1)} %get-tuple-element.66.coords_ref, f32[32,560]{1,0:T(8,128)S(1)} %get-tuple-element.77.weights, f32[32,32]{1,0:T(8,128)S(1)} %get-tuple-element.78.fit), custom_call_target="tpu_custom_call" | custom-call | tf_op jit(solution)/shard_map/fit/pallas_call | solution.py:917
  (25 shorter events, 0.1 us)
Async XLA Ops:
  3.5 1.5 %collective-permute-start = (bf16[1,112,128]{2,1,0:T(8,128)(2,1)S(1)}, bf16[1,112,128]{2,1,0:T(8,128)(2,1)S(1)}, u32[]{:S(2)}, u32[]{:S(2)}) collective-permute-start(bf16[1,112,128]{2,1,0:T(8,128)(2,1)S(1)} %get-tuple-element.46.after.first.refs_8_), channel_id=1, source_target_pairs={{0,1},{1,0},{2,3},{3,2},{4,5},{5,4},{6,7},{7,6},{8,9},{9,8},{10,11... | collective-permute-start | bytes 86024 | tf_op jit(solution)/shard_map/ppermute | solution.py:706
  5.0 3.8 %copy-start = (f32[5,5]{1,0:T(8,128)S(1)}, f32[5,5]{1,0:T(8,128)}, u32[]{:S(2)}) copy-start(f32[5,5]{1,0:T(8,128)} %refs_4_.2) | copy-start | bytes 304
  5.0 3.8 %copy-start.1 = (f32[5]{0:T(128)S(1)}, f32[5]{0:T(128)}, u32[]{:S(2)}) copy-start(f32[5]{0:T(128)} %refs_3_.3) | copy-start | bytes 64
  5.0 3.8 %copy-start.2 = (f32[16]{0:T(128)S(1)}, f32[16]{0:T(128)}, u32[]{:S(2)}) copy-start(f32[16]{0:T(128)} %refs_1_.2) | copy-start | bytes 196
  5.0 3.8 %copy-start.3 = (f32[5]{0:T(128)S(1)}, f32[5]{0:T(128)}, u32[]{:S(2)}) copy-start(f32[5]{0:T(128)} %refs_2_.3) | copy-start | bytes 64
  5.1 5.3 %collective-permute-start.1 = (bf16[1,96,128]{2,1,0:T(8,128)(2,1)S(1)}, bf16[1,96,128]{2,1,0:T(8,128)(2,1)S(1)}, u32[]{:S(2)}, u32[]{:S(2)}) collective-permute-start(bf16[1,96,128]{2,1,0:T(8,128)(2,1)S(1)} %get-tuple-element.50.after.sent), channel_id=1, source_target_pairs={{0,9},{1,8},{2,11},{3,10},{4,13},{5,12},{6,15},{7,14},{8,1},{9,0},... | collective-permute-start | bytes 73736 | tf_op jit(solution)/shard_map/ppermute | solution.py:706
  10.4 3.4 %collective-permute-start.2 = (bf16[1,128,128]{2,1,0:T(8,128)(2,1)S(1)}, bf16[1,128,128]{2,1,0:T(8,128)(2,1)S(1)}, u32[]{:S(2)}, u32[]{:S(2)}) collective-permute-start(bf16[1,128,128]{2,1,0:T(8,128)(2,1)S(1)} %get-tuple-element.57.after.sent), channel_id=1, source_target_pairs={{0,5},{1,4},{2,7},{3,6},{4,1},{5,0},{6,3},{7,2},{8,13},{9,12},{10,... | collective-permute-start | bytes 98312 | tf_op jit(solution)/shard_map/ppermute | solution.py:706
  13.8 3.8 %collective-permute-start.3 = (bf16[1,192,128]{2,1,0:T(8,128)(2,1)S(1)}, bf16[1,192,128]{2,1,0:T(8,128)(2,1)S(1)}, u32[]{:S(2)}, u32[]{:S(2)}) collective-permute-start(bf16[1,192,128]{2,1,0:T(8,128)(2,1)S(1)} %next.3.after.refs_10_), channel_id=1, source_target_pairs={{0,3},{1,2},{2,1},{3,0},{4,7},{5,6},{6,5},{7,4},{8,11},{9,10},{10,... | collective-permute-start | bytes 147464 | tf_op jit(solution)/shard_map/ppermute | solution.py:706
  21.5 1.2 %collective-permute-start.4 = (f32[1,16,128]{2,1,0:T(8,128)S(1)}, f32[1,16,128]{2,1,0:T(8,128)S(1)}, u32[]{:S(2)}, u32[]{:S(2)}) collective-permute-start(f32[1,16,128]{2,1,0:T(8,128)S(1)} %get-tuple-element.64), channel_id=1, source_target_pairs={{0,1},{1,0},{2,3},{3,2},{4,5},{5,4},{6,7},{7,6},{8,9},{9,8},{10,11... | collective-permute-start | bytes 24584 | tf_op jit(solution)/shard_map/ppermute | solution.py:706
  22.7 3.0 %collective-permute-start.5 = (f32[1,8,128]{2,1,0:T(8,128)S(1)}, f32[1,8,128]{2,1,0:T(8,128)S(1)}, u32[]{:S(2)}, u32[]{:S(2)}) collective-permute-start(f32[1,8,128]{2,1,0:T(8,128)S(1)} %get-tuple-element.69), channel_id=1, source_target_pairs={{0,3},{1,2},{2,1},{3,0},{4,7},{5,6},{6,5},{7,4},{8,11},{9,10},{10,... | collective-permute-start | bytes 12296 | tf_op jit(solution)/shard_map/ppermute | solution.py:706
  25.7 5.9 %copy-start.4 = (f32[32,560]{1,0:T(8,128)S(1)}, f32[32,560]{1,0:T(8,128)}, u32[]{:S(2)}) copy-start(f32[32,560]{1,0:T(8,128)} %constant.14.clone.second_ref) | copy-start | bytes 215044
  25.7 5.9 %copy-start.5 = (f32[32,560]{1,0:T(8,128)S(1)}, f32[32,560]{1,0:T(8,128)}, u32[]{:S(2)}) copy-start(f32[32,560]{1,0:T(8,128)} %constant.13.clone.first_ref) | copy-start | bytes 215044
  25.7 3.1 %collective-permute-start.6 = (f32[1,8,128]{2,1,0:T(8,128)S(1)}, f32[1,8,128]{2,1,0:T(8,128)S(1)}, u32[]{:S(2)}, u32[]{:S(2)}) collective-permute-start(f32[1,8,128]{2,1,0:T(8,128)S(1)} %add.13), channel_id=1, source_target_pairs={{0,5},{1,4},{2,7},{3,6},{4,1},{5,0},{6,3},{7,2},{8,13},{9,12},{10,... | collective-permute-start | bytes 12296 | tf_op jit(solution)/shard_map/ppermute | solution.py:706
  28.2 3.5 %copy-start.6 = (f32[1,560]{1,0:T(1,128)S(1)}, f32[1,560]{1,0:T(1,128)}, u32[]{:S(2)}) copy-start(f32[1,560]{1,0:T(1,128)} %constant.15.clone.lin_ref) | copy-start | bytes 6724
  28.8 4.1 %collective-permute-start.7 = (f32[1,8,128]{2,1,0:T(8,128)S(1)}, f32[1,8,128]{2,1,0:T(8,128)S(1)}, u32[]{:S(2)}, u32[]{:S(2)}) collective-permute-start(f32[1,8,128]{2,1,0:T(8,128)S(1)} %add.14), channel_id=1, source_target_pairs={{0,9},{1,8},{2,11},{3,10},{4,13},{5,12},{6,15},{7,14},{8,1},{9,0},... | collective-permute-start | bytes 12296 | tf_op jit(solution)/shard_map/ppermute | solution.py:706

commit v5 on v4

--- a/solution.py
+++ b/solution.py
@@ -358,11 +358,11 @@
             out[k, v] = rate[v] + 0.5 * TIME_STEP * again[v]
 
     def snaps(step, carry):
-        for i in range(UNROLL):
-            snap(step * UNROLL + i)
+        for i in range(8):
+            snap(step * 8 + i)
         return carry
 
-    lax.fori_loop(0, count // UNROLL, snaps, 0)
+    lax.fori_loop(0, count // 8, snaps, 0)
 
 
 def after_kernel(parts, *refs):
@@ -600,12 +600,12 @@
             count = share.shape[0] if chunks == 1 else CHUNK
 
             def snaps(step, carry, share=share, done=done):
-                for i in range(UNROLL):
-                    k = step * UNROLL + i
+                for i in range(count):
+                    k = step * count + i
                     snap(done + k, share, k if chunks == 1 else first + k)
                 return carry
 
-            lax.fori_loop(0, count // UNROLL, snaps, 0)
+            lax.fori_loop(0, count // count, snaps, 0)
             done += count
         partial[chunk, 8:, :] = project(flat(deriv, first, CHUNK), flat_basis())
         return carry
@@ -806,7 +806,7 @@
         compiler_params=pltpu.CompilerParams(vmem_limit_bytes=16 * 2**20),
         name="prepare",
     )(viscosity, coupling, groove_kernel, groove_gain, cells, message)
-    shares = [4, 12, 16] if chunks == 1 and bits == 3 else [snaps]
+    shares = [8, 8, 16] if chunks == 1 and bits == 3 else [snaps]
     bases, offset = [], 0
     for bit in range(bits - 1, -1, -1):
         got = swap_chip(message, 2 << bit)

time: 34.2 us -> 33.2 us (0.971)
  Pallas kernels: 16.3 us -> 14.8 us
  waiting for transfers between devices: 2.66 us -> 3.91 us
  starting transfers between devices: 13.5 us -> 12.9 us
    ppermute x8, waiting for transfers between devices: 2.66 us -> 3.91 us  [swap(): return lax.ppermute(value, 'passage', pairs)]
    pallas_call x1, Pallas kernels: 3.87 us -> 2.86 us  [body(): pl.pallas_call(functools.partial(after_kernel, len(bases)), out_shape=(ja...]
    ppermute x8, starting transfers between devices: 13.5 us -> 12.9 us  [swap(): return lax.ppermute(value, 'passage', pairs)]
    pallas_call x3, Pallas kernels: 4.37 us -> 3.78 us  [local(): pl.pallas_call(functools.partial(local_kernel, offset), out_shape=jax.Sha...]
  transfers between devices with their start and end apart: 8 -> 8, of which waited for: 5 -> 5; matrix products, arithmetic and copies ran while one was open for 0% -> 0% of each run, Pallas kernels for 27% -> 26%
where the time goes in v5:
time: 33.2 us; the launch traced here: 33 us
  Pallas kernels  14.8 us (45%)
  starting transfers between devices  12.9 us (39%)
  waiting for transfers between devices  3.91 us (12%)
  between operations  1.42 us (4%)
    ppermute x8, starting transfers between devices, swap(): return lax.ppermute(value, 'passage', pairs)  12.9 us
    ppermute x8, waiting for transfers between devices, swap(): return lax.ppermute(value, 'passage', pairs)  3.91 us
    pallas_call x3, Pallas kernels, local(): pl.pallas_call(functools.partial(local_kernel, offset), out_shape=jax.Sha...  3.78 us
    pallas_call x1, Pallas kernels, body(): pl.pallas_call(functools.partial(after_kernel, len(bases)), out_shape=(ja...  2.86 us
    pallas_call x2, Pallas kernels, small(): pl.pallas_call(kernel, out_shape=tuple((jax.ShapeDtypeStruct(shape, F32)...  2.29 us
    pallas_call x1, Pallas kernels, body(): pl.pallas_call(before_kernel, out_shape=(jax.ShapeDtypeStruct((chunks, RO...  2.23 us
    pallas_call x1, Pallas kernels, body(): pl.pallas_call(fit_kernel, out_shape=(jax.ShapeDtypeStruct((each, 2 * mod...  1 us
    pallas_call x1, Pallas kernels, body(): pl.pallas_call(coords_kernel, out_shape=tile, in_specs=[VMEM, VMEM, anywh...  0.95 us
  transfers between devices with their start and end apart: 8, of which 5 were waited for; matrix products, arithmetic and copies ran while one was open for 0% of the time, Pallas kernels for 26%

profile of v5, /device:TPU:0, one launch (start us, length us, event | category | flops | bytes accessed | tf_op | source)
XLA Modules:
  0.0 33.0 jit_solution(3586707451114277148)
XLA Ops:
  1.3 2.2 %before.1 = (bf16[1,112,128]{2,1,0:T(8,128)(2,1)S(1)}, bf16[32,5,16,128]{3,2,1,0:T(8,128)(2,1)S(1)}, bf16[32,5,16,128]{3,2,1,0:T(8,128)(2,1)S(1)}, f32[4,16,128]...) custom-call(s32[32]{0:T(128)} %refs_0_.1, s32[1]{0:T(128)S(6)} %copy.20.refs_1_, f32[5]{0:T(128)} %refs_3_.3, ...), custom_call_target="tpu_custom_call" | custom-call | tf_op jit(solution)/shard_map/before/pallas_call | solution.py:724
  3.5 0.5 %collective-permute-start = (bf16[1,112,128]{2,1,0:T(8,128)(2,1)S(1)}, bf16[1,112,128]{2,1,0:T(8,128)(2,1)S(1)}, u32[]{:S(2)}, u32[]{:S(2)}) collective-permute-start(bf16[1,112,128]{2,1,0:T(8,128)(2,1)S(1)} %get-tuple-element.46.after.first.refs_8_), channel_id=1, source_target_pairs={{0,1},{1,0},{2,3},{3,2},{4,5},{5,4},{6,7},{7,6},{8,9},{9,8},{10,11... | collective-permute-start | bytes 86024 | tf_op jit(solution)/shard_map/ppermute | solution.py:706
  4.0 0.9 %coords.1 = f32[1,8,128]{2,1,0:T(8,128)S(1)} custom-call(bf16[32,5,16,128]{3,2,1,0:T(8,128)(2,1)S(1)} %get-tuple-element.47.states, bf16[32,5,16,128]{3,2,1,0:T(8,128)(2,1)S(1)} %get-tuple-element.43.basis.refs_5_, bf16[1,112,128]{2,1,0:T(8,128)(2,1)S(1)} %get-tuple-element.46.after.first.refs_8_), custom_call_target="tpu_custom_call" | custom-call | flops 2000000000 | bytes 1048576 | tf_op jit(solution)/shard_map/coords/pallas_call | solution.py:764
  5.1 3.8 %collective-permute-start.1 = (bf16[1,96,128]{2,1,0:T(8,128)(2,1)S(1)}, bf16[1,96,128]{2,1,0:T(8,128)(2,1)S(1)}, u32[]{:S(2)}, u32[]{:S(2)}) collective-permute-start(bf16[1,96,128]{2,1,0:T(8,128)(2,1)S(1)} %get-tuple-element.50.after.sent), channel_id=1, source_target_pairs={{0,9},{1,8},{2,11},{3,10},{4,13},{5,12},{6,15},{7,14},{8,1},{9,0},... | collective-permute-start | bytes 73736 | tf_op jit(solution)/shard_map/ppermute | solution.py:706
  8.8 0.7 %prepare.1 = (bf16[80,240]{1,0:T(8,128)(2,1)S(1)}, f32[5,16,128]{2,1,0:T(8,128)S(1)}, f32[5,16,128]{2,1,0:T(8,128)S(1)}) custom-call(f32[5]{0:T(128)S(1)} %copy-done.1, f32[5,5]{1,0:T(8,128)S(1)} %copy-done, f32[16]{0:T(128)S(1)} %copy-done.2, f32[5]{0:T(128)S(1)} %copy-done.3, f32[4,16,128]{2,1,0:T(8,128)S(1)} %get-tuple-element.44.cells.refs_6_, ...), custom_call_target="tpu_custom_call" | custom-call | flops 2000000000 | bytes 1048576 | tf_op jit(solution)/shard_map/prepare/pallas_call | solution.py:796
  9.5 0.9 %local.3.refs_12_ = f32[8,5,16,128]{3,2,1,0:T(8,128)S(1)} custom-call(bf16[32,5,16,128]{3,2,1,0:T(8,128)(2,1)S(1)} %get-tuple-element.47.states, f32[4,16,128]{2,1,0:T(8,128)S(1)} %get-tuple-element.44.cells.refs_6_, f32[32,128]{1,0:T(8,128)S(1)} %get-tuple-element.51.cosines, bf16[80,240]{1,0:T(8,128)(2,1)S(1)} %get-tuple-element.52.mixer_ref, ...), custom_call_target="tpu_custom_call" | custom-call | flops 2000000000 | bytes 1048576 | tf_op jit(solution)/shard_map/local/pallas_call | solution.py:776
  10.5 1.5 %collective-permute-start.2 = (bf16[1,128,128]{2,1,0:T(8,128)(2,1)S(1)}, bf16[1,128,128]{2,1,0:T(8,128)(2,1)S(1)}, u32[]{:S(2)}, u32[]{:S(2)}) collective-permute-start(bf16[1,128,128]{2,1,0:T(8,128)(2,1)S(1)} %get-tuple-element.57.after.sent), channel_id=1, source_target_pairs={{0,5},{1,4},{2,7},{3,6},{4,1},{5,0},{6,3},{7,2},{8,13},{9,12},{10,... | collective-permute-start | bytes 98312 | tf_op jit(solution)/shard_map/ppermute | solution.py:706
  12.0 0.9 %local.4.refs_13_ = f32[8,5,16,128]{3,2,1,0:T(8,128)S(1)} custom-call(bf16[32,5,16,128]{3,2,1,0:T(8,128)(2,1)S(1)} %get-tuple-element.47.states, f32[4,16,128]{2,1,0:T(8,128)S(1)} %get-tuple-element.44.cells.refs_6_, f32[32,128]{1,0:T(8,128)S(1)} %get-tuple-element.51.cosines, bf16[80,240]{1,0:T(8,128)(2,1)S(1)} %get-tuple-element.52.mixer_ref, ...), custom_call_target="tpu_custom_call" | custom-call | flops 2000000000 | bytes 1048576 | tf_op jit(solution)/shard_map/local/pallas_call | solution.py:776
  13.0 0.9 %collective-permute-done.2.got = bf16[1,128,128]{2,1,0:T(8,128)(2,1)S(1)} collective-permute-done((bf16[1,128,128]{2,1,0:T(8,128)(2,1)S(1)}, bf16[1,128,128]{2,1,0:T(8,128)(2,1)S(1)}, u32[]{:S(2)}, u32[]{:S(2)}) %collective-permute-start.2) | collective-permute-done | bytes 32800 | tf_op jit(solution)/shard_map/ppermute | solution.py:706
  13.9 1.5 %collective-permute-start.3 = (bf16[1,192,128]{2,1,0:T(8,128)(2,1)S(1)}, bf16[1,192,128]{2,1,0:T(8,128)(2,1)S(1)}, u32[]{:S(2)}, u32[]{:S(2)}) collective-permute-start(bf16[1,192,128]{2,1,0:T(8,128)(2,1)S(1)} %next.3.after.refs_10_), channel_id=1, source_target_pairs={{0,3},{1,2},{2,1},{3,0},{4,7},{5,6},{6,5},{7,4},{8,11},{9,10},{10,... | collective-permute-start | bytes 147464 | tf_op jit(solution)/shard_map/ppermute | solution.py:706
  15.4 1.9 %local.5.refs_14_ = f32[16,5,16,128]{3,2,1,0:T(8,128)S(1)} custom-call(bf16[32,5,16,128]{3,2,1,0:T(8,128)(2,1)S(1)} %get-tuple-element.47.states, f32[4,16,128]{2,1,0:T(8,128)S(1)} %get-tuple-element.44.cells.refs_6_, f32[32,128]{1,0:T(8,128)S(1)} %get-tuple-element.51.cosines, bf16[80,240]{1,0:T(8,128)(2,1)S(1)} %get-tuple-element.52.mixer_ref, ...), custom_call_target="tpu_custom_call" | custom-call | flops 2000000000 | bytes 1048576 | tf_op jit(solution)/shard_map/local/pallas_call | solution.py:776
  17.3 0.4 %collective-permute-done.3.refs_11_ = bf16[1,192,128]{2,1,0:T(8,128)(2,1)S(1)} collective-permute-done((bf16[1,192,128]{2,1,0:T(8,128)(2,1)S(1)}, bf16[1,192,128]{2,1,0:T(8,128)(2,1)S(1)}, u32[]{:S(2)}, u32[]{:S(2)}) %collective-permute-start.3) | collective-permute-done | bytes 49184 | tf_op jit(solution)/shard_map/ppermute | solution.py:706
  17.7 2.9 %after.1 = (bf16[32,5,16,128]{3,2,1,0:T(8,128)(2,1)S(1)}, f32[1,16,128]{2,1,0:T(8,128)S(1)}) custom-call(s32[1]{0:T(128)} %bitcast.place.refs_0_, f32[16]{0:T(128)S(1)} %copy-done.2, f32[5]{0:T(128)S(1)} %copy-done.3, f32[5]{0:T(128)S(1)} %copy-done.1, f32[5,5]{1,0:T(8,128)S(1)} %copy-done, bf16[32,5,16,128]{3,2,1,0:T(8,128)(2,1)S(1)} %get-tuple-element.43.basis.refs_5_, ...), custom_call_target="tpu_custom_call" | custom-call | tf_op jit(solution)/shard_map/after/pallas_call | solution.py:825
  20.6 0.2 collective-permute-start.4
  20.8 1.0 %collective-permute-done.4 = f32[1,16,128]{2,1,0:T(8,128)S(1)} collective-permute-done((f32[1,16,128]{2,1,0:T(8,128)S(1)}, f32[1,16,128]{2,1,0:T(8,128)S(1)}, u32[]{:S(2)}, u32[]{:S(2)}) %collective-permute-start.4) | collective-permute-done | bytes 8224 | tf_op jit(solution)/shard_map/ppermute | solution.py:706
  21.8 1.3 %collective-permute-start.5 = (f32[1,8,128]{2,1,0:T(8,128)S(1)}, f32[1,8,128]{2,1,0:T(8,128)S(1)}, u32[]{:S(2)}, u32[]{:S(2)}) collective-permute-start(f32[1,8,128]{2,1,0:T(8,128)S(1)} %get-tuple-element.69), channel_id=1, source_target_pairs={{0,3},{1,2},{2,1},{3,0},{4,7},{5,6},{6,5},{7,4},{8,11},{9,10},{10,... | collective-permute-start | bytes 12296 | tf_op jit(solution)/shard_map/ppermute | solution.py:706
  23.1 0.9 %system.1 = (f32[32,32]{1,0:T(8,128)S(1)}, f32[32,64]{1,0:T(8,128)S(1)}, bf16[32,5,16,128]{3,2,1,0:T(8,128)(2,1)}) custom-call(f32[1,8,128]{2,1,0:T(8,128)S(1)} %get-tuple-element.66.coords_ref, bf16[32,5,16,128]{3,2,1,0:T(8,128)(2,1)S(1)} %get-tuple-element.67.deriv), custom_call_target="tpu_custom_call" | custom-call | flops 2000000000 | bytes 1048576 | tf_op jit(solution)/shard_map/system/pallas_call | solution.py:881
  24.0 0.8 %collective-permute-done.5 = f32[1,8,128]{2,1,0:T(8,128)S(1)} collective-permute-done((f32[1,8,128]{2,1,0:T(8,128)S(1)}, f32[1,8,128]{2,1,0:T(8,128)S(1)}, u32[]{:S(2)}, u32[]{:S(2)}) %collective-permute-start.5) | collective-permute-done | bytes 4128 | tf_op jit(solution)/shard_map/ppermute | solution.py:706
  24.8 1.4 %collective-permute-start.6 = (f32[1,8,128]{2,1,0:T(8,128)S(1)}, f32[1,8,128]{2,1,0:T(8,128)S(1)}, u32[]{:S(2)}, u32[]{:S(2)}) collective-permute-start(f32[1,8,128]{2,1,0:T(8,128)S(1)} %add.13), channel_id=1, source_target_pairs={{0,5},{1,4},{2,7},{3,6},{4,1},{5,0},{6,3},{7,2},{8,13},{9,12},{10,... | collective-permute-start | bytes 12296 | tf_op jit(solution)/shard_map/ppermute | solution.py:706
  26.2 1.0 %invert.1.system_ref = f32[32,64]{1,0:T(8,128)S(1)} custom-call(f32[32,64]{1,0:T(8,128)S(1)} %get-tuple-element.73.system_ref), custom_call_target="tpu_custom_call" | custom-call | flops 2000000000 | bytes 1048576 | tf_op jit(solution)/shard_map/invert/pallas_call | solution.py:869
  27.2 0.7 %collective-permute-done.6 = f32[1,8,128]{2,1,0:T(8,128)S(1)} collective-permute-done((f32[1,8,128]{2,1,0:T(8,128)S(1)}, f32[1,8,128]{2,1,0:T(8,128)S(1)}, u32[]{:S(2)}, u32[]{:S(2)}) %collective-permute-start.6) | collective-permute-done | bytes 4128 | tf_op jit(solution)/shard_map/ppermute | solution.py:706
  27.9 2.7 %collective-permute-start.7 = (f32[1,8,128]{2,1,0:T(8,128)S(1)}, f32[1,8,128]{2,1,0:T(8,128)S(1)}, u32[]{:S(2)}, u32[]{:S(2)}) collective-permute-start(f32[1,8,128]{2,1,0:T(8,128)S(1)} %add.14), channel_id=1, source_target_pairs={{0,9},{1,8},{2,11},{3,10},{4,13},{5,12},{6,15},{7,14},{8,1},{9,0},... | collective-permute-start | bytes 12296 | tf_op jit(solution)/shard_map/ppermute | solution.py:706
  30.6 1.3 %weights.1 = (f32[32,560]{1,0:T(8,128)S(1)}, f32[32,32]{1,0:T(8,128)S(1)}) custom-call(f32[1,8,128]{2,1,0:T(8,128)S(1)} %get-tuple-element.66.coords_ref, f32[32,32]{1,0:T(8,128)S(1)} %get-tuple-element.75.kernel_ref, f32[32,64]{1,0:T(8,128)S(1)} %invert.1.system_ref, f32[32,560]{1,0:T(8,128)S(1)} %copy-done.5, f32[32,560]{1,0:T(8,128)S(1)} %copy-done.4, ...), custom_call_target="tpu_custom_call" | custom-call | flops 2000000000 | bytes 1048576 | tf_op jit(solution)/shard_map/weights/pallas_call | solution.py:869
  32.0 1.0 %fit.1 = (f32[2,64]{1,0:T(2,128)}, f32[32,560]{1,0:T(8,128)}, f32[2,32]{1,0:T(2,128)}) custom-call(s32[1]{0:T(128)} %bitcast.place.refs_0_, f32[1,8,128]{2,1,0:T(8,128)S(1)} %add.15.rates_ref, f32[1,8,128]{2,1,0:T(8,128)S(1)} %get-tuple-element.66.coords_ref, f32[32,560]{1,0:T(8,128)S(1)} %get-tuple-element.77.weights, f32[32,32]{1,0:T(8,128)S(1)} %get-tuple-element.78.fit), custom_call_target="tpu_custom_call" | custom-call | tf_op jit(solution)/shard_map/fit/pallas_call | solution.py:917
  (25 shorter events, 0.1 us)
Async XLA Ops:
  3.5 1.5 %collective-permute-start = (bf16[1,112,128]{2,1,0:T(8,128)(2,1)S(1)}, bf16[1,112,128]{2,1,0:T(8,128)(2,1)S(1)}, u32[]{:S(2)}, u32[]{:S(2)}) collective-permute-start(bf16[1,112,128]{2,1,0:T(8,128)(2,1)S(1)} %get-tuple-element.46.after.first.refs_8_), channel_id=1, source_target_pairs={{0,1},{1,0},{2,3},{3,2},{4,5},{5,4},{6,7},{7,6},{8,9},{9,8},{10,11... | collective-permute-start | bytes 86024 | tf_op jit(solution)/shard_map/ppermute | solution.py:706
  5.0 3.8 %copy-start = (f32[5,5]{1,0:T(8,128)S(1)}, f32[5,5]{1,0:T(8,128)}, u32[]{:S(2)}) copy-start(f32[5,5]{1,0:T(8,128)} %refs_4_.2) | copy-start | bytes 304
  5.0 3.8 %copy-start.1 = (f32[5]{0:T(128)S(1)}, f32[5]{0:T(128)}, u32[]{:S(2)}) copy-start(f32[5]{0:T(128)} %refs_3_.3) | copy-start | bytes 64
  5.0 3.8 %copy-start.2 = (f32[16]{0:T(128)S(1)}, f32[16]{0:T(128)}, u32[]{:S(2)}) copy-start(f32[16]{0:T(128)} %refs_1_.2) | copy-start | bytes 196
  5.0 3.8 %copy-start.3 = (f32[5]{0:T(128)S(1)}, f32[5]{0:T(128)}, u32[]{:S(2)}) copy-start(f32[5]{0:T(128)} %refs_2_.3) | copy-start | bytes 64
  5.1 5.4 %collective-permute-start.1 = (bf16[1,96,128]{2,1,0:T(8,128)(2,1)S(1)}, bf16[1,96,128]{2,1,0:T(8,128)(2,1)S(1)}, u32[]{:S(2)}, u32[]{:S(2)}) collective-permute-start(bf16[1,96,128]{2,1,0:T(8,128)(2,1)S(1)} %get-tuple-element.50.after.sent), channel_id=1, source_target_pairs={{0,9},{1,8},{2,11},{3,10},{4,13},{5,12},{6,15},{7,14},{8,1},{9,0},... | collective-permute-start | bytes 73736 | tf_op jit(solution)/shard_map/ppermute | solution.py:706
  10.5 3.4 %collective-permute-start.2 = (bf16[1,128,128]{2,1,0:T(8,128)(2,1)S(1)}, bf16[1,128,128]{2,1,0:T(8,128)(2,1)S(1)}, u32[]{:S(2)}, u32[]{:S(2)}) collective-permute-start(bf16[1,128,128]{2,1,0:T(8,128)(2,1)S(1)} %get-tuple-element.57.after.sent), channel_id=1, source_target_pairs={{0,5},{1,4},{2,7},{3,6},{4,1},{5,0},{6,3},{7,2},{8,13},{9,12},{10,... | collective-permute-start | bytes 98312 | tf_op jit(solution)/shard_map/ppermute | solution.py:706
  13.9 3.8 %collective-permute-start.3 = (bf16[1,192,128]{2,1,0:T(8,128)(2,1)S(1)}, bf16[1,192,128]{2,1,0:T(8,128)(2,1)S(1)}, u32[]{:S(2)}, u32[]{:S(2)}) collective-permute-start(bf16[1,192,128]{2,1,0:T(8,128)(2,1)S(1)} %next.3.after.refs_10_), channel_id=1, source_target_pairs={{0,3},{1,2},{2,1},{3,0},{4,7},{5,6},{6,5},{7,4},{8,11},{9,10},{10,... | collective-permute-start | bytes 147464 | tf_op jit(solution)/shard_map/ppermute | solution.py:706
  20.6 1.2 %collective-permute-start.4 = (f32[1,16,128]{2,1,0:T(8,128)S(1)}, f32[1,16,128]{2,1,0:T(8,128)S(1)}, u32[]{:S(2)}, u32[]{:S(2)}) collective-permute-start(f32[1,16,128]{2,1,0:T(8,128)S(1)} %get-tuple-element.64), channel_id=1, source_target_pairs={{0,1},{1,0},{2,3},{3,2},{4,5},{5,4},{6,7},{7,6},{8,9},{9,8},{10,11... | collective-permute-start | bytes 24584 | tf_op jit(solution)/shard_map/ppermute | solution.py:706
  21.8 3.0 %collective-permute-start.5 = (f32[1,8,128]{2,1,0:T(8,128)S(1)}, f32[1,8,128]{2,1,0:T(8,128)S(1)}, u32[]{:S(2)}, u32[]{:S(2)}) collective-permute-start(f32[1,8,128]{2,1,0:T(8,128)S(1)} %get-tuple-element.69), channel_id=1, source_target_pairs={{0,3},{1,2},{2,1},{3,0},{4,7},{5,6},{6,5},{7,4},{8,11},{9,10},{10,... | collective-permute-start | bytes 12296 | tf_op jit(solution)/shard_map/ppermute | solution.py:706
  24.8 5.8 %copy-start.4 = (f32[32,560]{1,0:T(8,128)S(1)}, f32[32,560]{1,0:T(8,128)}, u32[]{:S(2)}) copy-start(f32[32,560]{1,0:T(8,128)} %constant.14.clone.second_ref) | copy-start | bytes 215044
  24.8 5.8 %copy-start.5 = (f32[32,560]{1,0:T(8,128)S(1)}, f32[32,560]{1,0:T(8,128)}, u32[]{:S(2)}) copy-start(f32[32,560]{1,0:T(8,128)} %constant.13.clone.first_ref) | copy-start | bytes 215044
  24.8 3.1 %collective-permute-start.6 = (f32[1,8,128]{2,1,0:T(8,128)S(1)}, f32[1,8,128]{2,1,0:T(8,128)S(1)}, u32[]{:S(2)}, u32[]{:S(2)}) collective-permute-start(f32[1,8,128]{2,1,0:T(8,128)S(1)} %add.13), channel_id=1, source_target_pairs={{0,5},{1,4},{2,7},{3,6},{4,1},{5,0},{6,3},{7,2},{8,13},{9,12},{10,... | collective-permute-start | bytes 12296 | tf_op jit(solution)/shard_map/ppermute | solution.py:706
  27.2 3.5 %copy-start.6 = (f32[1,560]{1,0:T(1,128)S(1)}, f32[1,560]{1,0:T(1,128)}, u32[]{:S(2)}) copy-start(f32[1,560]{1,0:T(1,128)} %constant.15.clone.lin_ref) | copy-start | bytes 6724
  27.9 4.1 %collective-permute-start.7 = (f32[1,8,128]{2,1,0:T(8,128)S(1)}, f32[1,8,128]{2,1,0:T(8,128)S(1)}, u32[]{:S(2)}, u32[]{:S(2)}) collective-permute-start(f32[1,8,128]{2,1,0:T(8,128)S(1)} %add.14), channel_id=1, source_target_pairs={{0,9},{1,8},{2,11},{3,10},{4,13},{5,12},{6,15},{7,14},{8,1},{9,0},... | collective-permute-start | bytes 12296 | tf_op jit(solution)/shard_map/ppermute | solution.py:706

commit v6 on v5

--- a/solution.py
+++ b/solution.py
@@ -587,7 +587,7 @@
             m0, m1 = grooves[0, at, :], grooves[1, at, :]
             e = jnp.where(lane == LANES - 1, 0.0, roll(m0, -1, 1))
             w = jnp.where(lane == 0, 0.0, roll(m0, 1, 1))
-            spread = 2 * LANES - 4 * k - 2
+            spread = LANES - 4 * k - 2
             lap = e + w + north_south(m0) - 4.0 * m0
             own = 0.5 * (m0 + m1) - speed_step * (e - w) - damp_step * m0
             for v in range(NV):

time: 33.2 us -> 33.2 us (level)
  no operation moved by 1% of the time
where the time goes in v6:
time: 33.2 us; the launch traced here: 33 us
  Pallas kernels  14.8 us (45%)
  starting transfers between devices  12.9 us (39%)
  waiting for transfers between devices  3.91 us (12%)
  between operations  1.42 us (4%)
    ppermute x8, starting transfers between devices, swap(): return lax.ppermute(value, 'passage', pairs)  12.9 us
    ppermute x8, waiting for transfers between devices, swap(): return lax.ppermute(value, 'passage', pairs)  3.91 us
    pallas_call x3, Pallas kernels, local(): pl.pallas_call(functools.partial(local_kernel, offset), out_shape=jax.Sha...  3.78 us
    pallas_call x1, Pallas kernels, body(): pl.pallas_call(functools.partial(after_kernel, len(bases)), out_shape=(ja...  2.86 us
    pallas_call x2, Pallas kernels, small(): pl.pallas_call(kernel, out_shape=tuple((jax.ShapeDtypeStruct(shape, F32)...  2.29 us
    pallas_call x1, Pallas kernels, body(): pl.pallas_call(before_kernel, out_shape=(jax.ShapeDtypeStruct((chunks, RO...  2.23 us
    pallas_call x1, Pallas kernels, body(): pl.pallas_call(fit_kernel, out_shape=(jax.ShapeDtypeStruct((each, 2 * mod...  1 us
    pallas_call x1, Pallas kernels, body(): pl.pallas_call(coords_kernel, out_shape=tile, in_specs=[VMEM, VMEM, anywh...  0.95 us
  transfers between devices with their start and end apart: 8, of which 5 were waited for; matrix products, arithmetic and copies ran while one was open for 0% of the time, Pallas kernels for 26%

profile of v6, /device:TPU:0, one launch (start us, length us, event | category | flops | bytes accessed | tf_op | source)
XLA Modules:
  0.0 33.0 jit_solution(3586707451114277148)
XLA Ops:
  1.3 2.2 %before.1 = (bf16[1,112,128]{2,1,0:T(8,128)(2,1)S(1)}, bf16[32,5,16,128]{3,2,1,0:T(8,128)(2,1)S(1)}, bf16[32,5,16,128]{3,2,1,0:T(8,128)(2,1)S(1)}, f32[4,16,128]...) custom-call(s32[32]{0:T(128)} %refs_0_.1, s32[1]{0:T(128)S(6)} %copy.20.refs_1_, f32[5]{0:T(128)} %refs_3_.3, ...), custom_call_target="tpu_custom_call" | custom-call | tf_op jit(solution)/shard_map/before/pallas_call | solution.py:724
  3.5 0.5 %collective-permute-start = (bf16[1,112,128]{2,1,0:T(8,128)(2,1)S(1)}, bf16[1,112,128]{2,1,0:T(8,128)(2,1)S(1)}, u32[]{:S(2)}, u32[]{:S(2)}) collective-permute-start(bf16[1,112,128]{2,1,0:T(8,128)(2,1)S(1)} %get-tuple-element.46.after.first.refs_8_), channel_id=1, source_target_pairs={{0,1},{1,0},{2,3},{3,2},{4,5},{5,4},{6,7},{7,6},{8,9},{9,8},{10,11... | collective-permute-start | bytes 86024 | tf_op jit(solution)/shard_map/ppermute | solution.py:706
  4.0 0.9 %coords.1 = f32[1,8,128]{2,1,0:T(8,128)S(1)} custom-call(bf16[32,5,16,128]{3,2,1,0:T(8,128)(2,1)S(1)} %get-tuple-element.47.states, bf16[32,5,16,128]{3,2,1,0:T(8,128)(2,1)S(1)} %get-tuple-element.43.basis.refs_5_, bf16[1,112,128]{2,1,0:T(8,128)(2,1)S(1)} %get-tuple-element.46.after.first.refs_8_), custom_call_target="tpu_custom_call" | custom-call | flops 2000000000 | bytes 1048576 | tf_op jit(solution)/shard_map/coords/pallas_call | solution.py:764
  5.1 3.8 %collective-permute-start.1 = (bf16[1,96,128]{2,1,0:T(8,128)(2,1)S(1)}, bf16[1,96,128]{2,1,0:T(8,128)(2,1)S(1)}, u32[]{:S(2)}, u32[]{:S(2)}) collective-permute-start(bf16[1,96,128]{2,1,0:T(8,128)(2,1)S(1)} %get-tuple-element.50.after.sent), channel_id=1, source_target_pairs={{0,9},{1,8},{2,11},{3,10},{4,13},{5,12},{6,15},{7,14},{8,1},{9,0},... | collective-permute-start | bytes 73736 | tf_op jit(solution)/shard_map/ppermute | solution.py:706
  8.8 0.7 %prepare.1 = (bf16[80,240]{1,0:T(8,128)(2,1)S(1)}, f32[5,16,128]{2,1,0:T(8,128)S(1)}, f32[5,16,128]{2,1,0:T(8,128)S(1)}) custom-call(f32[5]{0:T(128)S(1)} %copy-done.1, f32[5,5]{1,0:T(8,128)S(1)} %copy-done, f32[16]{0:T(128)S(1)} %copy-done.2, f32[5]{0:T(128)S(1)} %copy-done.3, f32[4,16,128]{2,1,0:T(8,128)S(1)} %get-tuple-element.44.cells.refs_6_, ...), custom_call_target="tpu_custom_call" | custom-call | flops 2000000000 | bytes 1048576 | tf_op jit(solution)/shard_map/prepare/pallas_call | solution.py:796
  9.5 0.9 %local.3.refs_12_ = f32[8,5,16,128]{3,2,1,0:T(8,128)S(1)} custom-call(bf16[32,5,16,128]{3,2,1,0:T(8,128)(2,1)S(1)} %get-tuple-element.47.states, f32[4,16,128]{2,1,0:T(8,128)S(1)} %get-tuple-element.44.cells.refs_6_, f32[32,128]{1,0:T(8,128)S(1)} %get-tuple-element.51.cosines, bf16[80,240]{1,0:T(8,128)(2,1)S(1)} %get-tuple-element.52.mixer_ref, ...), custom_call_target="tpu_custom_call" | custom-call | flops 2000000000 | bytes 1048576 | tf_op jit(solution)/shard_map/local/pallas_call | solution.py:776
  10.5 1.5 %collective-permute-start.2 = (bf16[1,128,128]{2,1,0:T(8,128)(2,1)S(1)}, bf16[1,128,128]{2,1,0:T(8,128)(2,1)S(1)}, u32[]{:S(2)}, u32[]{:S(2)}) collective-permute-start(bf16[1,128,128]{2,1,0:T(8,128)(2,1)S(1)} %get-tuple-element.57.after.sent), channel_id=1, source_target_pairs={{0,5},{1,4},{2,7},{3,6},{4,1},{5,0},{6,3},{7,2},{8,13},{9,12},{10,... | collective-permute-start | bytes 98312 | tf_op jit(solution)/shard_map/ppermute | solution.py:706
  12.0 0.9 %local.4.refs_13_ = f32[8,5,16,128]{3,2,1,0:T(8,128)S(1)} custom-call(bf16[32,5,16,128]{3,2,1,0:T(8,128)(2,1)S(1)} %get-tuple-element.47.states, f32[4,16,128]{2,1,0:T(8,128)S(1)} %get-tuple-element.44.cells.refs_6_, f32[32,128]{1,0:T(8,128)S(1)} %get-tuple-element.51.cosines, bf16[80,240]{1,0:T(8,128)(2,1)S(1)} %get-tuple-element.52.mixer_ref, ...), custom_call_target="tpu_custom_call" | custom-call | flops 2000000000 | bytes 1048576 | tf_op jit(solution)/shard_map/local/pallas_call | solution.py:776
  13.0 0.9 %collective-permute-done.2.got = bf16[1,128,128]{2,1,0:T(8,128)(2,1)S(1)} collective-permute-done((bf16[1,128,128]{2,1,0:T(8,128)(2,1)S(1)}, bf16[1,128,128]{2,1,0:T(8,128)(2,1)S(1)}, u32[]{:S(2)}, u32[]{:S(2)}) %collective-permute-start.2) | collective-permute-done | bytes 32800 | tf_op jit(solution)/shard_map/ppermute | solution.py:706
  13.9 1.5 %collective-permute-start.3 = (bf16[1,192,128]{2,1,0:T(8,128)(2,1)S(1)}, bf16[1,192,128]{2,1,0:T(8,128)(2,1)S(1)}, u32[]{:S(2)}, u32[]{:S(2)}) collective-permute-start(bf16[1,192,128]{2,1,0:T(8,128)(2,1)S(1)} %next.3.after.refs_10_), channel_id=1, source_target_pairs={{0,3},{1,2},{2,1},{3,0},{4,7},{5,6},{6,5},{7,4},{8,11},{9,10},{10,... | collective-permute-start | bytes 147464 | tf_op jit(solution)/shard_map/ppermute | solution.py:706
  15.4 1.9 %local.5.refs_14_ = f32[16,5,16,128]{3,2,1,0:T(8,128)S(1)} custom-call(bf16[32,5,16,128]{3,2,1,0:T(8,128)(2,1)S(1)} %get-tuple-element.47.states, f32[4,16,128]{2,1,0:T(8,128)S(1)} %get-tuple-element.44.cells.refs_6_, f32[32,128]{1,0:T(8,128)S(1)} %get-tuple-element.51.cosines, bf16[80,240]{1,0:T(8,128)(2,1)S(1)} %get-tuple-element.52.mixer_ref, ...), custom_call_target="tpu_custom_call" | custom-call | flops 2000000000 | bytes 1048576 | tf_op jit(solution)/shard_map/local/pallas_call | solution.py:776
  17.3 0.4 %collective-permute-done.3.refs_11_ = bf16[1,192,128]{2,1,0:T(8,128)(2,1)S(1)} collective-permute-done((bf16[1,192,128]{2,1,0:T(8,128)(2,1)S(1)}, bf16[1,192,128]{2,1,0:T(8,128)(2,1)S(1)}, u32[]{:S(2)}, u32[]{:S(2)}) %collective-permute-start.3) | collective-permute-done | bytes 49184 | tf_op jit(solution)/shard_map/ppermute | solution.py:706
  17.7 2.9 %after.1 = (bf16[32,5,16,128]{3,2,1,0:T(8,128)(2,1)S(1)}, f32[1,16,128]{2,1,0:T(8,128)S(1)}) custom-call(s32[1]{0:T(128)} %bitcast.place.refs_0_, f32[16]{0:T(128)S(1)} %copy-done.2, f32[5]{0:T(128)S(1)} %copy-done.3, f32[5]{0:T(128)S(1)} %copy-done.1, f32[5,5]{1,0:T(8,128)S(1)} %copy-done, bf16[32,5,16,128]{3,2,1,0:T(8,128)(2,1)S(1)} %get-tuple-element.43.basis.refs_5_, ...), custom_call_target="tpu_custom_call" | custom-call | tf_op jit(solution)/shard_map/after/pallas_call | solution.py:825
  20.6 0.2 collective-permute-start.4
  20.8 1.0 %collective-permute-done.4 = f32[1,16,128]{2,1,0:T(8,128)S(1)} collective-permute-done((f32[1,16,128]{2,1,0:T(8,128)S(1)}, f32[1,16,128]{2,1,0:T(8,128)S(1)}, u32[]{:S(2)}, u32[]{:S(2)}) %collective-permute-start.4) | collective-permute-done | bytes 8224 | tf_op jit(solution)/shard_map/ppermute | solution.py:706
  21.8 1.3 %collective-permute-start.5 = (f32[1,8,128]{2,1,0:T(8,128)S(1)}, f32[1,8,128]{2,1,0:T(8,128)S(1)}, u32[]{:S(2)}, u32[]{:S(2)}) collective-permute-start(f32[1,8,128]{2,1,0:T(8,128)S(1)} %get-tuple-element.69), channel_id=1, source_target_pairs={{0,3},{1,2},{2,1},{3,0},{4,7},{5,6},{6,5},{7,4},{8,11},{9,10},{10,... | collective-permute-start | bytes 12296 | tf_op jit(solution)/shard_map/ppermute | solution.py:706
  23.1 0.9 %system.1 = (f32[32,32]{1,0:T(8,128)S(1)}, f32[32,64]{1,0:T(8,128)S(1)}, bf16[32,5,16,128]{3,2,1,0:T(8,128)(2,1)}) custom-call(f32[1,8,128]{2,1,0:T(8,128)S(1)} %get-tuple-element.66.coords_ref, bf16[32,5,16,128]{3,2,1,0:T(8,128)(2,1)S(1)} %get-tuple-element.67.deriv), custom_call_target="tpu_custom_call" | custom-call | flops 2000000000 | bytes 1048576 | tf_op jit(solution)/shard_map/system/pallas_call | solution.py:881
  24.0 0.8 %collective-permute-done.5 = f32[1,8,128]{2,1,0:T(8,128)S(1)} collective-permute-done((f32[1,8,128]{2,1,0:T(8,128)S(1)}, f32[1,8,128]{2,1,0:T(8,128)S(1)}, u32[]{:S(2)}, u32[]{:S(2)}) %collective-permute-start.5) | collective-permute-done | bytes 4128 | tf_op jit(solution)/shard_map/ppermute | solution.py:706
  24.8 1.4 %collective-permute-start.6 = (f32[1,8,128]{2,1,0:T(8,128)S(1)}, f32[1,8,128]{2,1,0:T(8,128)S(1)}, u32[]{:S(2)}, u32[]{:S(2)}) collective-permute-start(f32[1,8,128]{2,1,0:T(8,128)S(1)} %add.13), channel_id=1, source_target_pairs={{0,5},{1,4},{2,7},{3,6},{4,1},{5,0},{6,3},{7,2},{8,13},{9,12},{10,... | collective-permute-start | bytes 12296 | tf_op jit(solution)/shard_map/ppermute | solution.py:706
  26.2 1.0 %invert.1.system_ref = f32[32,64]{1,0:T(8,128)S(1)} custom-call(f32[32,64]{1,0:T(8,128)S(1)} %get-tuple-element.73.system_ref), custom_call_target="tpu_custom_call" | custom-call | flops 2000000000 | bytes 1048576 | tf_op jit(solution)/shard_map/invert/pallas_call | solution.py:869
  27.2 0.7 %collective-permute-done.6 = f32[1,8,128]{2,1,0:T(8,128)S(1)} collective-permute-done((f32[1,8,128]{2,1,0:T(8,128)S(1)}, f32[1,8,128]{2,1,0:T(8,128)S(1)}, u32[]{:S(2)}, u32[]{:S(2)}) %collective-permute-start.6) | collective-permute-done | bytes 4128 | tf_op jit(solution)/shard_map/ppermute | solution.py:706
  27.9 2.7 %collective-permute-start.7 = (f32[1,8,128]{2,1,0:T(8,128)S(1)}, f32[1,8,128]{2,1,0:T(8,128)S(1)}, u32[]{:S(2)}, u32[]{:S(2)}) collective-permute-start(f32[1,8,128]{2,1,0:T(8,128)S(1)} %add.14), channel_id=1, source_target_pairs={{0,9},{1,8},{2,11},{3,10},{4,13},{5,12},{6,15},{7,14},{8,1},{9,0},... | collective-permute-start | bytes 12296 | tf_op jit(solution)/shard_map/ppermute | solution.py:706
  30.6 1.3 %weights.1 = (f32[32,560]{1,0:T(8,128)S(1)}, f32[32,32]{1,0:T(8,128)S(1)}) custom-call(f32[1,8,128]{2,1,0:T(8,128)S(1)} %get-tuple-element.66.coords_ref, f32[32,32]{1,0:T(8,128)S(1)} %get-tuple-element.75.kernel_ref, f32[32,64]{1,0:T(8,128)S(1)} %invert.1.system_ref, f32[32,560]{1,0:T(8,128)S(1)} %copy-done.5, f32[32,560]{1,0:T(8,128)S(1)} %copy-done.4, ...), custom_call_target="tpu_custom_call" | custom-call | flops 2000000000 | bytes 1048576 | tf_op jit(solution)/shard_map/weights/pallas_call | solution.py:869
  32.0 1.0 %fit.1 = (f32[2,64]{1,0:T(2,128)}, f32[32,560]{1,0:T(8,128)}, f32[2,32]{1,0:T(2,128)}) custom-call(s32[1]{0:T(128)} %bitcast.place.refs_0_, f32[1,8,128]{2,1,0:T(8,128)S(1)} %add.15.rates_ref, f32[1,8,128]{2,1,0:T(8,128)S(1)} %get-tuple-element.66.coords_ref, f32[32,560]{1,0:T(8,128)S(1)} %get-tuple-element.77.weights, f32[32,32]{1,0:T(8,128)S(1)} %get-tuple-element.78.fit), custom_call_target="tpu_custom_call" | custom-call | tf_op jit(solution)/shard_map/fit/pallas_call | solution.py:917
  (25 shorter events, 0.1 us)
Async XLA Ops:
  3.5 1.5 %collective-permute-start = (bf16[1,112,128]{2,1,0:T(8,128)(2,1)S(1)}, bf16[1,112,128]{2,1,0:T(8,128)(2,1)S(1)}, u32[]{:S(2)}, u32[]{:S(2)}) collective-permute-start(bf16[1,112,128]{2,1,0:T(8,128)(2,1)S(1)} %get-tuple-element.46.after.first.refs_8_), channel_id=1, source_target_pairs={{0,1},{1,0},{2,3},{3,2},{4,5},{5,4},{6,7},{7,6},{8,9},{9,8},{10,11... | collective-permute-start | bytes 86024 | tf_op jit(solution)/shard_map/ppermute | solution.py:706
  5.0 3.8 %copy-start = (f32[5,5]{1,0:T(8,128)S(1)}, f32[5,5]{1,0:T(8,128)}, u32[]{:S(2)}) copy-start(f32[5,5]{1,0:T(8,128)} %refs_4_.2) | copy-start | bytes 304
  5.0 3.8 %copy-start.1 = (f32[5]{0:T(128)S(1)}, f32[5]{0:T(128)}, u32[]{:S(2)}) copy-start(f32[5]{0:T(128)} %refs_3_.3) | copy-start | bytes 64
  5.0 3.8 %copy-start.2 = (f32[16]{0:T(128)S(1)}, f32[16]{0:T(128)}, u32[]{:S(2)}) copy-start(f32[16]{0:T(128)} %refs_1_.2) | copy-start | bytes 196
  5.0 3.8 %copy-start.3 = (f32[5]{0:T(128)S(1)}, f32[5]{0:T(128)}, u32[]{:S(2)}) copy-start(f32[5]{0:T(128)} %refs_2_.3) | copy-start | bytes 64
  5.1 5.4 %collective-permute-start.1 = (bf16[1,96,128]{2,1,0:T(8,128)(2,1)S(1)}, bf16[1,96,128]{2,1,0:T(8,128)(2,1)S(1)}, u32[]{:S(2)}, u32[]{:S(2)}) collective-permute-start(bf16[1,96,128]{2,1,0:T(8,128)(2,1)S(1)} %get-tuple-element.50.after.sent), channel_id=1, source_target_pairs={{0,9},{1,8},{2,11},{3,10},{4,13},{5,12},{6,15},{7,14},{8,1},{9,0},... | collective-permute-start | bytes 73736 | tf_op jit(solution)/shard_map/ppermute | solution.py:706
  10.5 3.4 %collective-permute-start.2 = (bf16[1,128,128]{2,1,0:T(8,128)(2,1)S(1)}, bf16[1,128,128]{2,1,0:T(8,128)(2,1)S(1)}, u32[]{:S(2)}, u32[]{:S(2)}) collective-permute-start(bf16[1,128,128]{2,1,0:T(8,128)(2,1)S(1)} %get-tuple-element.57.after.sent), channel_id=1, source_target_pairs={{0,5},{1,4},{2,7},{3,6},{4,1},{5,0},{6,3},{7,2},{8,13},{9,12},{10,... | collective-permute-start | bytes 98312 | tf_op jit(solution)/shard_map/ppermute | solution.py:706
  13.9 3.8 %collective-permute-start.3 = (bf16[1,192,128]{2,1,0:T(8,128)(2,1)S(1)}, bf16[1,192,128]{2,1,0:T(8,128)(2,1)S(1)}, u32[]{:S(2)}, u32[]{:S(2)}) collective-permute-start(bf16[1,192,128]{2,1,0:T(8,128)(2,1)S(1)} %next.3.after.refs_10_), channel_id=1, source_target_pairs={{0,3},{1,2},{2,1},{3,0},{4,7},{5,6},{6,5},{7,4},{8,11},{9,10},{10,... | collective-permute-start | bytes 147464 | tf_op jit(solution)/shard_map/ppermute | solution.py:706
  20.6 1.2 %collective-permute-start.4 = (f32[1,16,128]{2,1,0:T(8,128)S(1)}, f32[1,16,128]{2,1,0:T(8,128)S(1)}, u32[]{:S(2)}, u32[]{:S(2)}) collective-permute-start(f32[1,16,128]{2,1,0:T(8,128)S(1)} %get-tuple-element.64), channel_id=1, source_target_pairs={{0,1},{1,0},{2,3},{3,2},{4,5},{5,4},{6,7},{7,6},{8,9},{9,8},{10,11... | collective-permute-start | bytes 24584 | tf_op jit(solution)/shard_map/ppermute | solution.py:706
  21.8 3.0 %collective-permute-start.5 = (f32[1,8,128]{2,1,0:T(8,128)S(1)}, f32[1,8,128]{2,1,0:T(8,128)S(1)}, u32[]{:S(2)}, u32[]{:S(2)}) collective-permute-start(f32[1,8,128]{2,1,0:T(8,128)S(1)} %get-tuple-element.69), channel_id=1, source_target_pairs={{0,3},{1,2},{2,1},{3,0},{4,7},{5,6},{6,5},{7,4},{8,11},{9,10},{10,... | collective-permute-start | bytes 12296 | tf_op jit(solution)/shard_map/ppermute | solution.py:706
  24.8 5.8 %copy-start.4 = (f32[32,560]{1,0:T(8,128)S(1)}, f32[32,560]{1,0:T(8,128)}, u32[]{:S(2)}) copy-start(f32[32,560]{1,0:T(8,128)} %constant.14.clone.second_ref) | copy-start | bytes 215044
  24.8 5.8 %copy-start.5 = (f32[32,560]{1,0:T(8,128)S(1)}, f32[32,560]{1,0:T(8,128)}, u32[]{:S(2)}) copy-start(f32[32,560]{1,0:T(8,128)} %constant.13.clone.first_ref) | copy-start | bytes 215044
  24.8 3.1 %collective-permute-start.6 = (f32[1,8,128]{2,1,0:T(8,128)S(1)}, f32[1,8,128]{2,1,0:T(8,128)S(1)}, u32[]{:S(2)}, u32[]{:S(2)}) collective-permute-start(f32[1,8,128]{2,1,0:T(8,128)S(1)} %add.13), channel_id=1, source_target_pairs={{0,5},{1,4},{2,7},{3,6},{4,1},{5,0},{6,3},{7,2},{8,13},{9,12},{10,... | collective-permute-start | bytes 12296 | tf_op jit(solution)/shard_map/ppermute | solution.py:706
  27.2 3.5 %copy-start.6 = (f32[1,560]{1,0:T(1,128)S(1)}, f32[1,560]{1,0:T(1,128)}, u32[]{:S(2)}) copy-start(f32[1,560]{1,0:T(1,128)} %constant.15.clone.lin_ref) | copy-start | bytes 6724
  27.9 4.1 %collective-permute-start.7 = (f32[1,8,128]{2,1,0:T(8,128)S(1)}, f32[1,8,128]{2,1,0:T(8,128)S(1)}, u32[]{:S(2)}, u32[]{:S(2)}) collective-permute-start(f32[1,8,128]{2,1,0:T(8,128)S(1)} %add.14), channel_id=1, source_target_pairs={{0,9},{1,8},{2,11},{3,10},{4,13},{5,12},{6,15},{7,14},{8,1},{9,0},... | collective-permute-start | bytes 12296 | tf_op jit(solution)/shard_map/ppermute | solution.py:706

commit v7 on v6

--- a/solution.py
+++ b/solution.py
@@ -289,7 +289,12 @@
         out[chunk] = jnp.concatenate(rows, axis=0).astype(BF16)
 
 
-def prepare_kernel(visc, coup, kern, gain, cells, after, mixer, east_coef, west_coef):
+def prepare_kernel(visc, coup, kern, gain, cells, after, mixer, east_coef, west_coef, splats):
+    scalars = [gain[v] for v in range(NV)] + [visc[v] for v in range(NV)]
+    scalars += [coup[v, other] for v in range(NV) for other in range(NV)]
+    scalars += [kern[p] for p in range(kern.shape[0])]
+    for i, value in enumerate(scalars):
+        splats[i : i + 1, :] = jnp.full((1, LANES), value, F32)
     half_speed = 0.5 * cells[0]
     lane = iota((NX, LANES), 1)
     for v in range(NV):
@@ -365,11 +370,25 @@
     lax.fori_loop(0, count // 8, snaps, 0)
 
 
+class Splats:
+    def __init__(self, ref, first, shape):
+        self.ref, self.first, self.shape = ref, first, shape
+
+    def __getitem__(self, index):
+        if isinstance(index, tuple):
+            index = index[0] * self.shape[1] + index[1]
+        return self.ref[pl.ds(self.first + index, 1), :]
+
+
 def after_kernel(parts, *refs):
-    place, kern, gain, visc, coup, basis, cells, cos_lanes = refs[:8]
-    own_ref, near_ref, sent_ref, last_ref = refs[8:12]
-    bases = refs[12 : 12 + parts]
-    deriv, partial, mixed, raw, cyc0, grooves, ends = refs[12 + parts :]
+    place, splats, basis, cells, cos_lanes = refs[:5]
+    own_ref, near_ref, sent_ref, last_ref = refs[5:9]
+    bases = refs[9 : 9 + parts]
+    deriv, partial, mixed, raw, cyc0, grooves, ends = refs[9 + parts :]
+    gain, visc = Splats(splats, 0, (NV,)), Splats(splats, NV, (NV,))
+    coup = Splats(splats, 2 * NV, (NV, NV))
+    scalars = 2 * NV + NV * NV
+    kern = Splats(splats, scalars, (splats.shape[0] - scalars,))
     chunks = own_ref.shape[0]
     passages = kern.shape[0]
     me = place[0]
@@ -793,15 +812,16 @@
 
     start = functools.partial(start_kernel, bits - 1)
     message, edges = glue(start, "start", head + 2 * BLOB, first, near, coords)
-    mixer, east_coef, west_coef = pl.pallas_call(
+    mixer, east_coef, west_coef, splats = pl.pallas_call(
         prepare_kernel,
         out_shape=(
             jax.ShapeDtypeStruct((NV * NX, 3 * NV * NX), BF16),
             jax.ShapeDtypeStruct((NV, NX, LANES), F32),
             jax.ShapeDtypeStruct((NV, NX, LANES), F32),
+            jax.ShapeDtypeStruct((2 * NV + NV * NV + passages, LANES), F32),
         ),
         in_specs=[SMEM] * 4 + [VMEM, anywhere],
-        out_specs=(VMEM, VMEM, VMEM),
+        out_specs=(VMEM,) * 4,
         cost_estimate=hidden,
         compiler_params=pltpu.CompilerParams(vmem_limit_bytes=16 * 2**20),
         name="prepare",
@@ -828,7 +848,7 @@
             jax.ShapeDtypeStruct(states.shape, BF16),
             jax.ShapeDtypeStruct((chunks, 16, LANES), F32),
         ),
-        in_specs=[SMEM] * 5 + [VMEM] * (7 + len(bases)),
+        in_specs=[SMEM] + [VMEM] * (8 + len(bases)),
         out_specs=(VMEM, VMEM),
         scratch_shapes=[
             pltpu.VMEM((passages * BLOB, 6 * LANES), F32),
@@ -841,10 +861,7 @@
         name="after",
     )(
         place,
-        groove_kernel,
-        groove_gain,
-        viscosity,
-        coupling,
+        splats,
         held_basis,
         cells,
         cos_lanes,

time: 33.2 us -> 32.6 us (0.982)
  Pallas kernels: 14.8 us -> 14.2 us
    pallas_call x1, Pallas kernels: 2.86 us -> 2.26 us  [body(): pl.pallas_call(functools.partial(after_kernel, len(bases)), out_shape=(ja...]
  transfers between devices with their start and end apart: 8 -> 8, of which waited for: 5 -> 5; matrix products, arithmetic and copies ran while one was open for 0% -> 0% of each run, Pallas kernels for 26% -> 27%
where the time goes in v7:
time: 32.6 us; the launch traced here: 32.4 us
  Pallas kernels  14.2 us (44%)
  starting transfers between devices  12.8 us (39%)
  waiting for transfers between devices  3.91 us (12%)
  between operations  1.42 us (4%)
    ppermute x8, starting transfers between devices, swap(): return lax.ppermute(value, 'passage', pairs)  12.8 us
    ppermute x8, waiting for transfers between devices, swap(): return lax.ppermute(value, 'passage', pairs)  3.91 us
    pallas_call x3, Pallas kernels, local(): pl.pallas_call(functools.partial(local_kernel, offset), out_shape=jax.Sha...  3.78 us
    pallas_call x2, Pallas kernels, small(): pl.pallas_call(kernel, out_shape=tuple((jax.ShapeDtypeStruct(shape, F32)...  2.29 us
    pallas_call x1, Pallas kernels, body(): pl.pallas_call(functools.partial(after_kernel, len(bases)), out_shape=(ja...  2.26 us
    pallas_call x1, Pallas kernels, body(): pl.pallas_call(before_kernel, out_shape=(jax.ShapeDtypeStruct((chunks, RO...  2.23 us
    pallas_call x1, Pallas kernels, body(): pl.pallas_call(fit_kernel, out_shape=(jax.ShapeDtypeStruct((each, 2 * mod...  1 us
    pallas_call x1, Pallas kernels, body(): pl.pallas_call(coords_kernel, out_shape=tile, in_specs=[VMEM, VMEM, anywh...  0.95 us
  transfers between devices with their start and end apart: 8, of which 5 were waited for; matrix products, arithmetic and copies ran while one was open for 0% of the time, Pallas kernels for 27%

profile of v7, /device:TPU:0, one launch (start us, length us, event | category | flops | bytes accessed | tf_op | source)
XLA Modules:
  0.0 32.4 jit_solution(3535704985460268786)
XLA Ops:
  1.3 2.2 %before.1 = (bf16[1,112,128]{2,1,0:T(8,128)(2,1)S(1)}, bf16[32,5,16,128]{3,2,1,0:T(8,128)(2,1)S(1)}, bf16[32,5,16,128]{3,2,1,0:T(8,128)(2,1)S(1)}, f32[4,16,128]...) custom-call(s32[32]{0:T(128)} %refs_0_.1, s32[1]{0:T(128)S(6)} %copy.20.refs_1_, f32[5]{0:T(128)} %visc.1, ...), custom_call_target="tpu_custom_call" | custom-call | tf_op jit(solution)/shard_map/before/pallas_call | solution.py:743
  3.5 0.5 %collective-permute-start = (bf16[1,112,128]{2,1,0:T(8,128)(2,1)S(1)}, bf16[1,112,128]{2,1,0:T(8,128)(2,1)S(1)}, u32[]{:S(2)}, u32[]{:S(2)}) collective-permute-start(bf16[1,112,128]{2,1,0:T(8,128)(2,1)S(1)} %get-tuple-element.45.after.first.refs_5_), channel_id=1, source_target_pairs={{0,1},{1,0},{2,3},{3,2},{4,5},{5,4},{6,7},{7,6},{8,9},{9,8},{10,11... | collective-permute-start | bytes 86024 | tf_op jit(solution)/shard_map/ppermute | solution.py:725
  4.0 0.9 %coords.1 = f32[1,8,128]{2,1,0:T(8,128)S(1)} custom-call(bf16[32,5,16,128]{3,2,1,0:T(8,128)(2,1)S(1)} %get-tuple-element.46.states, bf16[32,5,16,128]{3,2,1,0:T(8,128)(2,1)S(1)} %get-tuple-element.47.basis.refs_2_, bf16[1,112,128]{2,1,0:T(8,128)(2,1)S(1)} %get-tuple-element.45.after.first.refs_5_), custom_call_target="tpu_custom_call" | custom-call | flops 2000000000 | bytes 1048576 | tf_op jit(solution)/shard_map/coords/pallas_call | solution.py:783
  5.1 3.8 %collective-permute-start.1 = (bf16[1,96,128]{2,1,0:T(8,128)(2,1)S(1)}, bf16[1,96,128]{2,1,0:T(8,128)(2,1)S(1)}, u32[]{:S(2)}, u32[]{:S(2)}) collective-permute-start(bf16[1,96,128]{2,1,0:T(8,128)(2,1)S(1)} %get-tuple-element.50.after.sent), channel_id=1, source_target_pairs={{0,9},{1,8},{2,11},{3,10},{4,13},{5,12},{6,15},{7,14},{8,1},{9,0},... | collective-permute-start | bytes 73736 | tf_op jit(solution)/shard_map/ppermute | solution.py:725
  8.8 0.7 %prepare.1 = (bf16[80,240]{1,0:T(8,128)(2,1)S(1)}, f32[5,16,128]{2,1,0:T(8,128)S(1)}, f32[5,16,128]{2,1,0:T(8,128)S(1)}, f32[51,128]{1,0:T(8,128)S(1)}) custom-call(f32[5]{0:T(128)S(1)} %copy-done.1, f32[5,5]{1,0:T(8,128)S(1)} %copy-done, f32[16]{0:T(128)S(1)} %copy-done.2, f32[5]{0:T(128)S(1)} %copy-done.3, ...), custom_call_target="tpu_custom_call" | custom-call | flops 2000000000 | bytes 1048576 | tf_op jit(solution)/shard_map/prepare/pallas_call | solution.py:815
  9.5 0.9 %local.3.refs_9_ = f32[8,5,16,128]{3,2,1,0:T(8,128)S(1)} custom-call(bf16[32,5,16,128]{3,2,1,0:T(8,128)(2,1)S(1)} %get-tuple-element.46.states, f32[4,16,128]{2,1,0:T(8,128)S(1)} %get-tuple-element.44.cells.refs_3_, f32[32,128]{1,0:T(8,128)S(1)} %get-tuple-element.53.cosines, bf16[80,240]{1,0:T(8,128)(2,1)S(1)} %get-tuple-element.54.mixer_ref, ...), custom_call_target="tpu_custom_call" | custom-call | flops 2000000000 | bytes 1048576 | tf_op jit(solution)/shard_map/local/pallas_call | solution.py:795
  10.5 1.5 %collective-permute-start.2 = (bf16[1,128,128]{2,1,0:T(8,128)(2,1)S(1)}, bf16[1,128,128]{2,1,0:T(8,128)(2,1)S(1)}, u32[]{:S(2)}, u32[]{:S(2)}) collective-permute-start(bf16[1,128,128]{2,1,0:T(8,128)(2,1)S(1)} %get-tuple-element.59.after.sent), channel_id=1, source_target_pairs={{0,5},{1,4},{2,7},{3,6},{4,1},{5,0},{6,3},{7,2},{8,13},{9,12},{10,... | collective-permute-start | bytes 98312 | tf_op jit(solution)/shard_map/ppermute | solution.py:725
  12.0 0.9 %local.4.refs_10_ = f32[8,5,16,128]{3,2,1,0:T(8,128)S(1)} custom-call(bf16[32,5,16,128]{3,2,1,0:T(8,128)(2,1)S(1)} %get-tuple-element.46.states, f32[4,16,128]{2,1,0:T(8,128)S(1)} %get-tuple-element.44.cells.refs_3_, f32[32,128]{1,0:T(8,128)S(1)} %get-tuple-element.53.cosines, bf16[80,240]{1,0:T(8,128)(2,1)S(1)} %get-tuple-element.54.mixer_ref, ...), custom_call_target="tpu_custom_call" | custom-call | flops 2000000000 | bytes 1048576 | tf_op jit(solution)/shard_map/local/pallas_call | solution.py:795
  13.0 0.9 %collective-permute-done.2.got = bf16[1,128,128]{2,1,0:T(8,128)(2,1)S(1)} collective-permute-done((bf16[1,128,128]{2,1,0:T(8,128)(2,1)S(1)}, bf16[1,128,128]{2,1,0:T(8,128)(2,1)S(1)}, u32[]{:S(2)}, u32[]{:S(2)}) %collective-permute-start.2) | collective-permute-done | bytes 32800 | tf_op jit(solution)/shard_map/ppermute | solution.py:725
  13.9 1.5 %collective-permute-start.3 = (bf16[1,192,128]{2,1,0:T(8,128)(2,1)S(1)}, bf16[1,192,128]{2,1,0:T(8,128)(2,1)S(1)}, u32[]{:S(2)}, u32[]{:S(2)}) collective-permute-start(bf16[1,192,128]{2,1,0:T(8,128)(2,1)S(1)} %next.3.after.refs_7_), channel_id=1, source_target_pairs={{0,3},{1,2},{2,1},{3,0},{4,7},{5,6},{6,5},{7,4},{8,11},{9,10},{10,... | collective-permute-start | bytes 147464 | tf_op jit(solution)/shard_map/ppermute | solution.py:725
  15.4 1.9 %local.5.refs_11_ = f32[16,5,16,128]{3,2,1,0:T(8,128)S(1)} custom-call(bf16[32,5,16,128]{3,2,1,0:T(8,128)(2,1)S(1)} %get-tuple-element.46.states, f32[4,16,128]{2,1,0:T(8,128)S(1)} %get-tuple-element.44.cells.refs_3_, f32[32,128]{1,0:T(8,128)S(1)} %get-tuple-element.53.cosines, bf16[80,240]{1,0:T(8,128)(2,1)S(1)} %get-tuple-element.54.mixer_ref, ...), custom_call_target="tpu_custom_call" | custom-call | flops 2000000000 | bytes 1048576 | tf_op jit(solution)/shard_map/local/pallas_call | solution.py:795
  17.3 0.4 %collective-permute-done.3.refs_8_ = bf16[1,192,128]{2,1,0:T(8,128)(2,1)S(1)} collective-permute-done((bf16[1,192,128]{2,1,0:T(8,128)(2,1)S(1)}, bf16[1,192,128]{2,1,0:T(8,128)(2,1)S(1)}, u32[]{:S(2)}, u32[]{:S(2)}) %collective-permute-start.3) | collective-permute-done | bytes 49184 | tf_op jit(solution)/shard_map/ppermute | solution.py:725
  17.7 2.3 %after.1 = (bf16[32,5,16,128]{3,2,1,0:T(8,128)(2,1)S(1)}, f32[1,16,128]{2,1,0:T(8,128)S(1)}) custom-call(s32[1]{0:T(128)} %bitcast.place.refs_0_, f32[51,128]{1,0:T(8,128)S(1)} %get-tuple-element.51.refs_1_, bf16[32,5,16,128]{3,2,1,0:T(8,128)(2,1)S(1)} %get-tuple-element.47.basis.refs_2_, f32[4,16,128]{2,1,0:T(8,128)S(1)} %get-tuple-element.44.cells.refs_3_, ...), custom_call_target="tpu_custom_call" | custom-call | tf_op jit(solution)/shard_map/after/pallas_call | solution.py:845
  20.0 0.2 collective-permute-start.4
  20.1 1.0 %collective-permute-done.4 = f32[1,16,128]{2,1,0:T(8,128)S(1)} collective-permute-done((f32[1,16,128]{2,1,0:T(8,128)S(1)}, f32[1,16,128]{2,1,0:T(8,128)S(1)}, u32[]{:S(2)}, u32[]{:S(2)}) %collective-permute-start.4) | collective-permute-done | bytes 8224 | tf_op jit(solution)/shard_map/ppermute | solution.py:725
  21.2 1.3 %collective-permute-start.5 = (f32[1,8,128]{2,1,0:T(8,128)S(1)}, f32[1,8,128]{2,1,0:T(8,128)S(1)}, u32[]{:S(2)}, u32[]{:S(2)}) collective-permute-start(f32[1,8,128]{2,1,0:T(8,128)S(1)} %get-tuple-element.71), channel_id=1, source_target_pairs={{0,3},{1,2},{2,1},{3,0},{4,7},{5,6},{6,5},{7,4},{8,11},{9,10},{10,... | collective-permute-start | bytes 12296 | tf_op jit(solution)/shard_map/ppermute | solution.py:725
  22.5 0.9 %system.1 = (f32[32,32]{1,0:T(8,128)S(1)}, f32[32,64]{1,0:T(8,128)S(1)}, bf16[32,5,16,128]{3,2,1,0:T(8,128)(2,1)}) custom-call(f32[1,8,128]{2,1,0:T(8,128)S(1)} %get-tuple-element.68.coords_ref, bf16[32,5,16,128]{3,2,1,0:T(8,128)(2,1)S(1)} %get-tuple-element.69.deriv), custom_call_target="tpu_custom_call" | custom-call | flops 2000000000 | bytes 1048576 | tf_op jit(solution)/shard_map/system/pallas_call | solution.py:898
  23.4 0.8 %collective-permute-done.5 = f32[1,8,128]{2,1,0:T(8,128)S(1)} collective-permute-done((f32[1,8,128]{2,1,0:T(8,128)S(1)}, f32[1,8,128]{2,1,0:T(8,128)S(1)}, u32[]{:S(2)}, u32[]{:S(2)}) %collective-permute-start.5) | collective-permute-done | bytes 4128 | tf_op jit(solution)/shard_map/ppermute | solution.py:725
  24.2 1.4 %collective-permute-start.6 = (f32[1,8,128]{2,1,0:T(8,128)S(1)}, f32[1,8,128]{2,1,0:T(8,128)S(1)}, u32[]{:S(2)}, u32[]{:S(2)}) collective-permute-start(f32[1,8,128]{2,1,0:T(8,128)S(1)} %add.13), channel_id=1, source_target_pairs={{0,5},{1,4},{2,7},{3,6},{4,1},{5,0},{6,3},{7,2},{8,13},{9,12},{10,... | collective-permute-start | bytes 12296 | tf_op jit(solution)/shard_map/ppermute | solution.py:725
  25.6 1.0 %invert.1.system_ref = f32[32,64]{1,0:T(8,128)S(1)} custom-call(f32[32,64]{1,0:T(8,128)S(1)} %get-tuple-element.75.system_ref), custom_call_target="tpu_custom_call" | custom-call | flops 2000000000 | bytes 1048576 | tf_op jit(solution)/shard_map/invert/pallas_call | solution.py:886
  26.6 0.7 %collective-permute-done.6 = f32[1,8,128]{2,1,0:T(8,128)S(1)} collective-permute-done((f32[1,8,128]{2,1,0:T(8,128)S(1)}, f32[1,8,128]{2,1,0:T(8,128)S(1)}, u32[]{:S(2)}, u32[]{:S(2)}) %collective-permute-start.6) | collective-permute-done | bytes 4128 | tf_op jit(solution)/shard_map/ppermute | solution.py:725
  27.3 2.7 %collective-permute-start.7 = (f32[1,8,128]{2,1,0:T(8,128)S(1)}, f32[1,8,128]{2,1,0:T(8,128)S(1)}, u32[]{:S(2)}, u32[]{:S(2)}) collective-permute-start(f32[1,8,128]{2,1,0:T(8,128)S(1)} %add.14), channel_id=1, source_target_pairs={{0,9},{1,8},{2,11},{3,10},{4,13},{5,12},{6,15},{7,14},{8,1},{9,0},... | collective-permute-start | bytes 12296 | tf_op jit(solution)/shard_map/ppermute | solution.py:725
  30.0 1.3 %weights.1 = (f32[32,560]{1,0:T(8,128)S(1)}, f32[32,32]{1,0:T(8,128)S(1)}) custom-call(f32[1,8,128]{2,1,0:T(8,128)S(1)} %get-tuple-element.68.coords_ref, f32[32,32]{1,0:T(8,128)S(1)} %get-tuple-element.77.kernel_ref, f32[32,64]{1,0:T(8,128)S(1)} %invert.1.system_ref, f32[32,560]{1,0:T(8,128)S(1)} %copy-done.5, f32[32,560]{1,0:T(8,128)S(1)} %copy-done.4, ...), custom_call_target="tpu_custom_call" | custom-call | flops 2000000000 | bytes 1048576 | tf_op jit(solution)/shard_map/weights/pallas_call | solution.py:886
  31.4 1.0 %fit.1 = (f32[2,64]{1,0:T(2,128)}, f32[32,560]{1,0:T(8,128)}, f32[2,32]{1,0:T(2,128)}) custom-call(s32[1]{0:T(128)} %bitcast.place.refs_0_, f32[1,8,128]{2,1,0:T(8,128)S(1)} %add.15.rates_ref, f32[1,8,128]{2,1,0:T(8,128)S(1)} %get-tuple-element.68.coords_ref, f32[32,560]{1,0:T(8,128)S(1)} %get-tuple-element.79.weights, f32[32,32]{1,0:T(8,128)S(1)} %get-tuple-element.80.fit), custom_call_target="tpu_custom_call" | custom-call | tf_op jit(solution)/shard_map/fit/pallas_call | solution.py:934
  (25 shorter events, 0.1 us)
Async XLA Ops:
  3.5 1.5 %collective-permute-start = (bf16[1,112,128]{2,1,0:T(8,128)(2,1)S(1)}, bf16[1,112,128]{2,1,0:T(8,128)(2,1)S(1)}, u32[]{:S(2)}, u32[]{:S(2)}) collective-permute-start(bf16[1,112,128]{2,1,0:T(8,128)(2,1)S(1)} %get-tuple-element.45.after.first.refs_5_), channel_id=1, source_target_pairs={{0,1},{1,0},{2,3},{3,2},{4,5},{5,4},{6,7},{7,6},{8,9},{9,8},{10,11... | collective-permute-start | bytes 86024 | tf_op jit(solution)/shard_map/ppermute | solution.py:725
  5.0 3.8 %copy-start = (f32[5,5]{1,0:T(8,128)S(1)}, f32[5,5]{1,0:T(8,128)}, u32[]{:S(2)}) copy-start(f32[5,5]{1,0:T(8,128)} %coup.1) | copy-start | bytes 304
  5.0 3.8 %copy-start.1 = (f32[5]{0:T(128)S(1)}, f32[5]{0:T(128)}, u32[]{:S(2)}) copy-start(f32[5]{0:T(128)} %visc.1) | copy-start | bytes 64
  5.0 3.8 %copy-start.2 = (f32[16]{0:T(128)S(1)}, f32[16]{0:T(128)}, u32[]{:S(2)}) copy-start(f32[16]{0:T(128)} %kern.1) | copy-start | bytes 196
  5.0 3.8 %copy-start.3 = (f32[5]{0:T(128)S(1)}, f32[5]{0:T(128)}, u32[]{:S(2)}) copy-start(f32[5]{0:T(128)} %gain.1) | copy-start | bytes 64
  5.1 5.4 %collective-permute-start.1 = (bf16[1,96,128]{2,1,0:T(8,128)(2,1)S(1)}, bf16[1,96,128]{2,1,0:T(8,128)(2,1)S(1)}, u32[]{:S(2)}, u32[]{:S(2)}) collective-permute-start(bf16[1,96,128]{2,1,0:T(8,128)(2,1)S(1)} %get-tuple-element.50.after.sent), channel_id=1, source_target_pairs={{0,9},{1,8},{2,11},{3,10},{4,13},{5,12},{6,15},{7,14},{8,1},{9,0},... | collective-permute-start | bytes 73736 | tf_op jit(solution)/shard_map/ppermute | solution.py:725
  10.5 3.4 %collective-permute-start.2 = (bf16[1,128,128]{2,1,0:T(8,128)(2,1)S(1)}, bf16[1,128,128]{2,1,0:T(8,128)(2,1)S(1)}, u32[]{:S(2)}, u32[]{:S(2)}) collective-permute-start(bf16[1,128,128]{2,1,0:T(8,128)(2,1)S(1)} %get-tuple-element.59.after.sent), channel_id=1, source_target_pairs={{0,5},{1,4},{2,7},{3,6},{4,1},{5,0},{6,3},{7,2},{8,13},{9,12},{10,... | collective-permute-start | bytes 98312 | tf_op jit(solution)/shard_map/ppermute | solution.py:725
  13.9 3.8 %collective-permute-start.3 = (bf16[1,192,128]{2,1,0:T(8,128)(2,1)S(1)}, bf16[1,192,128]{2,1,0:T(8,128)(2,1)S(1)}, u32[]{:S(2)}, u32[]{:S(2)}) collective-permute-start(bf16[1,192,128]{2,1,0:T(8,128)(2,1)S(1)} %next.3.after.refs_7_), channel_id=1, source_target_pairs={{0,3},{1,2},{2,1},{3,0},{4,7},{5,6},{6,5},{7,4},{8,11},{9,10},{10,... | collective-permute-start | bytes 147464 | tf_op jit(solution)/shard_map/ppermute | solution.py:725
  20.0 1.2 %collective-permute-start.4 = (f32[1,16,128]{2,1,0:T(8,128)S(1)}, f32[1,16,128]{2,1,0:T(8,128)S(1)}, u32[]{:S(2)}, u32[]{:S(2)}) collective-permute-start(f32[1,16,128]{2,1,0:T(8,128)S(1)} %get-tuple-element.66), channel_id=1, source_target_pairs={{0,1},{1,0},{2,3},{3,2},{4,5},{5,4},{6,7},{7,6},{8,9},{9,8},{10,11... | collective-permute-start | bytes 24584 | tf_op jit(solution)/shard_map/ppermute | solution.py:725
  21.2 3.0 %collective-permute-start.5 = (f32[1,8,128]{2,1,0:T(8,128)S(1)}, f32[1,8,128]{2,1,0:T(8,128)S(1)}, u32[]{:S(2)}, u32[]{:S(2)}) collective-permute-start(f32[1,8,128]{2,1,0:T(8,128)S(1)} %get-tuple-element.71), channel_id=1, source_target_pairs={{0,3},{1,2},{2,1},{3,0},{4,7},{5,6},{6,5},{7,4},{8,11},{9,10},{10,... | collective-permute-start | bytes 12296 | tf_op jit(solution)/shard_map/ppermute | solution.py:725
  24.2 5.8 %copy-start.4 = (f32[32,560]{1,0:T(8,128)S(1)}, f32[32,560]{1,0:T(8,128)}, u32[]{:S(2)}) copy-start(f32[32,560]{1,0:T(8,128)} %constant.14.clone.second_ref) | copy-start | bytes 215044
  24.2 5.8 %copy-start.5 = (f32[32,560]{1,0:T(8,128)S(1)}, f32[32,560]{1,0:T(8,128)}, u32[]{:S(2)}) copy-start(f32[32,560]{1,0:T(8,128)} %constant.13.clone.first_ref) | copy-start | bytes 215044
  24.2 3.1 %collective-permute-start.6 = (f32[1,8,128]{2,1,0:T(8,128)S(1)}, f32[1,8,128]{2,1,0:T(8,128)S(1)}, u32[]{:S(2)}, u32[]{:S(2)}) collective-permute-start(f32[1,8,128]{2,1,0:T(8,128)S(1)} %add.13), channel_id=1, source_target_pairs={{0,5},{1,4},{2,7},{3,6},{4,1},{5,0},{6,3},{7,2},{8,13},{9,12},{10,... | collective-permute-start | bytes 12296 | tf_op jit(solution)/shard_map/ppermute | solution.py:725
  26.6 3.5 %copy-start.6 = (f32[1,560]{1,0:T(1,128)S(1)}, f32[1,560]{1,0:T(1,128)}, u32[]{:S(2)}) copy-start(f32[1,560]{1,0:T(1,128)} %constant.15.clone.lin_ref) | copy-start | bytes 6724
  27.3 4.1 %collective-permute-start.7 = (f32[1,8,128]{2,1,0:T(8,128)S(1)}, f32[1,8,128]{2,1,0:T(8,128)S(1)}, u32[]{:S(2)}, u32[]{:S(2)}) collective-permute-start(f32[1,8,128]{2,1,0:T(8,128)S(1)} %add.14), channel_id=1, source_target_pairs={{0,9},{1,8},{2,11},{3,10},{4,13},{5,12},{6,15},{7,14},{8,1},{9,0},... | collective-permute-start | bytes 12296 | tf_op jit(solution)/shard_map/ppermute | solution.py:725
